TPU v7x, 32 devices: a whole 2x2x4 slice. The times are simulated.
32 devices in a mesh: section: 4 (over y, x), dp: 8 (over z, core).
Axes of the slice: x: 2, y: 2, z: 4, core: 2. Of those that a mesh axis runs over, the one named last changes fastest.
Arguments:
- images: bfloat16 [16, 32, 32, 512], P('dp', None, None, 'section'), may hold values from -6 to 6
- cotangent: bfloat16 [16, 16, 16, 1024], P('dp', None, None, 'section'), may hold values from -6 to 6
- res_codes: int32 [16], P('dp'), may hold values from 0 to 2, as said below
- section_weights: float32 [4, 1351680], P('section', 'dp'), may hold values from -2 to 2
Outputs:
- block_out: bfloat16 [16, 16, 16, 1024], P('dp', None, None, 'section')
- input_grad: bfloat16 [16, 32, 32, 512], P('dp', None, None, 'section')
- section_grads: float32 [4, 1351680], P('section', 'dp')
Inputs may be any that keep to these rules, and one draw needn't show every extreme that they name: `res_codes`: image 0 has code 2 and image 1 code 0.
All inputs are finite; a program needn't handle non-finite values.
Results may differ from a plain program's by a relative error of at most 0.019.
The roundings to bfloat16 on the way count: a program that leaves them out, or rounds other values in their place, can miss the bound.
Values may be sent and summed in bfloat16 or wider, within the bound.
A program may use at most 128 MiB of HBM per device.

v0:
```python
import math

import jax
import jax.numpy as jnp
from jax import lax
from jax.experimental import pallas as pl
from jax.experimental.pallas import tpu as pltpu
from jax.sharding import PartitionSpec as P

CIN = 512
COUT = 1024
CMID = 256
CSQ = 128
SIDE = 16
PX = SIDE * SIDE
HALF = 128
WSLOTS = 1351680
EPS = 1e-05
HIGH = lax.Precision.HIGHEST
MESH = pl.DeviceIdType.MESH
F32 = jnp.float32
BF16 = jnp.bfloat16
PHASES = 14


def layouts():
    first = (
        ("w_in", (CIN, CMID)),
        ("g_in", (CMID,)),
        ("b_in", (CMID,)),
        ("w_mid", (9, HALF, 2 * CMID)),
        ("g_mid", (2 * CMID,)),
        ("b_mid", (2 * CMID,)),
        ("w_sq", (CMID, CSQ)),
        ("g_sq", (CSQ,)),
        ("b_sq", (CSQ,)),
        ("w_ex", (CSQ, 2 * CMID)),
        ("b_ex", (2 * CMID,)),
        ("w_sc", (CIN, COUT)),
        ("g_sc", (COUT,)),
        ("b_sc", (COUT,)),
    )
    second = (
        ("w_out", (CMID, COUT)),
        ("g_out", (COUT,)),
        ("b_out", (COUT,)),
        ("w_in", (COUT, CMID)),
        ("g_in", (CMID,)),
        ("b_in", (CMID,)),
    )
    return (first, second, first[3:11], second[:3])


VECTORS = (
    (0, "g_in", True),
    (0, "b_in", True),
    (0, "g_mid", True),
    (0, "b_mid", True),
    (0, "g_sq", False),
    (0, "b_sq", False),
    (0, "b_ex", False),
    (0, "g_sc", True),
    (0, "b_sc", True),
    (1, "g_out", True),
    (1, "b_out", True),
    (1, "g_in", True),
    (1, "b_in", True),
    (2, "g_mid", True),
    (2, "b_mid", True),
    (2, "g_sq", False),
    (2, "b_sq", False),
    (2, "b_ex", False),
    (3, "g_out", True),
    (3, "b_out", True),
)
VROW = {(s, name): i for i, (s, name, _) in enumerate(VECTORS)}
VROWS = 24
VCOLS = 512


def dot(a, b):
    return lax.dot_general(a, b, (((1,), (0,)), ((), ())), preferred_element_type=F32)


def dot_rt(a, b):
    return lax.dot_general(a, b, (((1,), (1,)), ((), ())), preferred_element_type=F32)


def dot_lt(a, b):
    return lax.dot_general(a, b, (((0,), (0,)), ((), ())), preferred_element_type=F32)


def dot_hi(a, b, dims=((1,), (0,))):
    return lax.dot_general(a, b, (dims, ((), ())), precision=HIGH, preferred_element_type=F32)


def sigmoid(v):
    return 0.5 + 0.5 * jnp.tanh(0.5 * v)


def fold8(x):
    return jnp.sum(x.reshape(x.shape[0] // 8, 8, x.shape[1]), axis=0)


def lanes(x, count):
    return jnp.concatenate([x] * count, axis=1) if count > 1 else x


def make_kernel(n):
    chips = n // 2

    def kernel(
        img,
        cot,
        codes,
        w_in0,
        w_mid0,
        w_sq0,
        w_ex0,
        w_sc,
        w_out1,
        w_in1,
        w_mid2,
        w_sq2,
        w_ex2,
        w_out3,
        vec,
        out_o,
        out_i,
        gw_in0,
        gw_mid0,
        gw_sq0,
        gw_ex0,
        gw_sc,
        gw_out1,
        gw_in1,
        gw_mid2,
        gw_sq2,
        gw_ex2,
        gw_out3,
        gvec,
        snd,
        rcv,
        side_t,
        u,
        um,
        pool,
        ctb,
        mref,
        z1,
        z2,
        zs,
        z3,
        z4,
        z5,
        z6,
        v3,
        cols1,
        cols2,
        rr1,
        rr2,
        a1,
        a2,
        y1,
        dv6,
        dbuf,
        spb,
        pz,
        pda,
        pdp,
        dz4,
        dz1,
        dz3,
        dzs,
        ep,
        dh,
        obuf,
        ibuf,
        ssem,
        rsem,
        bs,
        br,
        img_s,
        img_r,
        ct_s,
        ct_r,
        oo_s,
        oo_r,
        oi_s,
        oi_r,
    ):
        s = lax.axis_index("section")
        d = lax.axis_index("dp")
        c = d // 2
        k = d % 2
        m = s % 2
        g = (s // 2) * chips + c

        def peer(o, kk):
            gg = lax.rem(g + o, n)
            return ((gg // chips) * 2 + m, 2 * (gg % chips) + kk)

        barrier = pltpu.get_barrier_semaphore()

        def greet(o, _):
            pl.semaphore_signal(barrier, inc=1, device_id=peer(o, 0), device_id_type=MESH)
            pl.semaphore_signal(barrier, inc=1, device_id=peer(o, 1), device_id_type=MESH)
            return 0

        lax.fori_loop(1, n, greet, 0)
        pl.semaphore_signal(barrier, inc=1, device_id=(s, 2 * c + 1 - k), device_id_type=MESH)
        for i in range(2):
            for kk in range(2):
                pl.semaphore_signal(
                    barrier,
                    inc=1,
                    device_id=(2 * i + 1 - m, 2 * c + kk),
                    device_id_type=MESH,
                )
        pl.semaphore_wait(barrier, 2 * n - 1 + 4)

        def to_twin(i, src, dst):
            return pltpu.make_async_remote_copy(
                src, dst, bs.at[i], br.at[i], device_id=(s, 2 * c + 1 - k), device_id_type=MESH
            )

        def move(src, dst, s_sem, r_sem, dev):
            own = (dev[0] == s) & (dev[1] == d)

            @pl.when(own)
            def _():
                pltpu.make_async_copy(src, dst, r_sem).start()

            @pl.when(jnp.logical_not(own))
            def _():
                pltpu.make_async_remote_copy(
                    src, dst, s_sem, r_sem, device_id=dev, device_id_type=MESH
                ).start()

        def end_move(src, s_sem, dev):
            own = (dev[0] == s) & (dev[1] == d)

            @pl.when(jnp.logical_not(own))
            def _():
                pltpu.make_async_copy(src, src, s_sem).wait()

        for slot in range(2):
            for kk in range(2):
                move(
                    img.at[slot, pl.ds(2 * kk, 2)],
                    u.at[s, pl.ds(2 * kk, 2)],
                    img_s.at[slot, kk],
                    img_r.at[s],
                    (2 * k + slot, 2 * c + kk),
                )
        for slot in range(2):
            move(
                cot.at[slot],
                ctb.at[lax.rem(s, 2)],
                ct_s.at[slot],
                ct_r.at[lax.rem(s, 2)],
                (2 * k + slot, 2 * c + s // 2),
            )
        for slot in range(2):
            width = (SIDE - 2 * codes[slot]).astype(F32)
            side_t[k, slot] = jnp.full((8, 128), width, F32)
        side_copy = to_twin(0, side_t.at[k], side_t.at[k])
        side_copy.start()
        snd[...] = jnp.zeros(snd.shape, F32)

        def put(ph, base, value):
            for j in range(value.shape[1] // 128):
                snd[ph, base + j : base + j + 1, :] = value[:, 128 * j : 128 * (j + 1)]

        def send(ph, rows, both=False):
            def one(o, _):
                pltpu.make_async_remote_copy(
                    snd.at[ph, pl.ds(0, rows)],
                    rcv.at[ph, k, o, pl.ds(0, rows)],
                    ssem.at[ph],
                    rsem.at[ph, k],
                    device_id=peer(o, k),
                    device_id_type=MESH,
                ).start()
                return 0

            def other(o, _):
                pltpu.make_async_remote_copy(
                    snd.at[ph, pl.ds(0, rows)],
                    rcv.at[ph, k, o, pl.ds(0, rows)],
                    ssem.at[ph],
                    rsem.at[ph, k],
                    device_id=peer(o, 1 - k),
                    device_id_type=MESH,
                ).start()
                return 0

            lax.fori_loop(1, n, one, 0)
            if both:
                lax.fori_loop(0, n, other, 0)
            rcv[ph, k, 0, 0:rows] = snd[ph, 0:rows]

        def receive(ph, rows, both=False):
            mine = rcv.at[ph, k, pl.ds(1, n - 1), pl.ds(0, rows)]
            pltpu.make_async_copy(mine, mine, rsem.at[ph, k]).wait()
            if both:
                theirs = rcv.at[ph, 1 - k, :, pl.ds(0, rows)]
                pltpu.make_async_copy(theirs, theirs, rsem.at[ph, 1 - k]).wait()

        def end_send(ph, rows, both=False):
            mine = rcv.at[ph, k, pl.ds(1, n - 1), pl.ds(0, rows)]
            pltpu.make_async_copy(mine, mine, ssem.at[ph]).wait()
            if both:
                theirs = rcv.at[ph, 1 - k, :, pl.ds(0, rows)]
                pltpu.make_async_copy(theirs, theirs, ssem.at[ph]).wait()

        def totals(ph, rows):
            return jnp.sum(rcv[ph, k, :, 0:rows, :], axis=0)

        def row(total, base, width):
            return jnp.concatenate(
                [total[base + j : base + j + 1, :] for j in range(width // 128)], axis=1
            )

        def across(ph, h, base, width):
            return jnp.concatenate(
                [rcv[ph, h, :, base + j, :] for j in range(width // 128)], axis=1
            )

        def vrow(key, width):
            i = VROW[key]
            return vec[i : i + 1, 0:width]

        def set_gvec(key, value):
            i = VROW[key]
            gvec[i : i + 1, 0 : value.shape[1]] = value

        def mean_rstd(total, base, width, count):
            mu = row(total, base, width) / count
            second = row(total, base + width // 128, width) / count
            return mu, lax.rsqrt(jnp.maximum(second - mu * mu, 0.0) + EPS)

        gvec[...] = jnp.zeros(gvec.shape, F32)

        side_copy.wait()
        side_row = jnp.where(
            m == 0, side_t[s // 2, 0, 0:1, :], side_t[s // 2, 1, 0:1, :]
        )
        pixel = lax.broadcasted_iota(jnp.int32, (PX, 128), 0)
        prow = (pixel // SIDE).astype(F32)
        pcol = (pixel % SIDE).astype(F32)
        mref[...] = jnp.where((prow < side_row) & (pcol < side_row), 1.0, 0.0)
        inv_own = 1.0 / (side_row * side_row)

        for q in range(4):
            here = u.at[q, pl.ds(2 * k, 2)]
            pltpu.make_async_copy(here, here, img_r.at[q]).wait()
            pltpu.make_async_remote_copy(
                here,
                here,
                bs.at[10 + q],
                br.at[10 + q],
                device_id=(s, 2 * c + 1 - k),
                device_id_type=MESH,
            ).start()
        for q in range(4):
            here = u.at[q, pl.ds(2 * (1 - k), 2)]
            pltpu.make_async_copy(here, here, br.at[10 + q]).wait()

        def mask_block(b, _):
            r = pl.multiple_of(b * 32, 32)
            rows = pl.ds(r, 32)
            mask = mref[rows, :]
            for q in range(4):
                total = jnp.zeros((32, 128), F32)
                for p in range(4):
                    x = u[q, p, rows, :].astype(F32) * mask
                    um[p, rows, 128 * q : 128 * (q + 1)] = x.astype(BF16)
                    total = total + x
                pool[rows, 128 * q : 128 * (q + 1)] = (total * 0.25).astype(BF16)
            return 0

        lax.fori_loop(0, 8, mask_block, 0)

        def z1_block(p, carry):
            z = dot(um[p], w_in0[k])
            z1[p] = z
            return (carry[0] + fold8(z), carry[1] + fold8(z * z))

        zero8 = jnp.zeros((8, 128), F32)
        t0, t1 = lax.fori_loop(0, 4, z1_block, (zero8, zero8))
        put(0, 0, jnp.sum(t0, axis=0, keepdims=True))
        put(0, 1, jnp.sum(t1, axis=0, keepdims=True))
        put(0, 2, side_row)
        send(0, 8)
        z = dot(pool[...], w_sc[...])
        zs[...] = z
        sum_s = jnp.sum(z, axis=0, keepdims=True)
        sq_s = jnp.sum(z * z, axis=0, keepdims=True)
        receive(0, 8)
        total = totals(0, 8)
        sides = across(0, k, 2, 128)
        inv_area = 1.0 / (sides * sides)
        count1 = jnp.sum(sides * sides, axis=0, keepdims=True)
        counts = {w: lanes(count1, w // 128) for w in (128, 256, 512)}
        mu1, rs1 = mean_rstd(total, 0, 128, 4.0 * count1)
        lin1 = rs1 * vrow((0, "g_in"), 128)
        off1 = vrow((0, "b_in"), 128) - mu1 * lin1

        colpos = lax.broadcasted_iota(jnp.int32, (PX, 128), 0) % SIDE

        def shift_cols(x, by):
            moved = pltpu.roll(x, by % PX, 0)
            edge = 0 if by == 1 else SIDE - 1
            return jnp.where(colpos == edge, 0.0, moved)

        def store_tap(cols, di, dj, x, shift):
            at = 128 * (3 * di + dj)
            span = slice(at, at + 128)
            x = x.astype(BF16)
            if shift == 1:
                cols[0:SIDE, span] = jnp.zeros((SIDE, 128), BF16)
                cols[SIDE:PX, span] = x[0 : PX - SIDE]
            elif shift == -1:
                cols[PX - SIDE : PX, span] = jnp.zeros((SIDE, 128), BF16)
                cols[0 : PX - SIDE, span] = x[SIDE:PX]
            else:
                cols[:, span] = x

        def plane_taps(parity):
            return ((1, 0),) if parity == 0 else ((0, 1), (2, 0))

        for p in range(4):
            v = z1[p] * lin1 + off1
            h = v * sigmoid(v) * mref[...]
            for dj, cshift in plane_taps(p % 2):
                x = shift_cols(h, 1) if cshift else h
                for di, rshift in plane_taps(p // 2):
                    store_tap(cols1, di, dj, x, rshift)

        def conv_forward(ph, cols, w_mid, zref):
            z = dot(cols[...], w_mid[...])
            zref[...] = z
            zm = z * lanes(mref[...], 2)
            put(ph, 0, jnp.sum(zm, axis=0, keepdims=True))
            put(ph, 2, jnp.sum(zm * z, axis=0, keepdims=True))
            send(ph, 8)

        def attention_forward(ph, twin, total, sec, zref, rr, w_sq, w_ex, aref, beside):
            mu, rs = mean_rstd(total, 0, 256, counts[256])
            lin = rs * vrow((sec, "g_mid"), 256)
            off = vrow((sec, "b_mid"), 256) - mu * lin

            def block(b, acc):
                rows = pl.ds(pl.multiple_of(b * 64, 64), 64)
                v = zref[rows, :] * lin + off
                r = v * sigmoid(v) * lanes(mref[rows, :], 2)
                rr[k, rows, :] = r
                return acc + fold8(r)

            acc = lax.fori_loop(0, 4, block, jnp.zeros((8, 256), F32))
            pooled_own = jnp.sum(acc, axis=0, keepdims=True) * lanes(inv_own, 2)
            put(ph, 0, pooled_own)
            send(ph, 16 if beside is not None else 8, both=True)
            swap = to_twin(twin, rr.at[k], rr.at[k])
            swap.start()
            receive(ph, 16 if beside is not None else 8, both=True)
            pooled = across(ph, 0, 0, 256) + across(ph, 1, 0, 256)
            zq = dot_hi(pooled, w_sq[...].astype(F32))
            mq = jnp.mean(zq, axis=0, keepdims=True)
            vq = jnp.mean(zq * zq, axis=0, keepdims=True) - mq * mq
            rq = lax.rsqrt(jnp.maximum(vq, 0.0) + EPS)
            hq = (zq - mq) * rq
            nq = hq * vrow((sec, "g_sq"), 128) + vrow((sec, "b_sq"), 128)
            sgq = sigmoid(nq)
            qq = nq * sgq
            logits = dot_hi(qq, w_ex[...].astype(F32)) + vrow((sec, "b_ex"), 512)
            diff = logits[:, 0:256] - logits[:, 256:512]
            sh0 = sigmoid(diff)
            sh1 = sigmoid(-diff)
            swap.wait()
            s0 = sh0[0:1, :]
            s1 = sh1[0:1, :]

            def mix(b, _):
                rows = pl.ds(pl.multiple_of(b * 64, 64), 64)
                aref[rows, :] = (s0 * rr[0, rows, :] + s1 * rr[1, rows, :]).astype(BF16)
                return 0

            lax.fori_loop(0, 4, mix, 0)
            return (mu, rs, lin, off), (pooled, rq, hq, nq, sgq, qq, sh0, sh1)

        def attention_backward(
            ph, sec, kept_mid, kept_q, zref, rr, w_sq, w_ex, g_sq, g_ex, cols, w_mid, g_mid, da, beside
        ):
            mu, rs, lin, off = kept_mid
            pooled, rq, hq, nq, sgq, qq, sh0, sh1 = kept_q

            def block(b, acc):
                rows = pl.ds(pl.multiple_of(b * 32, 32), 32)
                z = zref[rows, :]
                v = z * lin + off
                hat = (z - mu) * rs
                sg = sigmoid(v)
                sp = sg * (1.0 + v * (1.0 - sg)) * lanes(mref[rows, :], 2)
                grad = da(rows)
                t = grad * sp
                dbuf[rows, :] = grad
                spb[rows, :] = sp
                r = rr[k, rows, :]
                return tuple(
                    x + fold8(y)
                    for x, y in zip(acc, (grad * r, t, sp, t * hat, sp * hat))
                )

            acc = lax.fori_loop(0, 8, block, (jnp.zeros((8, 256), F32),) * 5)
            for j, x in enumerate(acc):
                put(ph, 2 * j, jnp.sum(x, axis=0, keepdims=True))
            send(ph, 16, both=True)
            beside()
            receive(ph, 16, both=True)
            ds0 = across(ph, 0, 0, 256)
            ds1 = across(ph, 1, 0, 256)
            mean = sh0 * ds0 + sh1 * ds1
            dl = jnp.concatenate([sh0 * (ds0 - mean), sh1 * (ds1 - mean)], axis=1)
            set_gvec((sec, "b_ex"), jnp.sum(dl, axis=0, keepdims=True))
            dq = dot_hi(dl, w_ex[...].astype(F32), ((1,), (1,)))
            dn = dq * sgq * (1.0 + nq * (1.0 - sgq))
            set_gvec((sec, "g_sq"), jnp.sum(dn * hq, axis=0, keepdims=True))
            set_gvec((sec, "b_sq"), jnp.sum(dn, axis=0, keepdims=True))
            dn = dn * vrow((sec, "g_sq"), 128)
            dzq = rq * (
                dn
                - jnp.mean(dn, axis=0, keepdims=True)
                - hq * jnp.mean(dn * hq, axis=0, keepdims=True)
            )
            dpool = dot_hi(dzq, w_sq[...].astype(F32), ((1,), (1,))) * lanes(inv_area, 2)
            share = jnp.where(k == 0, sh0, sh1)

            def both_sums(first, second):
                return jnp.sum(
                    share * across(ph, k, first, 256) + dpool * across(ph, k, second, 256),
                    axis=0,
                    keepdims=True,
                )

            sdv = both_sums(2, 4)
            sdh = both_sums(6, 8)
            set_gvec((sec, "b_mid"), sdv)
            set_gvec((sec, "g_mid"), sdh)
            own_share = share[0:1, :]
            own_pool = dpool[0:1, :]
            c1 = sdv / counts[256]
            c2 = sdh / counts[256]

            def block2(b, _):
                rows = pl.ds(pl.multiple_of(b * 32, 32), 32)
                hat = (zref[rows, :] - mu) * rs
                dv = (own_share * dbuf[rows, :] + own_pool) * spb[rows, :]
                dz = lin * (dv - c1 - hat * c2) * lanes(mref[rows, :], 2)
                rows_low[rows, :] = dz.astype(BF16)
                return 0

            rows_low = dz_low
            lax.fori_loop(0, 8, block2, 0)

            def rest():
                g_ex[...] = dot_hi(qq, dl, ((0,), (0,))).astype(g_ex.dtype)
                g_sq[...] = dot_hi(pooled, dzq, ((0,), (0,))).astype(g_sq.dtype)
                g_mid[...] = dot_lt(cols[...], dz_low[...]).astype(g_mid.dtype)

            return rest

        dz_low = dz3.at[:, pl.ds(0, 256)]

        conv_forward(1, cols1, w_mid0, z2)
        receive(1, 8)
        put(2, 8, sum_s)
        put(2, 12, sq_s)
        mid1, q1 = attention_forward(2, 2, totals(1, 8), 0, z2, rr1, w_sq0, w_ex0, a1, True)
        total = totals(2, 16)
        mus, rss = mean_rstd(total, 8, 512, counts[512])
        lins = rss * vrow((0, "g_sc"), 512)
        offs = vrow((0, "b_sc"), 512) - mus * lins

        def wide_forward(ph, aref, w, zref):
            z = dot(aref[...], w[...])
            zref[...] = z
            put(ph, 0, jnp.sum(z, axis=0, keepdims=True))
            put(ph, 4, jnp.sum(z * z, axis=0, keepdims=True))
            send(ph, 8)

        wide_forward(3, a1, w_out1, z3)
        receive(3, 8)
        mu3, rs3 = mean_rstd(totals(3, 8), 0, 512, counts[512])
        lin3 = rs3 * vrow((1, "g_out"), 512)
        off3 = vrow((1, "b_out"), 512) - mu3 * lin3

        def y1_block(b, _):
            rows = pl.ds(pl.multiple_of(b * 32, 32), 32)
            short = (zs[rows, :] * lins + offs).astype(BF16).astype(F32)
            v = z3[rows, :] * lin3 + off3 + short
            v3[rows, :] = v
            y1[rows, :] = (v * sigmoid(v) * lanes(mref[rows, :], 4)).astype(BF16)
            return 0

        lax.fori_loop(0, 8, y1_block, 0)
        pz[0] = dot(y1[...], w_in1[1 - k])
        swap = to_twin(3, pz.at[0], pz.at[1])
        swap.start()
        z = dot(y1[...], w_in1[k])
        swap.wait()
        z = z + pz[1]
        z4[...] = z
        put(4, 0, jnp.sum(z, axis=0, keepdims=True))
        put(4, 1, jnp.sum(z * z, axis=0, keepdims=True))
        send(4, 8)
        receive(4, 8)
        mu4, rs4 = mean_rstd(totals(4, 8), 0, 128, count1)
        lin4 = rs4 * vrow((1, "g_in"), 128)
        off4 = vrow((1, "b_in"), 128) - mu4 * lin4
        v = z4[...] * lin4 + off4
        h = v * sigmoid(v) * mref[...]
        for dj in range(3):
            x = h if dj == 1 else shift_cols(h, 1 - dj)
            for di in range(3):
                store_tap(cols2, di, dj, x, 1 - di)

        conv_forward(5, cols2, w_mid2, z5)
        receive(5, 8)
        mid2, q2 = attention_forward(6, 4, totals(5, 8), 2, z5, rr2, w_sq2, w_ex2, a2, None)
        wide_forward(7, a2, w_out3, z6)
        for i in range(2):
            pltpu.make_async_copy(ctb.at[i], ctb.at[i], ct_r.at[i]).wait()
        receive(7, 8)
        mu6, rs6 = mean_rstd(totals(7, 8), 0, 512, counts[512])
        lin6 = rs6 * vrow((3, "g_out"), 512)
        off6 = vrow((3, "b_out"), 512) - mu6 * lin6

        def out_block(b, acc):
            rows = pl.ds(pl.multiple_of(b * 32, 32), 32)
            z = z6[rows, :]
            mask = lanes(mref[rows, :], 4)
            v = z * lin6 + off6 + y1[rows, :].astype(F32)
            sg = sigmoid(v)
            y = (v * sg * mask).astype(BF16)
            obuf[0, rows, :] = y[:, 0:256]
            obuf[1, rows, :] = y[:, 256:512]
            ct = jnp.concatenate([ctb[0, rows, :], ctb[1, rows, :]], axis=1).astype(F32)
            dv = ct * (sg * (1.0 + v * (1.0 - sg)) * mask)
            dv6[rows, :] = dv
            return (acc[0] + fold8(dv), acc[1] + fold8(dv * ((z - mu6) * rs6)))

        zero512 = jnp.zeros((8, 512), F32)
        t0, t1 = lax.fori_loop(0, 8, out_block, (zero512, zero512))
        put(8, 0, jnp.sum(t0, axis=0, keepdims=True))
        put(8, 4, jnp.sum(t1, axis=0, keepdims=True))
        send(8, 8)
        for j in range(2):
            move(
                obuf.at[j],
                out_o.at[lax.rem(s, 2)],
                oo_s.at[j],
                oo_r.at[lax.rem(s, 2)],
                (2 * k + j, 2 * c + s // 2),
            )
        receive(8, 8)

        def wide_back(total, base, key_g, key_b, lin, mu, rs, zref, dvf, dst):
            sdv = row(total, base, 512)
            sdh = row(total, base + 4, 512)
            set_gvec(key_b, sdv)
            set_gvec(key_g, sdh)
            c1 = sdv / counts[512]
            c2 = sdh / counts[512]

            def block(b, _):
                rows = pl.ds(pl.multiple_of(b * 32, 32), 32)
                hat = (zref[rows, :] - mu) * rs
                dz = lin * (dvf(rows) - c1 - hat * c2) * lanes(mref[rows, :], 4)
                dst[rows, :] = dz.astype(BF16)
                return 0

            lax.fori_loop(0, 8, block, 0)

        wide_back(
            totals(8, 8),
            0,
            (3, "g_out"),
            (3, "b_out"),
            lin6,
            mu6,
            rs6,
            z6,
            lambda rows: dv6[rows, :],
            dz3,
        )

        def attended_grad(twin, w, aref, gw):
            pda[0] = dot_rt(dz3[...], w[...])
            swap = to_twin(twin, pda.at[0], pda.at[1])
            swap.start()
            gw[...] = dot_lt(aref[...], dz3[...]).astype(gw.dtype)
            swap.wait()

        def summed_grad(rows):
            return (pda[0, rows, :] + pda[1, rows, :]).astype(BF16).astype(F32)

        attended_grad(5, w_out3, a2, gw_out3)
        rest2 = attention_backward(
            9,
            2,
            mid2,
            q2,
            z5,
            rr2,
            w_sq2,
            w_ex2,
            gw_sq2,
            gw_ex2,
            cols2,
            w_mid2,
            gw_mid2,
            summed_grad,
            lambda: None,
        )

        ep[...] = jnp.zeros(ep.shape, F32)
        for di in range(3):
            part = dot_rt(dz_low[...], w_mid2[384 * di : 384 * (di + 1), :])
            for dj in range(3):
                lo = SIDE * di
                ep[dj, lo : lo + PX, :] += part[:, 128 * dj : 128 * (dj + 1)]
        grad = ep[1, SIDE : SIDE + PX, :]
        grad = grad + shift_cols(ep[0, SIDE : SIDE + PX, :], -1)
        grad = grad + shift_cols(ep[2, SIDE : SIDE + PX, :], 1)
        grad = grad.astype(BF16).astype(F32)
        v = z4[...] * lin4 + off4
        hat4 = (z4[...] - mu4) * rs4
        sg = sigmoid(v)
        dv4 = grad * (sg * (1.0 + v * (1.0 - sg)) * mref[...])
        dh[0] = dv4
        put(10, 0, jnp.sum(dv4, axis=0, keepdims=True))
        put(10, 1, jnp.sum(dv4 * hat4, axis=0, keepdims=True))
        send(10, 8)
        rest2()
        receive(10, 8)
        total = totals(10, 8)
        set_gvec((1, "b_in"), total[0:1, :])
        set_gvec((1, "g_in"), total[1:2, :])
        hat4 = (z4[...] - mu4) * rs4
        dz = lin4 * (dh[0] - total[0:1, :] / count1 - hat4 * (total[1:2, :] / count1)) * mref[...]
        dz4[k] = dz.astype(BF16)
        swap = to_twin(6, dz4.at[k], dz4.at[k])
        swap.start()
        swap.wait()

        def dy_block(b, acc):
            rows = pl.ds(pl.multiple_of(b * 64, 64), 64)
            dy = dot_rt(dz4[0, rows, :], w_in1[0]) + dot_rt(dz4[1, rows, :], w_in1[1])
            dy = dy + dv6[rows, :].astype(BF16).astype(F32)
            v = v3[rows, :]
            sg = sigmoid(v)
            dv = dy * (sg * (1.0 + v * (1.0 - sg)) * lanes(mref[rows, :], 4))
            v3[rows, :] = dv
            low = dv.astype(BF16).astype(F32)
            hat = (z3[rows, :] - mu3) * rs3
            hats = (zs[rows, :] - mus) * rss
            return tuple(
                x + fold8(y) for x, y in zip(acc, (dv, dv * hat, low, low * hats))
            )

        acc = lax.fori_loop(0, 4, dy_block, (zero512,) * 4)
        for j, x in enumerate(acc):
            put(11, 4 * j, jnp.sum(x, axis=0, keepdims=True))
        send(11, 16)
        both4 = jnp.concatenate([dz4[0], dz4[1]], axis=1)
        gw_in1[...] = dot_lt(y1[...], both4).astype(gw_in1.dtype)
        receive(11, 16)
        total = totals(11, 16)
        wide_back(
            total,
            0,
            (1, "g_out"),
            (1, "b_out"),
            lin3,
            mu3,
            rs3,
            z3,
            lambda rows: v3[rows, :],
            dz3,
        )
        wide_back(
            total,
            8,
            (0, "g_sc"),
            (0, "b_sc"),
            lins,
            mus,
            rss,
            zs,
            lambda rows: v3[rows, :].astype(BF16).astype(F32),
            dzs,
        )
        attended_grad(7, w_out1, a1, gw_out1)

        def short_back():
            part = dot_rt(dzs[...], w_sc[...])
            pdp[0] = jnp.where(k == 0, part[:, 256:512], part[:, 0:256])
            to_twin(8, pdp.at[0], pdp.at[1]).start()
            pdp[2] = jnp.where(k == 0, part[:, 0:256], part[:, 256:512])
            gw_sc[...] = dot_lt(pool[...], dzs[...]).astype(gw_sc.dtype)

        rest1 = attention_backward(
            12,
            0,
            mid1,
            q1,
            z2,
            rr1,
            w_sq0,
            w_ex0,
            gw_sq0,
            gw_ex0,
            cols1,
            w_mid0,
            gw_mid0,
            summed_grad,
            short_back,
        )

        for p in range(4):
            dh[p] = jnp.zeros((PX, 128), F32)
        for di in range(3):
            part = dot_rt(dz_low[...], w_mid0[384 * di : 384 * (di + 1), :])
            pr = 0 if di == 1 else 1
            for dj in range(3):
                x = part[:, 128 * dj : 128 * (dj + 1)]
                if dj == 0:
                    x = shift_cols(x, -1)
                p = 2 * pr + (0 if dj == 1 else 1)
                if di == 0:
                    dh[p, 0 : PX - SIDE, :] += x[SIDE:PX]
                else:
                    dh[p] += x

        def dv1_block(p, acc):
            z = z1[p]
            v = z * lin1 + off1
            sg = sigmoid(v)
            dv = dh[p] * (sg * (1.0 + v * (1.0 - sg)) * mref[...])
            dh[p] = dv
            return (acc[0] + fold8(dv), acc[1] + fold8(dv * ((z - mu1) * rs1)))

        t0, t1 = lax.fori_loop(0, 4, dv1_block, (zero8, zero8))
        put(13, 0, jnp.sum(t0, axis=0, keepdims=True))
        put(13, 1, jnp.sum(t1, axis=0, keepdims=True))
        send(13, 8)
        rest1()
        receive(13, 8)
        total = totals(13, 8)
        set_gvec((0, "b_in"), total[0:1, :])
        set_gvec((0, "g_in"), total[1:2, :])
        k1 = total[0:1, :] / (4.0 * count1)
        k2 = total[1:2, :] / (4.0 * count1)

        def dz1_block(p, _):
            hat = (z1[p] - mu1) * rs1
            dz1[k, p] = (lin1 * (dh[p] - k1 - hat * k2) * mref[...]).astype(BF16)
            return 0

        lax.fori_loop(0, 4, dz1_block, 0)
        swap = to_twin(9, dz1.at[k], dz1.at[k])
        swap.start()
        total = jnp.zeros((CIN, 128), F32)
        for p in range(4):
            total = total + dot_lt(um[p], dz1[k, p])
        gw_in0[...] = total.astype(gw_in0.dtype)
        swap.wait()
        to_twin(8, pdp.at[0], pdp.at[1]).wait()

        def du_block(p, _):
            mine = pl.ds(pl.multiple_of(256 * k, 256), 256)
            grad = dot_rt(dz1[0, p], w_in0[0, mine, :]) + dot_rt(dz1[1, p], w_in0[1, mine, :])
            grad = (grad + 0.25 * (pdp[1] + pdp[2])) * lanes(mref[...], 2)
            low = grad.astype(BF16)
            ibuf[0, p] = low[:, 0:128]
            ibuf[1, p] = low[:, 128:256]
            return 0

        lax.fori_loop(0, 4, du_block, 0)
        for j in range(2):
            move(
                ibuf.at[j],
                out_i.at[lax.rem(s, 2)],
                oi_s.at[j],
                oi_r.at[lax.rem(s, 2)],
                (2 * k + j, 2 * c + s // 2),
            )

        for slot in range(2):
            pltpu.make_async_copy(out_o.at[slot], out_o.at[slot], oo_r.at[slot]).wait()
            pltpu.make_async_copy(out_i.at[slot], out_i.at[slot], oi_r.at[slot]).wait()
        for slot in range(2):
            for kk in range(2):
                end_move(
                    img.at[slot, pl.ds(2 * kk, 2)],
                    img_s.at[slot, kk],
                    (2 * k + slot, 2 * c + kk),
                )
            end_move(cot.at[slot], ct_s.at[slot], (2 * k + slot, 2 * c + s // 2))
        for j in range(2):
            end_move(obuf.at[j], oo_s.at[j], (2 * k + j, 2 * c + s // 2))
            end_move(ibuf.at[j], oi_s.at[j], (2 * k + j, 2 * c + s // 2))
        for q in range(4):
            here = u.at[q, pl.ds(2 * k, 2)]
            pltpu.make_async_copy(here, here, bs.at[10 + q]).wait()
        for ph in range(PHASES):
            end_send(ph, 16 if ph in (2, 9, 11, 12) else 8, ph in (2, 6, 9, 12))

    return kernel


def call_kernel(n, operands):
    def vm(*shape, dtype=F32):
        return pltpu.VMEM(shape, dtype)

    def low(*shape):
        return pltpu.VMEM(shape, BF16)

    dma = pltpu.SemaphoreType.DMA
    scratch = [
        vm(PHASES, 16, 128),
        vm(PHASES, 2, n, 16, 128),
        vm(2, 2, 8, 128),
        low(4, 4, PX, 128),
        low(4, PX, CIN),
        low(PX, CIN),
        low(2, PX, 256),
        vm(PX, 128),
        vm(4, PX, 128),
        vm(PX, 256),
        vm(PX, 512),
        vm(PX, 512),
        vm(PX, 128),
        vm(PX, 256),
        vm(PX, 512),
        vm(PX, 512),
        low(PX, 1152),
        low(PX, 1152),
        vm(2, PX, 256),
        vm(2, PX, 256),
        low(PX, 256),
        low(PX, 256),
        low(PX, 512),
        vm(PX, 512),
        vm(PX, 256),
        vm(PX, 256),
        vm(2, PX, 128),
        vm(2, PX, 256),
        vm(3, PX, 256),
        low(2, PX, 128),
        low(2, 4, PX, 128),
        low(PX, 512),
        low(PX, 512),
        vm(3, PX + 2 * SIDE, 128),
        vm(4, PX, 128),
        low(2, PX, 256),
        low(2, 4, PX, 128),
        dma((PHASES,)),
        dma((PHASES, 2)),
        dma((14,)),
        dma((14,)),
        dma((2, 2)),
        dma((4,)),
        dma((2,)),
        dma((2,)),
        dma((2,)),
        dma((2,)),
        dma((2,)),
        dma((2,)),
    ]
    sds = jax.ShapeDtypeStruct
    outs = (
        sds((2, PX, 256), BF16),
        sds((2, 4, PX, 128), BF16),
        sds((CIN, 128), BF16),
        sds((1152, 256), BF16),
        sds((CMID, CSQ), BF16),
        sds((CSQ, 512), BF16),
        sds((CIN, 512), BF16),
        sds((CMID, 512), BF16),
        sds((512, CMID), BF16),
        sds((1152, 256), BF16),
        sds((CMID, CSQ), BF16),
        sds((CSQ, 512), BF16),
        sds((CMID, 512), BF16),
        sds((VROWS, VCOLS), F32),
    )
    vmem = pl.BlockSpec(memory_space=pltpu.VMEM)
    smem = pl.BlockSpec(memory_space=pltpu.SMEM)
    return pl.pallas_call(
        make_kernel(n),
        out_shape=outs,
        in_specs=[smem if i == 2 else vmem for i in range(len(operands))],
        out_specs=[vmem] * len(outs),
        scratch_shapes=scratch,
        compiler_params=pltpu.CompilerParams(
            collective_id=0, has_side_effects=True, vmem_limit_bytes=56 << 20
        ),
    )(*operands)


def unpack(flat, layout):
    pieces, offset = {}, 0
    for name, shape in layout:
        size = math.prod(shape)
        pieces[name] = flat[offset : offset + size].reshape(shape)
        offset += size
    return pieces


def per_device(images, cotangent, res_codes, section_weights):
    n = lax.axis_size("dp")
    k = lax.axis_index("dp") % 2
    flat = lax.all_gather(section_weights.astype(BF16), "dp", axis=1, tiled=True)
    flat = lax.all_gather(flat, "section", axis=0, tiled=True)
    w = [unpack(flat[i], layout) for i, layout in enumerate(layouts())]

    def half(x):
        size = x.shape[-1] // 2
        return lax.dynamic_slice_in_dim(x, k * size, size, x.ndim - 1)

    def mid(x):
        return half(x).reshape(1152, 256)

    vec = jnp.stack(
        [
            jnp.pad(half(w[i][name]) if cut else w[i][name], (0, VCOLS))[:VCOLS]
            for i, name, cut in VECTORS
        ]
        + [jnp.zeros((VCOLS,), BF16)] * (VROWS - len(VECTORS))
    ).astype(F32)
    planes = images.reshape(2, SIDE, 2, SIDE, 2, 128).transpose(0, 2, 4, 1, 3, 5)
    w_in1 = lax.dynamic_slice_in_dim(w[1]["w_in"], k * 512, 512, 0)
    operands = (
        planes.reshape(2, 4, PX, 128),
        cotangent.reshape(2, PX, 256),
        res_codes,
        w[0]["w_in"].reshape(CIN, 2, 128).transpose(1, 0, 2),
        mid(w[0]["w_mid"]),
        w[0]["w_sq"],
        w[0]["w_ex"],
        half(w[0]["w_sc"]),
        half(w[1]["w_out"]),
        w_in1.reshape(512, 2, 128).transpose(1, 0, 2),
        mid(w[2]["w_mid"]),
        w[2]["w_sq"],
        w[2]["w_ex"],
        half(w[3]["w_out"]),
        vec,
    )
    (
        out_o,
        out_i,
        g_in0,
        g_mid0,
        g_sq0,
        g_ex0,
        g_sc,
        g_out1,
        g_in1,
        g_mid2,
        g_sq2,
        g_ex2,
        g_out3,
        gvec,
    ) = call_kernel(n, operands)
    block_out = out_o.reshape(2, SIDE, SIDE, 256)
    input_grad = (
        out_i.reshape(2, 2, 2, SIDE, SIDE, 128).transpose(0, 3, 1, 4, 2, 5).reshape(images.shape)
    )

    first = (lax.axis_index("section") < 2) & (lax.axis_index("dp") < 2)

    def widen(x):
        zero = jnp.zeros_like(x)
        return jnp.where(
            k == 0, jnp.concatenate([x, zero], -1), jnp.concatenate([zero, x], -1)
        )

    def once(x, cut):
        keep = first if cut else first & (k == 0)
        return jnp.where(keep, x, jnp.zeros_like(x))

    grads = [{}, {}, {}, {}]
    for row, (i, name, cut) in enumerate(VECTORS):
        size = math.prod(dict(layouts()[i])[name])
        value = gvec[row, : size // 2 if cut else size]
        grads[i][name] = once(widen(value) if cut else value, cut).astype(BF16)
    grads[0]["w_in"] = widen(g_in0)
    grads[0]["w_mid"] = widen(g_mid0)
    grads[0]["w_sq"] = once(g_sq0, False)
    grads[0]["w_ex"] = once(g_ex0, False)
    grads[0]["w_sc"] = widen(g_sc)
    grads[1]["w_out"] = widen(g_out1)
    zero = jnp.zeros_like(g_in1)
    grads[1]["w_in"] = jnp.where(
        k == 0, jnp.concatenate([g_in1, zero], 0), jnp.concatenate([zero, g_in1], 0)
    )
    grads[2]["w_mid"] = widen(g_mid2)
    grads[2]["w_sq"] = once(g_sq2, False)
    grads[2]["w_ex"] = once(g_ex2, False)
    grads[3]["w_out"] = widen(g_out3)
    rows = []
    for i, layout in enumerate(layouts()):
        packed = jnp.concatenate([grads[i][name].reshape(-1) for name, _ in layout])
        rows.append(jnp.pad(packed, (0, WSLOTS - packed.shape[0])))
    packed = jnp.stack(rows)
    packed = lax.psum_scatter(packed, "section", scatter_dimension=0, tiled=True)
    packed = lax.psum_scatter(packed, "dp", scatter_dimension=1, tiled=True)
    return block_out, input_grad, packed.astype(F32)


def solution(mesh):
    return jax.shard_map(
        per_device,
        mesh=mesh,
        in_specs=(
            P("dp", None, None, "section"),
            P("dp", None, None, "section"),
            P("dp"),
            P("section", "dp"),
        ),
        out_specs=(
            P("dp", None, None, "section"),
            P("dp", None, None, "section"),
            P("section", "dp"),
        ),
        check_vma=False,
    )
```

profile of v0, /device:TPU:9, one launch (start us, length us, event | category | flops | bytes accessed | tf_op | source)
XLA Modules:
  0.0 963.5 jit_solution(17635336256378797061)
XLA Ops:
  7.2 2.2 convert_element_type.118
  9.5 57.9 %all-gather.4.cloned.1.call-done = bf16[1,1351680]{1,0:T(2,128)(2,1)} async-done(((bf16[1,168960]{1,0:T(2,128)(2,1)}), bf16[1,1351680]{1,0:T(2,128)(2,1)}) %all-gather.4.cloned.1.call-update) | async-done | bytes 2703376 | tf_op jit(solution)/shard_map/all_gather | solution.py:1026
  67.5 0.9 copy-done.7
  68.4 0.9 copy.24
  69.3 198.8 %all-gather.6.cloned.1.call-done = bf16[4,1,1351680]{2,1,0:T(2,128)(2,1)} async-done(((bf16[1,1,1351680]{2,1,0:T(2,128)(2,1)}), bf16[4,1,1351680]{2,1,0:T(2,128)(2,1)}) %all-gather.6.cloned.1.call-update) | async-done | bytes 10813456 | tf_op jit(solution)/shard_map/all_gather | solution.py:1027
  268.1 24.0 %copy.44 = bf16[4,1,1351680]{2,0,1:T(4,128)(2,1)S(1)} copy(bf16[4,1,1351680]{2,1,0:T(2,128)(2,1)} %all-gather.6.cloned.1.call-done) | data formatting | bytes 21626880
  292.1 1.5 slice_reduce_fusion.6
  293.6 25.0 %slice_reduce_fusion = (bf16[589824]{0:T(1024)(128)(2,1)S(1)}, bf16[589824]{0:T(1024)(128)(2,1)S(1)}) fusion(bf16[4,1351680]{1,0:T(4,128)(2,1)S(1)} %bitcast.102), kind=kLoop, calls=%fused_computation.8 | loop fusion | bytes 4718592 | tf_op jit(solution)/shard_map/slice | solution.py:1018
  318.6 1.4 slice_reduce_fusion.9
  320.0 2.1 slice_reduce_fusion.7
  322.1 18.0 %slice_reduce_fusion.2 = bf16[524288]{0:T(1024)(128)(2,1)S(1)} fusion(bf16[4,1351680]{1,0:T(4,128)(2,1)S(1)} %bitcast.105), kind=kLoop, calls=%fused_computation.10 | loop fusion | bytes 2097152 | tf_op jit(solution)/shard_map/slice | solution.py:1018
  340.1 12.2 %slice_reduce_fusion.3 = (bf16[262144]{0:T(1024)(128)(2,1)}, bf16[262144]{0:T(1024)(128)(2,1)}, bf16[262144]{0:T(1024)(128)(2,1)}) fusion(bf16[4,1351680]{1,0:T(4,128)(2,1)S(1)} %bitcast.106), kind=kLoop, calls=%fused_computation.13 | loop fusion | bytes 3145728 | tf_op jit(solution)/shard_map/slice | solution.py:1018
  354.7 0.7 copy.45
  355.5 1.5 reshape.195
  357.0 0.7 reshape.187
  357.7 1.7 reshape.190.w_ex0
  359.4 1.4 reshape.191
  360.9 1.0 reshape.199
  361.9 2.2 reshape.192
  364.1 2.0 reshape.193
  366.1 0.9 constant_dynamic-slice_fusion.18.w_sc
  367.0 1.8 constant_dynamic-slice_fusion.16
  368.7 1.8 copy.32
  370.5 1.8 copy.27
  372.3 0.7 reshape.198.w_ex2
  378.1 1.4 stack.78
  380.1 1.1 constant_dynamic-slice_fusion.15
  381.2 0.8 constant_dynamic-slice_fusion.14
  382.1 103.5 %shard_map.67 = (bf16[2,256,256]{2,1,0:T(8,128)(2,1)}, bf16[2,4,256,128]{3,2,1,0:T(8,128)(2,1)}, bf16[512,128]{1,0:T(8,128)(2,1)}, bf16[1152,256]{1,0:T(8,128)(2...) custom-call(bf16[2,4,256,128]{3,2,1,0:T(8,128)(2,1)} %bitcast.121, ...), custom_call_target="tpu_custom_call" | custom-call | tf_op jit(solution)/shard_map/pallas_call | solution.py:1002
  485.6 0.8 fusion.28
  486.5 0.8 fusion.29
  487.2 0.8 fusion.16
  488.1 0.8 fusion.6
  488.9 1.2 select_bitcast_fusion.3
  490.1 4.5 fusion.4
  494.6 4.5 stack.82
  501.3 1.3 dynamic-update-slice.6
  502.8 5.2 pad.119
  508.0 4.6 stack.81
  514.6 4.1 pad.118
  518.7 4.8 stack.80
  523.9 0.7 constant_dynamic-update-slice_fusion
  525.5 0.7 copy.35
  526.8 1.4 dynamic-update-slice.15
  528.2 1.4 dynamic-update-slice.16
  529.6 19.0 %dynamic-update-slice.17 = bf16[1347840]{0:T(1024)(128)(2,1)} dynamic-update-slice(bf16[1347840]{0:T(1024)(128)(2,1)} %dynamic-update-slice.16, bf16[589824]{0:T(1024)(128)(2,1)S(1)} %bitcast.116, s32[]{} %constant.221) | dynamic-update-slice | bytes 2359300
  548.6 1.4 dynamic-update-slice.18
  550.0 1.4 dynamic-update-slice.19
  551.4 2.3 dynamic-update-slice.20
  553.7 1.4 dynamic-update-slice.21
  555.1 1.4 dynamic-update-slice.22
  556.4 3.3 dynamic-update-slice.23
  559.7 1.4 dynamic-update-slice.24
  561.1 16.8 %dynamic-update-slice.25 = bf16[1347840]{0:T(1024)(128)(2,1)} dynamic-update-slice(bf16[1347840]{0:T(1024)(128)(2,1)} %dynamic-update-slice.24, bf16[524288]{0:T(1024)(128)(2,1)S(1)} %bitcast.118, s32[]{} %constant.229) | dynamic-update-slice | bytes 2097156
  577.9 1.4 dynamic-update-slice.26
  579.3 1.4 dynamic-update-slice.27
  580.8 2.5 pad.117
  583.3 3.0 stack.79
  586.3 28.2 %pad_maximum_fusion = bf16[4,1351680]{1,0:T(4,128)(2,1)} fusion(bf16[1,1351680]{1,0:T(2,128)(2,1)S(1)} %bitcast.112, bf16[1,1351680]{1,0:T(2,128)(2,1)S(1)} %bitcast.114, bf16[1,1351680]{1,0:T(2,128)(2,1)} %stack.80, bf16[1,1351680]{1,0:T(2,128)(2,1)S(1)} %stack.79), kind=kLoop, calls=%fused_computation | loop fusion | flops 43253760 | bytes 21626880 | tf_op jit(solution)/shard_map/stack | solution.py:1119
  615.8 209.5 %all-reduce.63.cloned.1.call-done = bf16[4,1351680]{1,0:T(4,128)(2,1)} async-done(((bf16[4,1351680]{1,0:T(4,128)(2,1)}), bf16[4,1351680]{1,0:T(4,128)(2,1)}) %all-reduce.63.cloned.1.call-update) | async-done | bytes 10813456
  825.3 8.4 constant_dynamic-slice_fusion.20
  835.6 1.3 copy.28
  836.9 116.5 %all-reduce.65.cloned.1.call-done = bf16[1,1351680]{1,0:T(2,128)(2,1)} async-done(((bf16[1,1351680]{1,0:T(2,128)(2,1)}), bf16[1,1351680]{1,0:T(2,128)(2,1)}) %all-reduce.65.cloned.1.call-update) | async-done | bytes 2703376
  953.5 2.4 dynamic-slice_convert_fusion
  (137 shorter events, 17.4 us)
Async XLA Ops:
  7.2 60.2 %all-gather.4.cloned.1.call-start = ((), (), s32[]{:S(2)}) async-start(), calls=%async_computation | async-start | bytes 6082560 | tf_op jit(solution)/shard_map/all_gather | solution.py:1026
  9.4 258.6 %all-gather.6.cloned.1.call-start = ((), (), s32[]{:S(2)}) async-start(), calls=%async_computation.1 | async-start | bytes 27033600 | tf_op jit(solution)/shard_map/all_gather | solution.py:1027
  67.4 1.0 copy-start.7
  67.4 757.9 %all-reduce.63.cloned.1.call-start = ((), (), s32[]{:S(2)}) async-start(), calls=%async_computation.2 | async-start | bytes 21626880
  357.7 3.2 copy-start.2
  360.9 5.2 copy-start.1
  361.9 18.2 %copy-start = (bf16[9,128,512]{2,1,0:T(8,128)(2,1)S(1)}, bf16[9,128,512]{2,1,0:T(8,128)(2,1)}, u32[]{:S(2)}) copy-start(bf16[9,128,512]{2,1,0:T(8,128)(2,1)} %reshape.195) | copy-start | bytes 3538948
  367.0 14.3 %copy-start.3 = (bf16[256,1024]{1,0:T(8,128)(2,1)S(1)}, bf16[256,1024]{1,0:T(8,128)(2,1)}, u32[]{:S(2)}) copy-start(bf16[256,1024]{1,0:T(8,128)(2,1)} %reshape.199) | copy-start | bytes 1572868
  367.0 14.3 %copy-start.4 = (bf16[256,1024]{1,0:T(8,128)(2,1)S(1)}, bf16[256,1024]{1,0:T(8,128)(2,1)}, u32[]{:S(2)}) copy-start(bf16[256,1024]{1,0:T(8,128)(2,1)} %reshape.192) | copy-start | bytes 1572868
  494.6 4.5 copy-start.6
  499.4 0.9 copy-start.15
  499.4 1.4 copy-start.17
  508.0 4.6 copy-start.12
  512.6 0.9 copy-start.11
  518.7 4.8 copy-start.14
  518.7 5.9 copy-start.5
  523.6 1.8 copy-start.16
  523.6 1.8 copy-start.13
  523.9 2.3 copy-start.9
  529.6 56.6 %slice-start.2 = ((s8[5406720]{0:T(1024)(128)(4,1)}), s8[1212416]{0:T(1024)(128)(4,1)S(1)}, s32[]{:S(2)}) async-start(s8[5406720]{0:T(1024)(128)(4,1)} %bitcast.113), calls=%async_computation.6 | async-start | bytes 2424832
  580.8 5.5 slice-start
  580.8 5.5 slice-start.3
  583.2 3.0 slice-start.1
  614.5 0.7 copy-start.19
  614.6 338.9 %all-reduce.65.cloned.1.call-start = ((), (), s32[]{:S(2)}) async-start(), calls=%async_computation.3 | async-start | bytes 10813440
  833.7 0.7 copy-start.18
  833.7 1.9 copy-start.8
  833.7 122.2 %copy-start.10 = (bf16[2,256,256]{2,1,0:T(8,128)(2,1)S(1)}, bf16[2,256,256]{2,1,0:T(8,128)(2,1)}, u32[]{:S(2)}) copy-start(bf16[2,256,256]{2,1,0:T(8,128)(2,1)} %get-tuple-element.17) | copy-start | bytes 786436
Sparse Core Ops, SparseCore 0:
  10.2 57.1 all-gather.3
  69.3 198.7 all-gather.5
  614.7 210.5 all-reduce.62
  833.9 119.5 all-reduce.64
where the time goes:
time: 979 us; the launch traced here: 964 us
  waiting for transfers between devices  583 us (60%)
  local copies, waits for them, and re-layouts  220 us (22%)
  Pallas kernels  104 us (11%)
  other arithmetic  41.9 us (4%)
  between operations  15.5 us (2%)
    unnamed x6, waiting for transfers between devices  326 us
    all_gather x1, waiting for transfers between devices, per_device(): flat = lax.all_gather(flat, 'section', axis=0, tiled=True)  199 us
    pallas_call x1, Pallas kernels, call_kernel(): pl.pallas_call(make_kernel(n), out_shape=outs, in_specs=[smem if i == 2 e...  104 us
    unnamed x85, local copies, waits for them, and re-layouts  97.9 us
    slice x10, local copies, waits for them, and re-layouts, unpack(): pieces[name] = flat[offset:offset + size].reshape(shape)  62.6 us
    all_gather x1, waiting for transfers between devices, per_device(): lax.all_gather(section_weights.astype(BF16), 'dp', axis=1, tiled=True)  57.9 us
    another operation x1, other arithmetic, per_device(): packed = jnp.stack(rows)  28.2 us
  transfers between devices with their start and end apart: 4, of which 4 were waited for; matrix products, arithmetic and copies ran while one was open for 0% of the time, Pallas kernels for 0%

commit v1 on v0

--- a/solution.py
+++ b/solution.py
@@ -1,5 +1,3 @@
-import math
-
 import jax
 import jax.numpy as jnp
 from jax import lax
@@ -23,59 +21,50 @@
 PHASES = 14
 
 
-def layouts():
-    first = (
-        ("w_in", (CIN, CMID)),
-        ("g_in", (CMID,)),
-        ("b_in", (CMID,)),
-        ("w_mid", (9, HALF, 2 * CMID)),
-        ("g_mid", (2 * CMID,)),
-        ("b_mid", (2 * CMID,)),
-        ("w_sq", (CMID, CSQ)),
-        ("g_sq", (CSQ,)),
-        ("b_sq", (CSQ,)),
-        ("w_ex", (CSQ, 2 * CMID)),
-        ("b_ex", (2 * CMID,)),
-        ("w_sc", (CIN, COUT)),
-        ("g_sc", (COUT,)),
-        ("b_sc", (COUT,)),
-    )
-    second = (
-        ("w_out", (CMID, COUT)),
-        ("g_out", (COUT,)),
-        ("b_out", (COUT,)),
-        ("w_in", (COUT, CMID)),
-        ("g_in", (CMID,)),
-        ("b_in", (CMID,)),
-    )
-    return (first, second, first[3:11], second[:3])
-
-
-VECTORS = (
-    (0, "g_in", True),
-    (0, "b_in", True),
-    (0, "g_mid", True),
-    (0, "b_mid", True),
-    (0, "g_sq", False),
-    (0, "b_sq", False),
-    (0, "b_ex", False),
-    (0, "g_sc", True),
-    (0, "b_sc", True),
-    (1, "g_out", True),
-    (1, "b_out", True),
-    (1, "g_in", True),
-    (1, "b_in", True),
-    (2, "g_mid", True),
-    (2, "b_mid", True),
-    (2, "g_sq", False),
-    (2, "b_sq", False),
-    (2, "b_ex", False),
-    (3, "g_out", True),
-    (3, "b_out", True),
-)
-VROW = {(s, name): i for i, (s, name, _) in enumerate(VECTORS)}
-VROWS = 24
-VCOLS = 512
+class Matrix:
+    def __init__(self, index, row, start, blocks, pieces, rows, first=0, split="columns"):
+        self.index = index
+        self.row = row
+        self.start = start
+        self.blocks = blocks
+        self.pieces = pieces
+        self.rows = rows
+        self.first = first
+        self.split = split
+        self.flat = blocks * rows
+        self.width = 128 * (blocks // 2 if split == "columns" else blocks)
+
+
+IN0 = Matrix(0, 0, 0, 2, 8, 16)
+MID0 = Matrix(1, 0, 1028, 4, 6, 48)
+REST0 = Matrix(2, 0, 5636, 1, 8, 25, split="none")
+SC0 = Matrix(3, 0, 6418, 8, 8, 16)
+OUT1 = Matrix(4, 1, 0, 8, 4, 16, first=4)
+IN1 = Matrix(5, 1, 2064, 2, 8, 16, split="rows")
+MID2 = Matrix(6, 2, 0, 4, 6, 48)
+REST2 = Matrix(7, 2, 4608, 1, 8, 25, split="none")
+OUT3 = Matrix(8, 3, 0, 8, 4, 16)
+MATRICES = (IN0, MID0, REST0, SC0, OUT1, IN1, MID2, REST2, OUT3)
+PRODUCTS = (IN0, MID0, SC0, OUT1, IN1, MID2, OUT3)
+USED = (10530, 4116, 5390, 2064)
+REST_ROWS = 782
+HOME_ROWS = 1152
+REST_PART = 98
+AT_SQ, AT_GSQ, AT_BSQ, AT_EX, AT_BEX = 8, 264, 265, 266, 778
+TABLE = {
+    (0, "g_in"): (0, 1024, 1),
+    (0, "b_in"): (2, 1026, 1),
+    (0, "g_sc"): (4, 10514, 4),
+    (0, "b_sc"): (12, 10522, 4),
+    (1, "g_out"): (20, 2048, 4),
+    (1, "b_out"): (28, 2056, 4),
+    (1, "g_in"): (36, 4112, 1),
+    (1, "b_in"): (38, 4114, 1),
+    (3, "g_out"): (40, 2048, 4),
+    (3, "b_out"): (48, 2056, 4),
+}
+TABLE_ROWS = 56
+RANGES = ((0, 1024, 4, 0), (0, 10514, 16, 4), (1, 2048, 16, 20), (1, 4112, 4, 36), (3, 2048, 16, 40))
 
 
 def dot(a, b):
@@ -108,37 +97,17 @@
 
 def make_kernel(n):
     chips = n // 2
+    shard_rows = WSLOTS // (128 * n)
+    fill_rows = shard_rows + 20 * (4 * n - 1)
 
     def kernel(
         img,
         cot,
         codes,
-        w_in0,
-        w_mid0,
-        w_sq0,
-        w_ex0,
-        w_sc,
-        w_out1,
-        w_in1,
-        w_mid2,
-        w_sq2,
-        w_ex2,
-        w_out3,
-        vec,
+        shard,
         out_o,
         out_i,
-        gw_in0,
-        gw_mid0,
-        gw_sq0,
-        gw_ex0,
-        gw_sc,
-        gw_out1,
-        gw_in1,
-        gw_mid2,
-        gw_sq2,
-        gw_ex2,
-        gw_out3,
-        gvec,
+        out_w,
         snd,
         rcv,
         side_t,
@@ -176,6 +145,78 @@
         dh,
         obuf,
         ibuf,
+        sround,
+        nought,
+        fill,
+        fill2,
+        table,
+        w_in0,
+        w_mid0,
+        rest0,
+        w_sc,
+        w_out1,
+        w_in1,
+        w_mid2,
+        rest2,
+        w_out3,
+        ln_in0,
+        ln_mid0,
+        ln_rest0,
+        ln_sc,
+        ln_out1,
+        ln_in1,
+        ln_mid2,
+        ln_rest2,
+        ln_out3,
+        st_in0,
+        st_mid0,
+        st_sc,
+        st_out1,
+        st_in1,
+        st_mid2,
+        st_out3,
+        gw_in0,
+        gw_mid0,
+        gw_sc,
+        gw_out1,
+        gw_in1,
+        gw_mid2,
+        gw_out3,
+        ga_mid0,
+        ga_sc,
+        ga_out1,
+        ga_in1,
+        ga_mid2,
+        ga_out3,
+        gp_mid0,
+        gp_sc,
+        gp_out1,
+        gp_in1,
+        gp_mid2,
+        gp_out3,
+        gb_in0,
+        gb_mid0,
+        gb_sc,
+        gb_out1,
+        gb_in1,
+        gb_mid2,
+        gb_out3,
+        gf_in0,
+        gf_mid0,
+        gf_sc,
+        gf_out1,
+        gf_in1,
+        gf_mid2,
+        gf_out3,
+        rg0,
+        rg2,
+        rl0,
+        rl2,
+        rf0,
+        rf2,
+        gvt,
+        gvl,
+        gvs,
         ssem,
         rsem,
         bs,
@@ -188,6 +229,21 @@
         oo_r,
         oi_s,
         oi_r,
+        h_s,
+        t_r,
+        h_r,
+        a_s,
+        c_r,
+        f_s,
+        q_r,
+        ga_s,
+        ga_r,
+        gb_s,
+        gb_r,
+        gc_s,
+        gc_r,
+        v_s,
+        v_r,
     ):
         s = lax.axis_index("section")
         d = lax.axis_index("dp")
@@ -200,24 +256,19 @@
             gg = lax.rem(g + o, n)
             return ((gg // chips) * 2 + m, 2 * (gg % chips) + kk)
 
+        nought[...] = jnp.zeros(nought.shape, F32)
+        sround[...] = shard[...].astype(BF16).astype(F32)
+
         barrier = pltpu.get_barrier_semaphore()
-
-        def greet(o, _):
-            pl.semaphore_signal(barrier, inc=1, device_id=peer(o, 0), device_id_type=MESH)
-            pl.semaphore_signal(barrier, inc=1, device_id=peer(o, 1), device_id_type=MESH)
+        me = s * n + d
+
+        def greet(i, _):
+            e = lax.rem(me + i, 4 * n)
+            pl.semaphore_signal(barrier, inc=1, device_id=(e // n, e % n), device_id_type=MESH)
             return 0
 
-        lax.fori_loop(1, n, greet, 0)
-        pl.semaphore_signal(barrier, inc=1, device_id=(s, 2 * c + 1 - k), device_id_type=MESH)
-        for i in range(2):
-            for kk in range(2):
-                pl.semaphore_signal(
-                    barrier,
-                    inc=1,
-                    device_id=(2 * i + 1 - m, 2 * c + kk),
-                    device_id_type=MESH,
-                )
-        pl.semaphore_wait(barrier, 2 * n - 1 + 4)
+        lax.fori_loop(1, 4 * n, greet, 0)
+        pl.semaphore_wait(barrier, 4 * n - 1)
 
         def to_twin(i, src, dst):
             return pltpu.make_async_remote_copy(
@@ -243,6 +294,118 @@
             @pl.when(jnp.logical_not(own))
             def _():
                 pltpu.make_async_copy(src, src, s_sem).wait()
+
+        def is_self(dev):
+            return (dev[0] == s) & (dev[1] == d)
+
+        def move_rows(src, src_at, dst, dst_at, count, full, s_sem, r_sem, dev):
+            def go(size, at):
+                move(
+                    src.at[pl.ds(src_at + at, size)],
+                    dst.at[pl.ds(dst_at + at, size)],
+                    s_sem,
+                    r_sem,
+                    dev,
+                )
+
+            def chunks(size, start, many):
+                def one(i, _):
+                    go(size, start + i * size)
+                    return 0
+
+                lax.fori_loop(0, many, one, 0)
+
+            if full > 4:
+
+                @pl.when(count == full)
+                def _():
+                    go(full, 0)
+
+                @pl.when(count < full)
+                def _():
+                    if full > 16:
+                        chunks(16, 0, count // 16)
+                        chunks(1, (count // 16) * 16, count % 16)
+                    else:
+                        chunks(1, 0, count)
+
+            else:
+                chunks(1, 0, count)
+            return jnp.where(is_self(dev), 0, count)
+
+        def fill_up(src, dst, first, last, sem):
+            def chunks(size, start, many):
+                def one(i, _):
+                    pltpu.make_async_copy(
+                        src.at[pl.ds(0, size)], dst.at[pl.ds(start + i * size, size)], sem
+                    ).start()
+                    return 0
+
+                lax.fori_loop(0, many, one, 0)
+
+            count = last - first
+            chunks(128, first, count // 128)
+            chunks(16, first + (count // 128) * 128, count % 128 // 16)
+            chunks(1, first + (count // 16) * 16, count % 16)
+
+        used = jnp.where(
+            s == 0, USED[0], jnp.where(s == 1, USED[1], jnp.where(s == 2, USED[2], USED[3]))
+        )
+        fill_up(nought, out_w, jnp.clip(used - d * shard_rows, 0, shard_rows), shard_rows, gc_r)
+
+        mine_from = d * shard_rows
+        mine_to = mine_from + shard_rows
+
+        def scatter_pieces(mat, land):
+            total = mat.pieces * 4 * (2 if mat.split == "rows" else 1)
+            first = jnp.maximum(mine_from - mat.start, 0) // mat.flat
+            last = (jnp.maximum(mine_to - mat.start, 0) + mat.flat - 1) // mat.flat
+
+            def one(p, sent):
+                start = mat.start + p * mat.flat
+                lo = jnp.maximum(start, mine_from)
+                count = jnp.minimum(start + mat.flat, mine_to) - lo
+                h = p // (4 * mat.pieces)
+                q = p % (4 * mat.pieces)
+                dev = (q // mat.pieces, mat.first + q % mat.pieces)
+                return sent + move_rows(
+                    sround,
+                    lo - mine_from,
+                    land,
+                    h * mat.flat + lo - start,
+                    count,
+                    mat.flat,
+                    h_s,
+                    h_r.at[mat.index],
+                    dev,
+                )
+
+            return lax.fori_loop(first, jnp.minimum(last, total), one, jnp.int32(0))
+
+        def scatter_table(start, rows, at):
+            lo = jnp.maximum(start, mine_from)
+            count = jnp.maximum(jnp.minimum(start + rows, mine_to) - lo, 0)
+
+            def one(i, sent):
+                e = lax.rem(me + i, 4 * n)
+                return sent + move_rows(
+                    sround,
+                    lo - mine_from,
+                    table,
+                    at + lo - start,
+                    count,
+                    rows,
+                    h_s,
+                    t_r,
+                    (e // n, e % n),
+                )
+
+            return lax.fori_loop(0, jnp.where(count > 0, 4 * n, 0), one, jnp.int32(0))
+
+        def when_row(r, body):
+            return lax.cond(s == r, body, lambda: jnp.int32(0))
+
+        sent = when_row(0, lambda: scatter_pieces(IN0, ln_in0))
 
         for slot in range(2):
             for kk in range(2):
@@ -268,6 +431,271 @@
         side_copy.start()
         snd[...] = jnp.zeros(snd.shape, F32)
 
+        def row0():
+            count = scatter_table(*RANGES[0][1:]) + scatter_pieces(MID0, ln_mid0)
+            count = count + scatter_pieces(REST0, ln_rest0) + scatter_pieces(SC0, ln_sc)
+            return count + scatter_table(*RANGES[1][1:])
+
+        def row1():
+            count = scatter_pieces(OUT1, ln_out1) + scatter_table(*RANGES[2][1:])
+            return count + scatter_pieces(IN1, ln_in1) + scatter_table(*RANGES[3][1:])
+
+        sent = sent + when_row(0, row0)
+        sent = sent + when_row(1, row1)
+        sent = sent + when_row(2, lambda: scatter_pieces(MID2, ln_mid2) + scatter_pieces(REST2, ln_rest2))
+        sent = sent + when_row(3, lambda: scatter_pieces(OUT3, ln_out3) + scatter_table(*RANGES[4][1:]))
+
+        fill_up(nought, fill, sent, fill_rows, h_s)
+
+        def holds(mat):
+            return (d >= mat.first) & (d < mat.first + mat.pieces)
+
+        def full_wait(ref, sem):
+            pltpu.make_async_copy(ref, ref, sem).wait()
+
+        def cut(mat, land, stage):
+            for j in range(mat.blocks):
+                for h in range(2):
+                    if mat.split == "rows":
+                        x = land[pl.ds(h * mat.flat + j, mat.rows, stride=mat.blocks), :]
+                        stage[h, j] = x.astype(BF16)
+                    elif j // (mat.blocks // 2) == h:
+                        x = land[pl.ds(j, mat.rows, stride=mat.blocks), :]
+                        at = 128 * (j % (mat.blocks // 2))
+                        stage[h, :, at : at + 128] = x.astype(BF16)
+
+        def spread(mat, land, stage, whole):
+            @pl.when(holds(mat))
+            def _():
+                full_wait(land, h_r.at[mat.index])
+                if mat.split != "none":
+                    cut(mat, land, stage)
+                p = s * mat.pieces + d - mat.first
+
+                def one(i, _):
+                    e = lax.rem(d + i, n)
+                    h = e % 2
+                    if mat.split == "none":
+                        src, dst = land, whole.at[pl.ds(p * mat.flat, mat.flat)]
+                    elif mat.split == "rows":
+                        src, dst = stage.at[h], whole.at[:, p]
+                    else:
+                        src, dst = stage.at[h], whole.at[p]
+                    move(src, dst, a_s.at[mat.index], c_r.at[mat.index], (s, e))
+                    return 0
+
+                lax.fori_loop(0, n, one, 0)
+
+        def quarters(mat, whole, first, many):
+            if mat.split == "none":
+                size = mat.flat * mat.pieces
+                return whole.at[pl.ds(first * size, many * size)]
+            if mat.split == "rows":
+                return whole.at[:, pl.ds(first * mat.pieces, many * mat.pieces)]
+            return whole.at[pl.ds(first * mat.pieces, many * mat.pieces)]
+
+        def pass_on(mat, whole):
+            here = quarters(mat, whole, s, 1)
+            full_wait(here, c_r.at[mat.index])
+            for i in range(1, 4):
+                pltpu.make_async_remote_copy(
+                    here,
+                    here,
+                    f_s.at[mat.index],
+                    q_r.at[mat.index],
+                    device_id=(lax.rem(s + i, 4), d),
+                    device_id_type=MESH,
+                ).start()
+
+        def arrived(mat, whole):
+            full_wait(quarters(mat, whole, 0, 3), q_r.at[mat.index])
+
+        def end_spread(mat, land, stage, whole):
+            @pl.when(holds(mat))
+            def _():
+                rows = mat.flat if mat.split == "none" else mat.rows * mat.width // 256
+                full_wait(fill.at[pl.ds(0, (n - 1) * rows)], a_s.at[mat.index])
+
+            full_wait(quarters(mat, whole, 0, 3), f_s.at[mat.index])
+
+        @pl.when(holds(IN0))
+        def _():
+            full_wait(ln_in0, h_r.at[0])
+            cut(IN0, ln_in0, st_in0)
+
+            def one(i, _):
+                e = lax.rem(me + i, 4 * n)
+                h = e % 2
+                move(
+                    st_in0.at[h],
+                    w_in0.at[h, s * 8 + d],
+                    a_s.at[0],
+                    c_r.at[0],
+                    (e // n, e % n),
+                )
+                return 0
+
+            lax.fori_loop(0, 4 * n, one, 0)
+
+        spread(MID0, ln_mid0, st_mid0, w_mid0)
+
+        def shed(mat, gw, land):
+            for i in range(1, 4):
+                to = lax.rem(s + i, 4)
+                pltpu.make_async_remote_copy(
+                    gw.at[pl.ds(to * mat.pieces, mat.pieces)],
+                    land.at[i - 1],
+                    ga_s.at[mat.index],
+                    ga_r.at[mat.index],
+                    device_id=(to, d),
+                    device_id_type=MESH,
+                ).start()
+
+        def shed_more(mat, gw, land, part, land2):
+            full_wait(land, ga_r.at[mat.index])
+
+            def one(i, _):
+                x = gw[s * mat.pieces + i].astype(F32)
+                for j in range(3):
+                    x = x + land[j, i].astype(F32)
+                part[i] = x.astype(BF16)
+                move(
+                    part.at[i],
+                    land2.at[c, k],
+                    gb_s.at[mat.index],
+                    gb_r.at[mat.index],
+                    (s, mat.first + i),
+                )
+                return 0
+
+            lax.fori_loop(0, mat.pieces, one, 0)
+
+        def home_rows(src, src_at, start, rows, limit, r, active):
+            left = jnp.int32(0)
+            for i in range((rows + shard_rows - 2) // shard_rows + 1):
+                owner = start // shard_rows + i
+                lo = jnp.maximum(start, owner * shard_rows)
+                hi = jnp.minimum(jnp.minimum(start + rows, limit), (owner + 1) * shard_rows)
+                count = jnp.where(active, jnp.maximum(hi - lo, 0), 0)
+                owner = jnp.minimum(owner, n - 1)
+
+                def go():
+                    return move_rows(
+                        src,
+                        src_at + lo - start,
+                        out_w,
+                        lo - owner * shard_rows,
+                        count,
+                        rows,
+                        gc_s,
+                        gc_r,
+                        (r, owner),
+                    )
+
+                left = left + lax.cond(count > 0, go, lambda: jnp.int32(0))
+            return left
+
+        def home(mat, land2, flat):
+            @pl.when(holds(mat))
+            def _():
+                full_wait(land2, gb_r.at[mat.index])
+                for h in range(2):
+                    x = jnp.sum(land2[:, h].astype(F32), axis=0)
+                    for j in range(mat.width // 128):
+                        if mat.split == "rows":
+                            at = h * mat.flat + j
+                        else:
+                            at = h * (mat.blocks // 2) + j
+                        flat[pl.ds(at, mat.rows, stride=mat.blocks), :] = x[:, 128 * j : 128 * (j + 1)]
+
+            p = s * mat.pieces + d - mat.first
+            left = home_rows(
+                flat, 0, mat.start + p * mat.flat, mat.flat, USED[mat.row], mat.row, holds(mat)
+            )
+            if mat.split == "rows":
+                p = p + 4 * mat.pieces
+                left = left + home_rows(
+                    flat,
+                    mat.flat,
+                    mat.start + p * mat.flat,
+                    mat.flat,
+                    USED[mat.row],
+                    mat.row,
+                    holds(mat),
+                )
+            return left
+
+        def end_shed(mat, gw, land):
+            full_wait(land, ga_s.at[mat.index])
+
+            @pl.when(holds(mat))
+            def _():
+                full_wait(gw.at[pl.ds(0, mat.pieces - 1)], gb_s.at[mat.index])
+
+            @pl.when(jnp.logical_not(holds(mat)))
+            def _():
+                full_wait(gw.at[pl.ds(0, mat.pieces)], gb_s.at[mat.index])
+
+        def rest_meet(i, mat, rg, land):
+            @pl.when((s == mat.row) & (d < 8))
+            def _():
+                pltpu.make_async_remote_copy(
+                    rg.at[pl.ds(REST_PART * d, REST_PART)],
+                    land,
+                    v_s.at[i],
+                    v_r.at[i],
+                    device_id=(s + 1, d),
+                    device_id_type=MESH,
+                ).start()
+
+        def rest_home(i, mat, rg, land, flat):
+            active = (s == mat.row + 1) & (d < 8)
+            at = REST_PART * jnp.minimum(d, 7)
+
+            @pl.when(active)
+            def _():
+                full_wait(land, v_r.at[i])
+                flat[...] = rg[pl.ds(at, REST_PART), :] + land[...]
+
+            return home_rows(
+                flat, 0, mat.start + at, REST_PART, mat.start + REST_ROWS, mat.row, active
+            )
+
+        def table_meet(i, first, rows):
+            @pl.when((s == 0) & (d < 2))
+            def _():
+                pltpu.make_async_remote_copy(
+                    gvt.at[pl.ds(first, rows)],
+                    gvl.at[pl.ds(first, rows)],
+                    v_s.at[i],
+                    v_r.at[i],
+                    device_id=(s + 1, d),
+                    device_id_type=MESH,
+                ).start()
+
+        def table_home(i, first, rows):
+            active = (s == 1) & (d < 2)
+
+            @pl.when(active)
+            def _():
+                span = pl.ds(first, rows)
+                full_wait(gvl.at[span], v_r.at[i])
+                gvs[first : first + rows, :] = gvt[first : first + rows, :] + gvl[first : first + rows, :]
+
+            left = jnp.int32(0)
+            for (r, _), (at, start, many) in TABLE.items():
+                if first <= at < first + rows:
+                    left = left + home_rows(
+                        gvs,
+                        at + many * k,
+                        start + many * k,
+                        many,
+                        start + 2 * many,
+                        r,
+                        active,
+                    )
+            return left
+
         def put(ph, base, value):
             for j in range(value.shape[1] // 128):
                 snd[ph, base + j : base + j + 1, :] = value[:, 128 * j : 128 * (j + 1)]
@@ -308,11 +736,8 @@
                 pltpu.make_async_copy(theirs, theirs, rsem.at[ph, 1 - k]).wait()
 
         def end_send(ph, rows, both=False):
-            mine = rcv.at[ph, k, pl.ds(1, n - 1), pl.ds(0, rows)]
-            pltpu.make_async_copy(mine, mine, ssem.at[ph]).wait()
-            if both:
-                theirs = rcv.at[ph, 1 - k, :, pl.ds(0, rows)]
-                pltpu.make_async_copy(theirs, theirs, ssem.at[ph]).wait()
+            many = 2 * n - 1 if both else n - 1
+            full_wait(fill.at[pl.ds(0, many * rows)], ssem.at[ph])
 
         def totals(ph, rows):
             return jnp.sum(rcv[ph, k, :, 0:rows, :], axis=0)
@@ -327,20 +752,28 @@
                 [rcv[ph, h, :, base + j, :] for j in range(width // 128)], axis=1
             )
 
-        def vrow(key, width):
-            i = VROW[key]
-            return vec[i : i + 1, 0:width]
+        def rows_of(ref, at, many):
+            return jnp.concatenate([ref[pl.ds(at + j, 1), :] for j in range(many)], axis=1)
+
+        def vrow(key):
+            at, _, many = TABLE[key]
+            return rows_of(table, at + many * k, many)
 
         def set_gvec(key, value):
-            i = VROW[key]
-            gvec[i : i + 1, 0 : value.shape[1]] = value
+            at, _, many = TABLE[key]
+            for j in range(many):
+                gvt[pl.ds(at + many * k + j, 1), :] = value[:, 128 * j : 128 * (j + 1)]
+
+        def set_rows(ref, at, value):
+            for j in range(value.shape[1] // 128):
+                ref[at + j : at + j + 1, :] = value[:, 128 * j : 128 * (j + 1)]
 
         def mean_rstd(total, base, width, count):
             mu = row(total, base, width) / count
             second = row(total, base + width // 128, width) / count
             return mu, lax.rsqrt(jnp.maximum(second - mu * mu, 0.0) + EPS)
 
-        gvec[...] = jnp.zeros(gvec.shape, F32)
+        gvt[...] = jnp.zeros(gvt.shape, F32)
 
         side_copy.wait()
         side_row = jnp.where(
@@ -381,9 +814,10 @@
             return 0
 
         lax.fori_loop(0, 8, mask_block, 0)
+        full_wait(w_in0.at[k], c_r.at[0])
 
         def z1_block(p, carry):
-            z = dot(um[p], w_in0[k])
+            z = dot(um[p], w_in0[k].reshape(CIN, 128))
             z1[p] = z
             return (carry[0] + fold8(z), carry[1] + fold8(z * z))
 
@@ -393,10 +827,10 @@
         put(0, 1, jnp.sum(t1, axis=0, keepdims=True))
         put(0, 2, side_row)
         send(0, 8)
-        z = dot(pool[...], w_sc[...])
-        zs[...] = z
-        sum_s = jnp.sum(z, axis=0, keepdims=True)
-        sq_s = jnp.sum(z * z, axis=0, keepdims=True)
+        pass_on(MID0, w_mid0)
+        spread(REST0, ln_rest0, None, rest0)
+        spread(SC0, ln_sc, st_sc, w_sc)
+        full_wait(table, t_r)
         receive(0, 8)
         total = totals(0, 8)
         sides = across(0, k, 2, 128)
@@ -404,8 +838,8 @@
         count1 = jnp.sum(sides * sides, axis=0, keepdims=True)
         counts = {w: lanes(count1, w // 128) for w in (128, 256, 512)}
         mu1, rs1 = mean_rstd(total, 0, 128, 4.0 * count1)
-        lin1 = rs1 * vrow((0, "g_in"), 128)
-        off1 = vrow((0, "b_in"), 128) - mu1 * lin1
+        lin1 = rs1 * vrow((0, "g_in"))
+        off1 = vrow((0, "b_in")) - mu1 * lin1
 
         colpos = lax.broadcasted_iota(jnp.int32, (PX, 128), 0) % SIDE
 
@@ -439,17 +873,24 @@
                     store_tap(cols1, di, dj, x, rshift)
 
         def conv_forward(ph, cols, w_mid, zref):
-            z = dot(cols[...], w_mid[...])
+            z = dot(cols[...], w_mid[...].reshape(1152, 256))
             zref[...] = z
             zm = z * lanes(mref[...], 2)
             put(ph, 0, jnp.sum(zm, axis=0, keepdims=True))
             put(ph, 2, jnp.sum(zm * z, axis=0, keepdims=True))
             send(ph, 8)
 
-        def attention_forward(ph, twin, total, sec, zref, rr, w_sq, w_ex, aref, beside):
+        def small(rest):
+            w_sq = rest[AT_SQ : AT_SQ + CMID, :]
+            w_ex = jnp.concatenate(
+                [rest[pl.ds(AT_EX + j, CSQ, stride=4), :] for j in range(4)], axis=1
+            )
+            return w_sq, w_ex
+
+        def attention_forward(ph, twin, total, rest, zref, rr, aref, beside):
             mu, rs = mean_rstd(total, 0, 256, counts[256])
-            lin = rs * vrow((sec, "g_mid"), 256)
-            off = vrow((sec, "b_mid"), 256) - mu * lin
+            lin = rs * rows_of(rest, 2 * k, 2)
+            off = rows_of(rest, 4 + 2 * k, 2) - mu * lin
 
             def block(b, acc):
                 rows = pl.ds(pl.multiple_of(b * 64, 64), 64)
@@ -461,20 +902,22 @@
             acc = lax.fori_loop(0, 4, block, jnp.zeros((8, 256), F32))
             pooled_own = jnp.sum(acc, axis=0, keepdims=True) * lanes(inv_own, 2)
             put(ph, 0, pooled_own)
-            send(ph, 16 if beside is not None else 8, both=True)
+            send(ph, 8, both=True)
             swap = to_twin(twin, rr.at[k], rr.at[k])
             swap.start()
-            receive(ph, 16 if beside is not None else 8, both=True)
+            beside()
+            receive(ph, 8, both=True)
+            w_sq, w_ex = small(rest)
             pooled = across(ph, 0, 0, 256) + across(ph, 1, 0, 256)
-            zq = dot_hi(pooled, w_sq[...].astype(F32))
+            zq = dot_hi(pooled, w_sq)
             mq = jnp.mean(zq, axis=0, keepdims=True)
             vq = jnp.mean(zq * zq, axis=0, keepdims=True) - mq * mq
             rq = lax.rsqrt(jnp.maximum(vq, 0.0) + EPS)
             hq = (zq - mq) * rq
-            nq = hq * vrow((sec, "g_sq"), 128) + vrow((sec, "b_sq"), 128)
+            nq = hq * rows_of(rest, AT_GSQ, 1) + rows_of(rest, AT_BSQ, 1)
             sgq = sigmoid(nq)
             qq = nq * sgq
-            logits = dot_hi(qq, w_ex[...].astype(F32)) + vrow((sec, "b_ex"), 512)
+            logits = dot_hi(qq, w_ex) + rows_of(rest, AT_BEX, 4)
             diff = logits[:, 0:256] - logits[:, 256:512]
             sh0 = sigmoid(diff)
             sh1 = sigmoid(-diff)
@@ -491,7 +934,7 @@
             return (mu, rs, lin, off), (pooled, rq, hq, nq, sgq, qq, sh0, sh1)
 
         def attention_backward(
-            ph, sec, kept_mid, kept_q, zref, rr, w_sq, w_ex, g_sq, g_ex, cols, w_mid, g_mid, da, beside
+            ph, kept_mid, kept_q, rest, rg, zref, rr, cols, mat, gw_mid, ga_mid, da, beside
         ):
             mu, rs, lin, off = kept_mid
             pooled, rq, hq, nq, sgq, qq, sh0, sh1 = kept_q
@@ -523,31 +966,34 @@
             ds1 = across(ph, 1, 0, 256)
             mean = sh0 * ds0 + sh1 * ds1
             dl = jnp.concatenate([sh0 * (ds0 - mean), sh1 * (ds1 - mean)], axis=1)
-            set_gvec((sec, "b_ex"), jnp.sum(dl, axis=0, keepdims=True))
-            dq = dot_hi(dl, w_ex[...].astype(F32), ((1,), (1,)))
+            w_sq, w_ex = small(rest)
+            set_rows(rg, AT_BEX, jnp.sum(dl, axis=0, keepdims=True))
+            dq = dot_hi(dl, w_ex, ((1,), (1,)))
             dn = dq * sgq * (1.0 + nq * (1.0 - sgq))
-            set_gvec((sec, "g_sq"), jnp.sum(dn * hq, axis=0, keepdims=True))
-            set_gvec((sec, "b_sq"), jnp.sum(dn, axis=0, keepdims=True))
-            dn = dn * vrow((sec, "g_sq"), 128)
+            set_rows(rg, AT_GSQ, jnp.sum(dn * hq, axis=0, keepdims=True))
+            set_rows(rg, AT_BSQ, jnp.sum(dn, axis=0, keepdims=True))
+            dn = dn * rows_of(rest, AT_GSQ, 1)
             dzq = rq * (
                 dn
                 - jnp.mean(dn, axis=0, keepdims=True)
                 - hq * jnp.mean(dn * hq, axis=0, keepdims=True)
             )
-            dpool = dot_hi(dzq, w_sq[...].astype(F32), ((1,), (1,))) * lanes(inv_area, 2)
+            dpool = dot_hi(dzq, w_sq, ((1,), (1,))) * lanes(inv_area, 2)
             share = jnp.where(k == 0, sh0, sh1)
 
-            def both_sums(first, second):
+            def both_sums(h, part, first, second):
                 return jnp.sum(
-                    share * across(ph, k, first, 256) + dpool * across(ph, k, second, 256),
+                    part * across(ph, h, first, 256) + dpool * across(ph, h, second, 256),
                     axis=0,
                     keepdims=True,
                 )
 
-            sdv = both_sums(2, 4)
-            sdh = both_sums(6, 8)
-            set_gvec((sec, "b_mid"), sdv)
-            set_gvec((sec, "g_mid"), sdh)
+            sums = [(both_sums(h, x, 2, 4), both_sums(h, x, 6, 8)) for h, x in enumerate((sh0, sh1))]
+            for h in range(2):
+                set_rows(rg, 2 * h, sums[h][1])
+                set_rows(rg, 4 + 2 * h, sums[h][0])
+            sdv = jnp.where(k == 0, sums[0][0], sums[1][0])
+            sdh = jnp.where(k == 0, sums[0][1], sums[1][1])
             own_share = share[0:1, :]
             own_pool = dpool[0:1, :]
             c1 = sdv / counts[256]
@@ -565,36 +1011,57 @@
             lax.fori_loop(0, 8, block2, 0)
 
             def rest():
-                g_ex[...] = dot_hi(qq, dl, ((0,), (0,))).astype(g_ex.dtype)
-                g_sq[...] = dot_hi(pooled, dzq, ((0,), (0,))).astype(g_sq.dtype)
-                g_mid[...] = dot_lt(cols[...], dz_low[...]).astype(g_mid.dtype)
+                gw_mid[...] = dot_lt(cols[...], dz_low[...]).astype(BF16).reshape(24, 48, 256)
+                shed(mat, gw_mid, ga_mid)
+                g_ex = dot_hi(qq, dl, ((0,), (0,)))
+                for j in range(4):
+                    rg[pl.ds(AT_EX + j, CSQ, stride=4), :] = g_ex[:, 128 * j : 128 * (j + 1)]
+                rg[AT_SQ : AT_SQ + CMID, :] = dot_hi(pooled, dzq, ((0,), (0,)))
 
             return rest
 
         dz_low = dz3.at[:, pl.ds(0, 256)]
 
+        arrived(MID0, w_mid0)
         conv_forward(1, cols1, w_mid0, z2)
+        pass_on(REST0, rest0)
+        pass_on(SC0, w_sc)
+        spread(OUT1, ln_out1, st_out1, w_out1)
+        spread(IN1, ln_in1, st_in1, w_in1)
+        arrived(REST0, rest0)
         receive(1, 8)
-        put(2, 8, sum_s)
-        put(2, 12, sq_s)
-        mid1, q1 = attention_forward(2, 2, totals(1, 8), 0, z2, rr1, w_sq0, w_ex0, a1, True)
-        total = totals(2, 16)
-        mus, rss = mean_rstd(total, 8, 512, counts[512])
-        lins = rss * vrow((0, "g_sc"), 512)
-        offs = vrow((0, "b_sc"), 512) - mus * lins
-
-        def wide_forward(ph, aref, w, zref):
-            z = dot(aref[...], w[...])
+
+        def short_forward():
+            pass_on(OUT1, w_out1)
+            arrived(SC0, w_sc)
+            z = dot(pool[...], w_sc[...].reshape(CIN, 512))
+            zs[...] = z
+            put(3, 8, jnp.sum(z, axis=0, keepdims=True))
+            put(3, 12, jnp.sum(z * z, axis=0, keepdims=True))
+            pass_on(IN1, w_in1)
+
+        mid1, q1 = attention_forward(2, 2, totals(1, 8), rest0, z2, rr1, a1, short_forward)
+        arrived(OUT1, w_out1)
+
+        def wide_forward(ph, rows, aref, w, zref):
+            z = dot(aref[...], w[...].reshape(CMID, 512))
             zref[...] = z
             put(ph, 0, jnp.sum(z, axis=0, keepdims=True))
             put(ph, 4, jnp.sum(z * z, axis=0, keepdims=True))
-            send(ph, 8)
-
-        wide_forward(3, a1, w_out1, z3)
-        receive(3, 8)
-        mu3, rs3 = mean_rstd(totals(3, 8), 0, 512, counts[512])
-        lin3 = rs3 * vrow((1, "g_out"), 512)
-        off3 = vrow((1, "b_out"), 512) - mu3 * lin3
+            send(ph, rows)
+
+        wide_forward(3, 16, a1, w_out1, z3)
+        spread(MID2, ln_mid2, st_mid2, w_mid2)
+        arrived(IN1, w_in1)
+        receive(3, 16)
+        total = totals(3, 16)
+        mus, rss = mean_rstd(total, 8, 512, counts[512])
+        lins = rss * vrow((0, "g_sc"))
+        offs = vrow((0, "b_sc")) - mus * lins
+
+        mu3, rs3 = mean_rstd(total, 0, 512, counts[512])
+        lin3 = rs3 * vrow((1, "g_out"))
+        off3 = vrow((1, "b_out")) - mu3 * lin3
 
         def y1_block(b, _):
             rows = pl.ds(pl.multiple_of(b * 32, 32), 32)
@@ -605,20 +1072,22 @@
             return 0
 
         lax.fori_loop(0, 8, y1_block, 0)
-        pz[0] = dot(y1[...], w_in1[1 - k])
+        pz[0] = dot(y1[...], w_in1[1 - k].reshape(512, 128))
         swap = to_twin(3, pz.at[0], pz.at[1])
         swap.start()
-        z = dot(y1[...], w_in1[k])
+        z = dot(y1[...], w_in1[k].reshape(512, 128))
         swap.wait()
         z = z + pz[1]
         z4[...] = z
         put(4, 0, jnp.sum(z, axis=0, keepdims=True))
         put(4, 1, jnp.sum(z * z, axis=0, keepdims=True))
         send(4, 8)
+        pass_on(MID2, w_mid2)
+        spread(REST2, ln_rest2, None, rest2)
         receive(4, 8)
         mu4, rs4 = mean_rstd(totals(4, 8), 0, 128, count1)
-        lin4 = rs4 * vrow((1, "g_in"), 128)
-        off4 = vrow((1, "b_in"), 128) - mu4 * lin4
+        lin4 = rs4 * vrow((1, "g_in"))
+        off4 = vrow((1, "b_in")) - mu4 * lin4
         v = z4[...] * lin4 + off4
         h = v * sigmoid(v) * mref[...]
         for dj in range(3):
@@ -626,16 +1095,27 @@
             for di in range(3):
                 store_tap(cols2, di, dj, x, 1 - di)
 
+        arrived(MID2, w_mid2)
         conv_forward(5, cols2, w_mid2, z5)
+        pass_on(REST2, rest2)
+        spread(OUT3, ln_out3, st_out3, w_out3)
+        arrived(REST2, rest2)
         receive(5, 8)
-        mid2, q2 = attention_forward(6, 4, totals(5, 8), 2, z5, rr2, w_sq2, w_ex2, a2, None)
-        wide_forward(7, a2, w_out3, z6)
+
+        def last_weights():
+            pass_on(OUT3, w_out3)
+            to_twin(14, w_in0.at[k], w_in0.at[k]).start()
+
+        mid2, q2 = attention_forward(6, 4, totals(5, 8), rest2, z5, rr2, a2, last_weights)
+        arrived(OUT3, w_out3)
+        wide_forward(7, 8, a2, w_out3, z6)
+        to_twin(14, w_in0.at[k], w_in0.at[k]).wait()
         for i in range(2):
             pltpu.make_async_copy(ctb.at[i], ctb.at[i], ct_r.at[i]).wait()
         receive(7, 8)
         mu6, rs6 = mean_rstd(totals(7, 8), 0, 512, counts[512])
-        lin6 = rs6 * vrow((3, "g_out"), 512)
-        off6 = vrow((3, "b_out"), 512) - mu6 * lin6
+        lin6 = rs6 * vrow((3, "g_out"))
+        off6 = vrow((3, "b_out")) - mu6 * lin6
 
         def out_block(b, acc):
             rows = pl.ds(pl.multiple_of(b * 32, 32), 32)
@@ -664,6 +1144,13 @@
                 oo_r.at[lax.rem(s, 2)],
                 (2 * k + j, 2 * c + s // 2),
             )
+        for mat, land, stage, whole in (
+            (MID0, ln_mid0, st_mid0, w_mid0),
+            (REST0, ln_rest0, None, rest0),
+            (SC0, ln_sc, st_sc, w_sc),
+            (OUT1, ln_out1, st_out1, w_out1),
+        ):
+            end_spread(mat, land, stage, whole)
         receive(8, 8)
 
         def wide_back(total, base, key_g, key_b, lin, mu, rs, zref, dvf, dst):
@@ -696,38 +1183,48 @@
             dz3,
         )
 
-        def attended_grad(twin, w, aref, gw):
-            pda[0] = dot_rt(dz3[...], w[...])
+        def attended_grad(twin, w, aref, mat, gw, land):
+            pda[0] = dot_rt(dz3[...], w[...].reshape(CMID, 512))
             swap = to_twin(twin, pda.at[0], pda.at[1])
             swap.start()
-            gw[...] = dot_lt(aref[...], dz3[...]).astype(gw.dtype)
+            gw[...] = dot_lt(aref[...], dz3[...]).astype(BF16).reshape(16, 16, 512)
+            shed(mat, gw, land)
             swap.wait()
 
         def summed_grad(rows):
             return (pda[0, rows, :] + pda[1, rows, :]).astype(BF16).astype(F32)
 
-        attended_grad(5, w_out3, a2, gw_out3)
-        rest2 = attention_backward(
+        attended_grad(5, w_out3, a2, OUT3, gw_out3, ga_out3)
+
+        def beside9():
+            for mat, land, stage, whole in (
+                (IN1, ln_in1, st_in1, w_in1),
+                (MID2, ln_mid2, st_mid2, w_mid2),
+                (REST2, ln_rest2, None, rest2),
+                (OUT3, ln_out3, st_out3, w_out3),
+            ):
+                end_spread(mat, land, stage, whole)
+            shed_more(OUT3, gw_out3, ga_out3, gp_out3, gb_out3)
+
+        grad_rest2 = attention_backward(
             9,
-            2,
             mid2,
             q2,
+            rest2,
+            rg2,
             z5,
             rr2,
-            w_sq2,
-            w_ex2,
-            gw_sq2,
-            gw_ex2,
             cols2,
-            w_mid2,
+            MID2,
             gw_mid2,
+            ga_mid2,
             summed_grad,
-            lambda: None,
+            beside9,
         )
 
         ep[...] = jnp.zeros(ep.shape, F32)
         for di in range(3):
-            part = dot_rt(dz_low[...], w_mid2[384 * di : 384 * (di + 1), :])
+            part = dot_rt(dz_low[...], w_mid2[8 * di : 8 * (di + 1)].reshape(384, 256))
             for dj in range(3):
                 lo = SIDE * di
                 ep[dj, lo : lo + PX, :] += part[:, 128 * dj : 128 * (dj + 1)]
@@ -743,7 +1240,9 @@
         put(10, 0, jnp.sum(dv4, axis=0, keepdims=True))
         put(10, 1, jnp.sum(dv4 * hat4, axis=0, keepdims=True))
         send(10, 8)
-        rest2()
+        grad_rest2()
+        rest_meet(2, REST2, rg2, rl2)
+        left = home(OUT3, gb_out3, gf_out3)
         receive(10, 8)
         total = totals(10, 8)
         set_gvec((1, "b_in"), total[0:1, :])
@@ -757,7 +1256,8 @@
 
         def dy_block(b, acc):
             rows = pl.ds(pl.multiple_of(b * 64, 64), 64)
-            dy = dot_rt(dz4[0, rows, :], w_in1[0]) + dot_rt(dz4[1, rows, :], w_in1[1])
+            dy = dot_rt(dz4[0, rows, :], w_in1[0].reshape(512, 128))
+            dy = dy + dot_rt(dz4[1, rows, :], w_in1[1].reshape(512, 128))
             dy = dy + dv6[rows, :].astype(BF16).astype(F32)
             v = v3[rows, :]
             sg = sigmoid(v)
@@ -775,7 +1275,10 @@
             put(11, 4 * j, jnp.sum(x, axis=0, keepdims=True))
         send(11, 16)
         both4 = jnp.concatenate([dz4[0], dz4[1]], axis=1)
-        gw_in1[...] = dot_lt(y1[...], both4).astype(gw_in1.dtype)
+        gw_in1[...] = dot_lt(y1[...], both4).astype(BF16).reshape(32, 16, 256)
+        shed(IN1, gw_in1, ga_in1)
+        shed_more(MID2, gw_mid2, ga_mid2, gp_mid2, gb_mid2)
+        left = left + rest_home(2, REST2, rg2, rl2, rf2)
         receive(11, 16)
         total = totals(11, 16)
         wide_back(
@@ -802,29 +1305,31 @@
             lambda rows: v3[rows, :].astype(BF16).astype(F32),
             dzs,
         )
-        attended_grad(7, w_out1, a1, gw_out1)
+        attended_grad(7, w_out1, a1, OUT1, gw_out1, ga_out1)
 
         def short_back():
-            part = dot_rt(dzs[...], w_sc[...])
+            part = dot_rt(dzs[...], w_sc[...].reshape(CIN, 512))
             pdp[0] = jnp.where(k == 0, part[:, 256:512], part[:, 0:256])
             to_twin(8, pdp.at[0], pdp.at[1]).start()
             pdp[2] = jnp.where(k == 0, part[:, 0:256], part[:, 256:512])
-            gw_sc[...] = dot_lt(pool[...], dzs[...]).astype(gw_sc.dtype)
-
-        rest1 = attention_backward(
+            gw_sc[...] = dot_lt(pool[...], dzs[...]).astype(BF16).reshape(32, 16, 512)
+            shed(SC0, gw_sc, ga_sc)
+            table_meet(0, 4, TABLE_ROWS - 4)
+            shed_more(IN1, gw_in1, ga_in1, gp_in1, gb_in1)
+            shed_more(OUT1, gw_out1, ga_out1, gp_out1, gb_out1)
+
+        grad_rest0 = attention_backward(
             12,
-            0,
             mid1,
             q1,
+            rest0,
+            rg0,
             z2,
             rr1,
-            w_sq0,
-            w_ex0,
-            gw_sq0,
-            gw_ex0,
             cols1,
-            w_mid0,
+            MID0,
             gw_mid0,
+            ga_mid0,
             summed_grad,
             short_back,
         )
@@ -832,7 +1337,7 @@
         for p in range(4):
             dh[p] = jnp.zeros((PX, 128), F32)
         for di in range(3):
-            part = dot_rt(dz_low[...], w_mid0[384 * di : 384 * (di + 1), :])
+            part = dot_rt(dz_low[...], w_mid0[8 * di : 8 * (di + 1)].reshape(384, 256))
             pr = 0 if di == 1 else 1
             for dj in range(3):
                 x = part[:, 128 * dj : 128 * (dj + 1)]
@@ -856,11 +1361,18 @@
         put(13, 0, jnp.sum(t0, axis=0, keepdims=True))
         put(13, 1, jnp.sum(t1, axis=0, keepdims=True))
         send(13, 8)
-        rest1()
+        grad_rest0()
+        rest_meet(1, REST0, rg0, rl0)
+        shed_more(SC0, gw_sc, ga_sc, gp_sc, gb_sc)
+        left = left + home(MID2, gb_mid2, gf_mid2)
+        left = left + home(IN1, gb_in1, gf_in1)
+        left = left + home(OUT1, gb_out1, gf_out1)
+        left = left + table_home(0, 4, TABLE_ROWS - 4)
         receive(13, 8)
         total = totals(13, 8)
         set_gvec((0, "b_in"), total[0:1, :])
         set_gvec((0, "g_in"), total[1:2, :])
+        table_meet(3, 0, 4)
         k1 = total[0:1, :] / (4.0 * count1)
         k2 = total[1:2, :] / (4.0 * count1)
 
@@ -875,13 +1387,28 @@
         total = jnp.zeros((CIN, 128), F32)
         for p in range(4):
             total = total + dot_lt(um[p], dz1[k, p])
-        gw_in0[...] = total.astype(gw_in0.dtype)
+        gw_in0[...] = total.astype(BF16).reshape(32, 16, 128)
+
+        def shed_in0(i, _):
+            p = lax.rem(8 * s + i, 32)
+            move(
+                gw_in0.at[p],
+                gb_in0.at[s * chips + c, k],
+                gb_s.at[0],
+                gb_r.at[0],
+                (p // 8, p % 8),
+            )
+            return 0
+
+        lax.fori_loop(0, 32, shed_in0, 0)
+        shed_more(MID0, gw_mid0, ga_mid0, gp_mid0, gb_mid0)
         swap.wait()
         to_twin(8, pdp.at[0], pdp.at[1]).wait()
 
         def du_block(p, _):
-            mine = pl.ds(pl.multiple_of(256 * k, 256), 256)
-            grad = dot_rt(dz1[0, p], w_in0[0, mine, :]) + dot_rt(dz1[1, p], w_in0[1, mine, :])
+            mine = pl.ds(16 * k, 16)
+            grad = dot_rt(dz1[0, p], w_in0[0, mine].reshape(256, 128))
+            grad = grad + dot_rt(dz1[1, p], w_in0[1, mine].reshape(256, 128))
             grad = (grad + 0.25 * (pdp[1] + pdp[2])) * lanes(mref[...], 2)
             low = grad.astype(BF16)
             ibuf[0, p] = low[:, 0:128]
@@ -898,6 +1425,46 @@
                 (2 * k + j, 2 * c + s // 2),
             )
 
+        left = left + home(SC0, gb_sc, gf_sc)
+        left = left + rest_home(1, REST0, rg0, rl0, rf0)
+        left = left + table_home(3, 0, 4)
+        left = left + home(IN0, gb_in0, gf_in0)
+        left = left + home(MID0, gb_mid0, gf_mid0)
+
+        for mat, gw, land in (
+            (MID0, gw_mid0, ga_mid0),
+            (SC0, gw_sc, ga_sc),
+            (OUT1, gw_out1, ga_out1),
+            (IN1, gw_in1, ga_in1),
+            (MID2, gw_mid2, ga_mid2),
+            (OUT3, gw_out3, ga_out3),
+        ):
+            end_shed(mat, gw, land)
+
+        @pl.when(holds(IN0))
+        def _():
+            full_wait(gw_in0.at[pl.ds(0, 31)], gb_s.at[0])
+            full_wait(fill.at[pl.ds(0, 8 * (4 * n - 1))], a_s.at[0])
+
+        @pl.when(jnp.logical_not(holds(IN0)))
+        def _():
+            full_wait(gw_in0, gb_s.at[0])
+
+        for i, mat, land in ((1, REST0, rl0), (2, REST2, rl2)):
+
+            @pl.when((s == mat.row) & (d < 8))
+            def _():
+                full_wait(land, v_s.at[i])
+
+        @pl.when((s == 0) & (d < 2))
+        def _():
+            full_wait(gvl.at[pl.ds(4, TABLE_ROWS - 4)], v_s.at[0])
+            full_wait(gvl.at[pl.ds(0, 4)], v_s.at[3])
+
+        fill_up(nought, fill2, left, HOME_ROWS, gc_s)
+        full_wait(fill2, gc_s)
+        full_wait(fill, h_s)
+        full_wait(out_w, gc_r)
         for slot in range(2):
             pltpu.make_async_copy(out_o.at[slot], out_o.at[slot], oo_r.at[slot]).wait()
             pltpu.make_async_copy(out_i.at[slot], out_i.at[slot], oi_r.at[slot]).wait()
@@ -916,12 +1483,16 @@
             here = u.at[q, pl.ds(2 * k, 2)]
             pltpu.make_async_copy(here, here, bs.at[10 + q]).wait()
         for ph in range(PHASES):
-            end_send(ph, 16 if ph in (2, 9, 11, 12) else 8, ph in (2, 6, 9, 12))
+            end_send(ph, 16 if ph in (3, 9, 11, 12) else 8, ph in (2, 6, 9, 12))
 
     return kernel
 
 
 def call_kernel(n, operands):
+    chips = n // 2
+    shard_rows = WSLOTS // (128 * n)
+    fill_rows = shard_rows + 20 * (4 * n - 1)
+
     def vm(*shape, dtype=F32):
         return pltpu.VMEM(shape, dtype)
 
@@ -967,10 +1538,82 @@
         vm(4, PX, 128),
         low(2, PX, 256),
         low(2, 4, PX, 128),
+        vm(shard_rows, 128),
+        vm(128, 128),
+        vm(fill_rows, 128),
+        vm(HOME_ROWS, 128),
+        vm(TABLE_ROWS, 128),
+        low(2, 32, 16, 128),
+        low(24, 48, 256),
+        vm(800, 128),
+        low(32, 16, 512),
+        low(16, 16, 512),
+        low(2, 32, 16, 128),
+        low(24, 48, 256),
+        vm(800, 128),
+        low(16, 16, 512),
+        vm(32, 128),
+        vm(192, 128),
+        vm(25, 128),
+        vm(128, 128),
+        vm(128, 128),
+        vm(64, 128),
+        vm(192, 128),
+        vm(25, 128),
+        vm(128, 128),
+        low(2, 16, 128),
+        low(2, 48, 256),
+        low(2, 16, 512),
+        low(2, 16, 512),
+        low(2, 2, 16, 128),
+        low(2, 48, 256),
+        low(2, 16, 512),
+        low(32, 16, 128),
+        low(24, 48, 256),
+        low(32, 16, 512),
+        low(16, 16, 512),
+        low(32, 16, 256),
+        low(24, 48, 256),
+        low(16, 16, 512),
+        low(3, 6, 48, 256),
+        low(3, 8, 16, 512),
+        low(3, 4, 16, 512),
+        low(3, 8, 16, 256),
+        low(3, 6, 48, 256),
+        low(3, 4, 16, 512),
+        low(6, 48, 256),
+        low(8, 16, 512),
+        low(4, 16, 512),
+        low(8, 16, 256),
+        low(6, 48, 256),
+        low(4, 16, 512),
+        low(4 * chips, 2, 16, 128),
+        low(chips, 2, 48, 256),
+        low(chips, 2, 16, 512),
+        low(chips, 2, 16, 512),
+        low(chips, 2, 16, 256),
+        low(chips, 2, 48, 256),
+        low(chips, 2, 16, 512),
+        vm(32, 128),
+        vm(192, 128),
+        vm(128, 128),
+        vm(128, 128),
+        vm(64, 128),
+        vm(192, 128),
+        vm(128, 128),
+        vm(784, 128),
+        vm(784, 128),
+        vm(REST_PART, 128),
+        vm(REST_PART, 128),
+        vm(REST_PART, 128),
+        vm(REST_PART, 128),
+        vm(64, 128),
+        vm(64, 128),
+        vm(64, 128),
         dma((PHASES,)),
         dma((PHASES, 2)),
-        dma((14,)),
-        dma((14,)),
+        dma((15,)),
+        dma((15,)),
         dma((2, 2)),
         dma((4,)),
         dma((2,)),
@@ -979,23 +1622,27 @@
         dma((2,)),
         dma((2,)),
         dma((2,)),
+        dma,
+        dma,
+        dma((9,)),
+        dma((9,)),
+        dma((9,)),
+        dma((9,)),
+        dma((9,)),
+        dma((9,)),
+        dma((9,)),
+        dma((9,)),
+        dma((9,)),
+        dma,
+        dma,
+        dma((4,)),
+        dma((4,)),
     ]
     sds = jax.ShapeDtypeStruct
     outs = (
         sds((2, PX, 256), BF16),
         sds((2, 4, PX, 128), BF16),
-        sds((CIN, 128), BF16),
-        sds((1152, 256), BF16),
-        sds((CMID, CSQ), BF16),
-        sds((CSQ, 512), BF16),
-        sds((CIN, 512), BF16),
-        sds((CMID, 512), BF16),
-        sds((512, CMID), BF16),
-        sds((1152, 256), BF16),
-        sds((CMID, CSQ), BF16),
-        sds((CSQ, 512), BF16),
-        sds((CMID, 512), BF16),
-        sds((VROWS, VCOLS), F32),
+        sds((shard_rows, 128), F32),
     )
     vmem = pl.BlockSpec(memory_space=pltpu.VMEM)
     smem = pl.BlockSpec(memory_space=pltpu.SMEM)
@@ -1006,120 +1653,28 @@
         out_specs=[vmem] * len(outs),
         scratch_shapes=scratch,
         compiler_params=pltpu.CompilerParams(
-            collective_id=0, has_side_effects=True, vmem_limit_bytes=56 << 20
+            collective_id=0, has_side_effects=True, vmem_limit_bytes=60 << 20
         ),
     )(*operands)
 
 
-def unpack(flat, layout):
-    pieces, offset = {}, 0
-    for name, shape in layout:
-        size = math.prod(shape)
-        pieces[name] = flat[offset : offset + size].reshape(shape)
-        offset += size
-    return pieces
-
-
 def per_device(images, cotangent, res_codes, section_weights):
     n = lax.axis_size("dp")
-    k = lax.axis_index("dp") % 2
-    flat = lax.all_gather(section_weights.astype(BF16), "dp", axis=1, tiled=True)
-    flat = lax.all_gather(flat, "section", axis=0, tiled=True)
-    w = [unpack(flat[i], layout) for i, layout in enumerate(layouts())]
-
-    def half(x):
-        size = x.shape[-1] // 2
-        return lax.dynamic_slice_in_dim(x, k * size, size, x.ndim - 1)
-
-    def mid(x):
-        return half(x).reshape(1152, 256)
-
-    vec = jnp.stack(
-        [
-            jnp.pad(half(w[i][name]) if cut else w[i][name], (0, VCOLS))[:VCOLS]
-            for i, name, cut in VECTORS
-        ]
-        + [jnp.zeros((VCOLS,), BF16)] * (VROWS - len(VECTORS))
-    ).astype(F32)
     planes = images.reshape(2, SIDE, 2, SIDE, 2, 128).transpose(0, 2, 4, 1, 3, 5)
-    w_in1 = lax.dynamic_slice_in_dim(w[1]["w_in"], k * 512, 512, 0)
-    operands = (
-        planes.reshape(2, 4, PX, 128),
-        cotangent.reshape(2, PX, 256),
-        res_codes,
-        w[0]["w_in"].reshape(CIN, 2, 128).transpose(1, 0, 2),
-        mid(w[0]["w_mid"]),
-        w[0]["w_sq"],
-        w[0]["w_ex"],
-        half(w[0]["w_sc"]),
-        half(w[1]["w_out"]),
-        w_in1.reshape(512, 2, 128).transpose(1, 0, 2),
-        mid(w[2]["w_mid"]),
-        w[2]["w_sq"],
-        w[2]["w_ex"],
-        half(w[3]["w_out"]),
-        vec,
+    out_o, out_i, out_w = call_kernel(
+        n,
+        (
+            planes.reshape(2, 4, PX, 128),
+            cotangent.reshape(2, PX, 256),
+            res_codes,
+            section_weights.reshape(-1, 128),
+        ),
     )
-    (
-        out_o,
-        out_i,
-        g_in0,
-        g_mid0,
-        g_sq0,
-        g_ex0,
-        g_sc,
-        g_out1,
-        g_in1,
-        g_mid2,
-        g_sq2,
-        g_ex2,
-        g_out3,
-        gvec,
-    ) = call_kernel(n, operands)
     block_out = out_o.reshape(2, SIDE, SIDE, 256)
     input_grad = (
         out_i.reshape(2, 2, 2, SIDE, SIDE, 128).transpose(0, 3, 1, 4, 2, 5).reshape(images.shape)
     )
-
-    first = (lax.axis_index("section") < 2) & (lax.axis_index("dp") < 2)
-
-    def widen(x):
-        zero = jnp.zeros_like(x)
-        return jnp.where(
-            k == 0, jnp.concatenate([x, zero], -1), jnp.concatenate([zero, x], -1)
-        )
-
-    def once(x, cut):
-        keep = first if cut else first & (k == 0)
-        return jnp.where(keep, x, jnp.zeros_like(x))
-
-    grads = [{}, {}, {}, {}]
-    for row, (i, name, cut) in enumerate(VECTORS):
-        size = math.prod(dict(layouts()[i])[name])
-        value = gvec[row, : size // 2 if cut else size]
-        grads[i][name] = once(widen(value) if cut else value, cut).astype(BF16)
-    grads[0]["w_in"] = widen(g_in0)
-    grads[0]["w_mid"] = widen(g_mid0)
-    grads[0]["w_sq"] = once(g_sq0, False)
-    grads[0]["w_ex"] = once(g_ex0, False)
-    grads[0]["w_sc"] = widen(g_sc)
-    grads[1]["w_out"] = widen(g_out1)
-    zero = jnp.zeros_like(g_in1)
-    grads[1]["w_in"] = jnp.where(
-        k == 0, jnp.concatenate([g_in1, zero], 0), jnp.concatenate([zero, g_in1], 0)
-    )
-    grads[2]["w_mid"] = widen(g_mid2)
-    grads[2]["w_sq"] = once(g_sq2, False)
-    grads[2]["w_ex"] = once(g_ex2, False)
-    grads[3]["w_out"] = widen(g_out3)
-    rows = []
-    for i, layout in enumerate(layouts()):
-        packed = jnp.concatenate([grads[i][name].reshape(-1) for name, _ in layout])
-        rows.append(jnp.pad(packed, (0, WSLOTS - packed.shape[0])))
-    packed = jnp.stack(rows)
-    packed = lax.psum_scatter(packed, "section", scatter_dimension=0, tiled=True)
-    packed = lax.psum_scatter(packed, "dp", scatter_dimension=1, tiled=True)
-    return block_out, input_grad, packed.astype(F32)
+    return block_out, input_grad, out_w.reshape(section_weights.shape)
 
 
 def solution(mesh):

time: 979 us -> 180 us (0.18); the launches traced: 964 us -> 180 us
  waiting for transfers between devices: 583 us -> 0 us
  local copies, waits for them, and re-layouts: 220 us -> 5.91 us
  Pallas kernels: 104 us -> 174 us
  other arithmetic: 41.9 us -> 0 us
  between operations: 15.5 us -> 0.66 us
    unnamed x6 -> x0, waiting for transfers between devices: 326 us -> none
    all_gather x2 -> x0, waiting for transfers between devices: 257 us -> none  [the longest x1 199 us: per_device(): flat = lax.all_gather(flat, 'section', axis=0, tiled=True)]
    unnamed x85 -> x6, local copies, waits for them, and re-layouts: 97.9 us -> 1.55 us
    pallas_call x1, Pallas kernels: 104 us -> 174 us  [call_kernel(): pl.pallas_call(make_kernel(n), out_shape=outs, in_specs=[smem if i == 2 e...]
    slice x22 -> x0, local copies, waits for them, and re-layouts: 65.7 us -> none  [the longest x10 62.6 us: unpack(): pieces[name] = flat[offset:offset + size].reshape(shape)]
    another operation x1 -> x0, other arithmetic: 28.2 us -> none  [per_device(): packed = jnp.stack(rows)]
    another operation x19 -> x0, local copies, waits for them, and re-layouts: 19.1 us -> none  [the longest x4 16.9 us: per_device(): packed = jnp.stack(rows)]
    reshape x9 -> x0, local copies, waits for them, and re-layouts: 13.1 us -> none  [the longest x8 11.3 us: unpack(): pieces[name] = flat[offset:offset + size].reshape(shape)]
  transfers between devices with their start and end apart: 4 -> 0, of which waited for: 4 -> 0; matrix products, arithmetic and copies ran while one was open for 0% -> 0% of each run, Pallas kernels for 0% -> 0%
where the time goes in v1:
time: 180 us
  Pallas kernels  174 us (97%)
  local copies, waits for them, and re-layouts  5.91 us (3%)
    pallas_call x1, Pallas kernels, call_kernel(): pl.pallas_call(make_kernel(n), out_shape=outs, in_specs=[smem if i == 2 e...  174 us

profile of v1, /device:TPU:9, one launch (start us, length us, event | category | flops | bytes accessed | tf_op | source)
XLA Modules:
  0.0 180.1 jit_solution(3835459657026349518)
XLA Ops:
  0.6 1.9 %copy.7 = bf16[2,16,2,16,2,128]{5,3,1,4,2,0:T(8,128)(2,1)} copy(bf16[2,16,2,16,2,128]{5,4,3,2,1,0:T(2,128)(2,1)} %bitcast.15) | data formatting | bytes 1048576 | tf_op jit(solution)/shard_map/reshape | solution.py:1663
  2.5 173.5 %shard_map.67 = (bf16[2,256,256]{2,1,0:T(8,128)(2,1)}, bf16[2,4,256,128]{3,2,1,0:T(8,128)(2,1)}, f32[1320,128]{1,0:T(8,128)}) custom-call(bf16[2,4,256,128]{3,2,1,0:T(8,128)(2,1)} %bitcast.12, bf16[2,256,256]{2,1,0:T(8,128)(2,1)} %bitcast.19, s32[2]{0:T(128)} %codes.1, f32[1320,128]{1,0:T(8,128)} %bitcast.13), custom_call_target="tpu_custom_call" | custom-call | tf_op jit(solution)/shard_map/pallas_call | solution.py:1649
  176.1 0.0 copy-start.1
  176.1 0.0 copy-start
  176.1 2.5 %copy.8 = bf16[2,16,2,16,2,128]{5,4,3,2,1,0:T(2,128)(2,1)} copy(bf16[2,16,2,16,2,128]{5,3,1,4,2,0:T(8,128)(2,1)} %bitcast.17) | data formatting | bytes 1048576 | tf_op jit(solution)/shard_map/transpose | solution.py:1675
  178.5 0.0 copy-done.1
  178.5 0.7 copy.11
  179.2 0.0 copy-done
  179.2 0.8 copy.12
Async XLA Ops:
  176.1 2.5 %copy-start.1 = (bf16[2,256,256]{2,1,0:T(8,128)(2,1)S(1)}, bf16[2,256,256]{2,1,0:T(8,128)(2,1)}, u32[]{:S(2)}) copy-start(bf16[2,256,256]{2,1,0:T(8,128)(2,1)} %get-tuple-element.6) | copy-start | bytes 786436
  176.1 3.2 %copy-start = (f32[1320,128]{1,0:T(8,128)S(1)}, f32[1320,128]{1,0:T(8,128)}, u32[]{:S(2)}) copy-start(f32[1320,128]{1,0:T(8,128)} %get-tuple-element.8) | copy-start | bytes 2027524

commit v2 on v1

--- a/solution.py
+++ b/solution.py
@@ -22,7 +22,7 @@
 
 
 class Matrix:
-    def __init__(self, index, row, start, blocks, pieces, rows, first=0, split="columns"):
+    def __init__(self, index, row, start, blocks, pieces, rows, first, step, split="columns"):
         self.index = index
         self.row = row
         self.start = start
@@ -30,20 +30,21 @@
         self.pieces = pieces
         self.rows = rows
         self.first = first
+        self.step = step
         self.split = split
         self.flat = blocks * rows
         self.width = 128 * (blocks // 2 if split == "columns" else blocks)
 
 
-IN0 = Matrix(0, 0, 0, 2, 8, 16)
-MID0 = Matrix(1, 0, 1028, 4, 6, 48)
-REST0 = Matrix(2, 0, 5636, 1, 8, 25, split="none")
-SC0 = Matrix(3, 0, 6418, 8, 8, 16)
-OUT1 = Matrix(4, 1, 0, 8, 4, 16, first=4)
-IN1 = Matrix(5, 1, 2064, 2, 8, 16, split="rows")
-MID2 = Matrix(6, 2, 0, 4, 6, 48)
-REST2 = Matrix(7, 2, 4608, 1, 8, 25, split="none")
-OUT3 = Matrix(8, 3, 0, 8, 4, 16)
+IN0 = Matrix(0, 0, 0, 2, 8, 16, 0, 1)
+MID0 = Matrix(1, 0, 1028, 4, 6, 48, 0, 1)
+REST0 = Matrix(2, 0, 5636, 1, 8, 25, 0, 1, split="none")
+SC0 = Matrix(3, 0, 6418, 8, 8, 16, 0, 1)
+OUT1 = Matrix(4, 1, 0, 8, 4, 16, 1, 2)
+IN1 = Matrix(5, 1, 2064, 2, 8, 16, 0, 1, split="rows")
+MID2 = Matrix(6, 2, 0, 4, 6, 48, 2, 1)
+REST2 = Matrix(7, 2, 4608, 1, 8, 25, 0, 1, split="none")
+OUT3 = Matrix(8, 3, 0, 8, 4, 16, 0, 2)
 MATRICES = (IN0, MID0, REST0, SC0, OUT1, IN1, MID2, REST2, OUT3)
 PRODUCTS = (IN0, MID0, SC0, OUT1, IN1, MID2, OUT3)
 USED = (10530, 4116, 5390, 2064)
@@ -56,15 +57,25 @@
     (0, "b_in"): (2, 1026, 1),
     (0, "g_sc"): (4, 10514, 4),
     (0, "b_sc"): (12, 10522, 4),
-    (1, "g_out"): (20, 2048, 4),
-    (1, "b_out"): (28, 2056, 4),
-    (1, "g_in"): (36, 4112, 1),
-    (1, "b_in"): (38, 4114, 1),
-    (3, "g_out"): (40, 2048, 4),
-    (3, "b_out"): (48, 2056, 4),
+    (1, "g_out"): (28, 2048, 4),
+    (1, "b_out"): (36, 2056, 4),
+    (1, "g_in"): (44, 4112, 1),
+    (1, "b_in"): (46, 4114, 1),
+    (3, "g_out"): (48, 2048, 4),
+    (3, "b_out"): (56, 2056, 4),
 }
-TABLE_ROWS = 56
-RANGES = ((0, 1024, 4, 0), (0, 10514, 16, 4), (1, 2048, 16, 20), (1, 4112, 4, 36), (3, 2048, 16, 40))
+TABLE_ROWS = 72
+SECTION_ROWS = {0: (0, 28), 1: (28, 20), 2: (64, 8), 3: (48, 16)}
+AT_MID = {0: 20, 2: 64}
+RANGES = (
+    (0, 1024, 4, 0),
+    (0, 5636, 8, 20),
+    (0, 10514, 16, 4),
+    (1, 2048, 16, 28),
+    (1, 4112, 4, 44),
+    (2, 4608, 8, 64),
+    (3, 2048, 16, 48),
+)
 
 
 def dot(a, b):
@@ -98,7 +109,7 @@
 def make_kernel(n):
     chips = n // 2
     shard_rows = WSLOTS // (128 * n)
-    fill_rows = shard_rows + 20 * (4 * n - 1)
+    fill_rows = max(shard_rows + 28 * n, 96 * (n - 1), 100 * n, 8 * (4 * n - 1), 16 * (2 * n - 1))
 
     def kernel(
         img,
@@ -175,6 +186,12 @@
         st_in1,
         st_mid2,
         st_out3,
+        cu_in0,
+        cu_mid0,
+        cu_sc,
+        cu_out1,
+        cu_mid2,
+        cu_out3,
         gw_in0,
         gw_mid0,
         gw_sc,
@@ -230,6 +247,7 @@
         oi_s,
         oi_r,
         h_s,
+        t_s,
         t_r,
         h_r,
         a_s,
@@ -261,6 +279,8 @@
 
         barrier = pltpu.get_barrier_semaphore()
         me = s * n + d
+        beside_x = s + 1 - 2 * (s % 2)
+        beside_y = lax.rem(s + 2, 4)
 
         def greet(i, _):
             e = lax.rem(me + i, 4 * n)
@@ -315,7 +335,7 @@
 
                 lax.fori_loop(0, many, one, 0)
 
-            if full > 4:
+            if full > 1:
 
                 @pl.when(count == full)
                 def _():
@@ -356,7 +376,76 @@
         mine_from = d * shard_rows
         mine_to = mine_from + shard_rows
 
-        def scatter_pieces(mat, land):
+        def cut(mat, land, stage, base):
+            for j in range(mat.blocks):
+                for h in range(2):
+                    if mat.split == "rows":
+                        x = land[pl.ds(base + h * mat.flat + j, mat.rows, stride=mat.blocks), :]
+                        stage[h, j] = x.astype(BF16)
+                    elif j // (mat.blocks // 2) == h:
+                        x = land[pl.ds(base + j, mat.rows, stride=mat.blocks), :]
+                        at = 128 * (j % (mat.blocks // 2))
+                        stage[h, :, at : at + 128] = x.astype(BF16)
+
+        def holds(mat):
+            i = d - mat.first
+            inside = (i >= 0) & (i < mat.step * mat.pieces)
+            return inside & (i % mat.step == 0) if mat.step > 1 else inside
+
+        def piece(mat):
+            return s * mat.pieces + jnp.maximum(d - mat.first, 0) // mat.step
+
+        def scatter_cut(mat, land, stage, ready, part=0, parts=1):
+            first = jnp.maximum(mine_from - mat.start, 0) // mat.flat
+            last = (jnp.maximum(mine_to - mat.start, 0) + mat.flat - 1) // mat.flat
+            last = jnp.minimum(last, 4 * mat.pieces)
+
+            def one(p, sent):
+                start = mat.start + p * mat.flat
+                lo = jnp.maximum(start, mine_from)
+                count = jnp.minimum(start + mat.flat, mine_to) - lo
+                dev = (p // mat.pieces, mat.first + mat.step * (p % mat.pieces))
+
+                def in_one():
+                    to = ready.at[p - first]
+                    cut(mat, sround, to, lo - mine_from)
+                    move(to, stage, h_s, h_r.at[mat.index], dev)
+                    return jnp.where(is_self(dev), 0, mat.flat // 2)
+
+                def in_rows():
+                    return move_rows(
+                        sround,
+                        lo - mine_from,
+                        land,
+                        lo - start,
+                        count,
+                        mat.flat,
+                        h_s,
+                        h_r.at[mat.index],
+                        dev,
+                    )
+
+                return sent + lax.cond(count == mat.flat, in_one, in_rows)
+
+            step = (jnp.maximum(last - first, 0) + parts - 1) // parts
+            begin = first + part * step
+            end = jnp.minimum(last, begin + step)
+            return lax.fori_loop(begin, end, one, jnp.int32(0))
+
+        def stage_ready(mat, land, stage):
+            start = mat.start + piece(mat) * mat.flat
+            whole = start // shard_rows == (start + mat.flat - 1) // shard_rows
+
+            @pl.when(whole)
+            def _():
+                full_wait(stage, h_r.at[mat.index])
+
+            @pl.when(jnp.logical_not(whole))
+            def _():
+                full_wait(land, h_r.at[mat.index])
+                cut(mat, land, stage, 0)
+
+        def scatter_pieces(mat, land, part=0, parts=1):
             total = mat.pieces * 4 * (2 if mat.split == "rows" else 1)
             first = jnp.maximum(mine_from - mat.start, 0) // mat.flat
             last = (jnp.maximum(mine_to - mat.start, 0) + mat.flat - 1) // mat.flat
@@ -367,7 +456,7 @@
                 count = jnp.minimum(start + mat.flat, mine_to) - lo
                 h = p // (4 * mat.pieces)
                 q = p % (4 * mat.pieces)
-                dev = (q // mat.pieces, mat.first + q % mat.pieces)
+                dev = (q // mat.pieces, mat.first + mat.step * (q % mat.pieces))
                 return sent + move_rows(
                     sround,
                     lo - mine_from,
@@ -380,14 +469,18 @@
                     dev,
                 )
 
-            return lax.fori_loop(first, jnp.minimum(last, total), one, jnp.int32(0))
+            last = jnp.minimum(last, total)
+            step = (jnp.maximum(last - first, 0) + parts - 1) // parts
+            begin = first + part * step
+            end = jnp.minimum(last, begin + step)
+            return lax.fori_loop(begin, end, one, jnp.int32(0))
 
         def scatter_table(start, rows, at):
             lo = jnp.maximum(start, mine_from)
             count = jnp.maximum(jnp.minimum(start + rows, mine_to) - lo, 0)
 
             def one(i, sent):
-                e = lax.rem(me + i, 4 * n)
+                e = lax.rem(d + i, n)
                 return sent + move_rows(
                     sround,
                     lo - mine_from,
@@ -396,16 +489,51 @@
                     count,
                     rows,
                     h_s,
-                    t_r,
-                    (e // n, e % n),
+                    t_r.at[0],
+                    (s, e),
                 )
 
-            return lax.fori_loop(0, jnp.where(count > 0, 4 * n, 0), one, jnp.int32(0))
+            return lax.fori_loop(0, jnp.where(count > 0, n, 0), one, jnp.int32(0))
+
+        def pass_table():
+            for r, (at, many) in SECTION_ROWS.items():
+
+                @pl.when(s == r)
+                def _():
+                    here = table.at[pl.ds(at, many)]
+                    full_wait(here, t_r.at[0])
+                    for i in range(1, 4):
+                        pltpu.make_async_remote_copy(
+                            here,
+                            here,
+                            t_s,
+                            t_r.at[1],
+                            device_id=(lax.rem(s + i, 4), d),
+                            device_id_type=MESH,
+                        ).start()
+
+        def table_arrived():
+            for r in range(4):
+                rest = TABLE_ROWS - SECTION_ROWS.get(r, (0, 0))[1]
+
+                @pl.when(s == r)
+                def _():
+                    full_wait(table.at[pl.ds(0, rest)], t_r.at[1])
+
+        def end_table():
+            for r, (_, many) in SECTION_ROWS.items():
+
+                @pl.when(s == r)
+                def _():
+                    full_wait(fill.at[pl.ds(0, 3 * many)], t_s)
+
+        def full_wait(ref, sem):
+            pltpu.make_async_copy(ref, ref, sem).wait()
 
         def when_row(r, body):
             return lax.cond(s == r, body, lambda: jnp.int32(0))
 
-        sent = when_row(0, lambda: scatter_pieces(IN0, ln_in0))
+        sent = when_row(0, lambda: scatter_cut(IN0, ln_in0, st_in0, cu_in0))
 
         for slot in range(2):
             for kk in range(2):
@@ -417,14 +545,6 @@
                     (2 * k + slot, 2 * c + kk),
                 )
         for slot in range(2):
-            move(
-                cot.at[slot],
-                ctb.at[lax.rem(s, 2)],
-                ct_s.at[slot],
-                ct_r.at[lax.rem(s, 2)],
-                (2 * k + slot, 2 * c + s // 2),
-            )
-        for slot in range(2):
             width = (SIDE - 2 * codes[slot]).astype(F32)
             side_t[k, slot] = jnp.full((8, 128), width, F32)
         side_copy = to_twin(0, side_t.at[k], side_t.at[k])
@@ -432,96 +552,142 @@
         snd[...] = jnp.zeros(snd.shape, F32)
 
         def row0():
-            count = scatter_table(*RANGES[0][1:]) + scatter_pieces(MID0, ln_mid0)
-            count = count + scatter_pieces(REST0, ln_rest0) + scatter_pieces(SC0, ln_sc)
-            return count + scatter_table(*RANGES[1][1:])
+            count = scatter_cut(MID0, ln_mid0, st_mid0, cu_mid0) + scatter_table(*RANGES[0][1:])
+            count = count + scatter_table(*RANGES[1][1:]) + scatter_table(*RANGES[2][1:])
+            return count + scatter_cut(SC0, ln_sc, st_sc, cu_sc)
 
         def row1():
-            count = scatter_pieces(OUT1, ln_out1) + scatter_table(*RANGES[2][1:])
-            return count + scatter_pieces(IN1, ln_in1) + scatter_table(*RANGES[3][1:])
+            count = scatter_cut(OUT1, ln_out1, st_out1, cu_out1) + scatter_table(*RANGES[3][1:])
+            return count + scatter_table(*RANGES[4][1:])
 
         sent = sent + when_row(0, row0)
         sent = sent + when_row(1, row1)
-        sent = sent + when_row(2, lambda: scatter_pieces(MID2, ln_mid2) + scatter_pieces(REST2, ln_rest2))
-        sent = sent + when_row(3, lambda: scatter_pieces(OUT3, ln_out3) + scatter_table(*RANGES[4][1:]))
-
-        fill_up(nought, fill, sent, fill_rows, h_s)
-
-        def holds(mat):
-            return (d >= mat.first) & (d < mat.first + mat.pieces)
-
-        def full_wait(ref, sem):
-            pltpu.make_async_copy(ref, ref, sem).wait()
-
-        def cut(mat, land, stage):
-            for j in range(mat.blocks):
-                for h in range(2):
-                    if mat.split == "rows":
-                        x = land[pl.ds(h * mat.flat + j, mat.rows, stride=mat.blocks), :]
-                        stage[h, j] = x.astype(BF16)
-                    elif j // (mat.blocks // 2) == h:
-                        x = land[pl.ds(j, mat.rows, stride=mat.blocks), :]
-                        at = 128 * (j % (mat.blocks // 2))
-                        stage[h, :, at : at + 128] = x.astype(BF16)
+        sent = sent + when_row(2, lambda: scatter_table(*RANGES[5][1:]))
+        sent = sent + when_row(3, lambda: scatter_table(*RANGES[6][1:]))
+
+        def scatter_some(sent, part, parts):
+            sent = sent + when_row(2, lambda: scatter_cut(MID2, ln_mid2, st_mid2, cu_mid2, part, parts))
+            return sent + when_row(3, lambda: scatter_cut(OUT3, ln_out3, st_out3, cu_out3, part, parts))
+
+        def scatter_early(sent):
+            sent = sent + when_row(0, lambda: scatter_pieces(REST0, ln_rest0))
+            sent = sent + when_row(1, lambda: scatter_pieces(IN1, ln_in1))
+            return scatter_some(sent, 1, 3)
+
+        def scatter_late(sent):
+            sent = scatter_some(sent, 2, 3)
+            sent = sent + when_row(2, lambda: scatter_pieces(REST2, ln_rest2))
+            fill_up(nought, fill, sent, fill_rows, h_s)
+
+        sent = scatter_some(sent, 0, 3)
 
         def spread(mat, land, stage, whole):
             @pl.when(holds(mat))
             def _():
-                full_wait(land, h_r.at[mat.index])
-                if mat.split != "none":
-                    cut(mat, land, stage)
-                p = s * mat.pieces + d - mat.first
+                if mat.split == "rows":
+                    full_wait(land, h_r.at[mat.index])
+                    cut(mat, land, stage, 0)
+                else:
+                    stage_ready(mat, land, stage)
+                p = piece(mat)
 
                 def one(i, _):
                     e = lax.rem(d + i, n)
                     h = e % 2
-                    if mat.split == "none":
-                        src, dst = land, whole.at[pl.ds(p * mat.flat, mat.flat)]
-                    elif mat.split == "rows":
-                        src, dst = stage.at[h], whole.at[:, p]
-                    else:
-                        src, dst = stage.at[h], whole.at[p]
-                    move(src, dst, a_s.at[mat.index], c_r.at[mat.index], (s, e))
+                    dst = whole.at[:, p] if mat.split == "rows" else whole.at[p]
+                    move(stage.at[h], dst, a_s.at[mat.index], c_r.at[mat.index], (s, e))
                     return 0
 
                 lax.fori_loop(0, n, one, 0)
 
-        def quarters(mat, whole, first, many):
-            if mat.split == "none":
-                size = mat.flat * mat.pieces
-                return whole.at[pl.ds(first * size, many * size)]
-            if mat.split == "rows":
-                return whole.at[:, pl.ds(first * mat.pieces, many * mat.pieces)]
-            return whole.at[pl.ds(first * mat.pieces, many * mat.pieces)]
+        def quarters(mat, whole, first, many, part=None):
+            if part is None:
+                span = pl.ds(first * mat.pieces, many * mat.pieces)
+            else:
+                half = mat.pieces // 2
+                span = pl.ds(first * mat.pieces + part * half, half)
+            return whole.at[:, span] if mat.split == "rows" else whole.at[span]
+
+        def hand(mat, here, i, to):
+            pltpu.make_async_remote_copy(
+                here,
+                here,
+                f_s.at[mat.index],
+                q_r.at[mat.index, i],
+                device_id=(to, d),
+                device_id_type=MESH,
+            ).start()
 
         def pass_on(mat, whole):
             here = quarters(mat, whole, s, 1)
             full_wait(here, c_r.at[mat.index])
-            for i in range(1, 4):
-                pltpu.make_async_remote_copy(
-                    here,
-                    here,
-                    f_s.at[mat.index],
-                    q_r.at[mat.index],
-                    device_id=(lax.rem(s + i, 4), d),
-                    device_id_type=MESH,
-                ).start()
+            hand(mat, here, 0, beside_x)
+            hand(mat, here, 1, beside_y)
+
+        def pass_far(mat, whole):
+            full_wait(quarters(mat, whole, beside_x, 1), q_r.at[mat.index, 0])
+            hand(mat, quarters(mat, whole, beside_x, 1, 0), 2, beside_y)
+            full_wait(quarters(mat, whole, beside_y, 1), q_r.at[mat.index, 1])
+            hand(mat, quarters(mat, whole, beside_y, 1, 1), 3, beside_x)
 
         def arrived(mat, whole):
-            full_wait(quarters(mat, whole, 0, 3), q_r.at[mat.index])
-
-        def end_spread(mat, land, stage, whole):
+            far = 3 - s
+            for i in range(2):
+                full_wait(quarters(mat, whole, far, 1, i), q_r.at[mat.index, 2 + i])
+
+        def end_spread(mat, whole):
             @pl.when(holds(mat))
             def _():
-                rows = mat.flat if mat.split == "none" else mat.rows * mat.width // 256
+                rows = mat.rows * mat.width // 256
                 full_wait(fill.at[pl.ds(0, (n - 1) * rows)], a_s.at[mat.index])
 
             full_wait(quarters(mat, whole, 0, 3), f_s.at[mat.index])
+
+        def spread_rest(mat, land, whole):
+            @pl.when(holds(mat))
+            def _():
+                full_wait(land, h_r.at[mat.index])
+                at = piece(mat) * mat.flat
+
+                def one(i, _):
+                    e = lax.rem(s * chips + c + i, 4 * chips)
+                    move(
+                        land,
+                        whole.at[pl.ds(at, mat.flat)],
+                        a_s.at[mat.index],
+                        c_r.at[mat.index],
+                        (e // chips, 2 * (e % chips)),
+                    )
+                    return 0
+
+                lax.fori_loop(0, 4 * chips, one, 0)
+
+        def share_rest(mat, whole, i):
+            @pl.when(k == 0)
+            def _():
+                full_wait(whole, c_r.at[mat.index])
+                to_twin(i, whole, whole).start()
+
+        def rest_arrived(whole, i):
+            @pl.when(k == 1)
+            def _():
+                to_twin(i, whole, whole).wait_recv()
+
+        def end_rest(mat, whole, i):
+            @pl.when(k == 0)
+            def _():
+                to_twin(i, whole, whole).wait_send()
+
+            for kk in range(2):
+
+                @pl.when(holds(mat) & (k == kk))
+                def _():
+                    rows = (4 * chips - 1 + kk) * mat.flat
+                    full_wait(fill.at[pl.ds(0, rows)], a_s.at[mat.index])
 
         @pl.when(holds(IN0))
         def _():
-            full_wait(ln_in0, h_r.at[0])
-            cut(IN0, ln_in0, st_in0)
+            stage_ready(IN0, ln_in0, st_in0)
 
             def one(i, _):
                 e = lax.rem(me + i, 4 * n)
@@ -537,8 +703,6 @@
 
             lax.fori_loop(0, 4 * n, one, 0)
 
-        spread(MID0, ln_mid0, st_mid0, w_mid0)
-
         def shed(mat, gw, land):
             for i in range(1, 4):
                 to = lax.rem(s + i, 4)
@@ -564,7 +728,7 @@
                     land2.at[c, k],
                     gb_s.at[mat.index],
                     gb_r.at[mat.index],
-                    (s, mat.first + i),
+                    (s, mat.first + mat.step * i),
                 )
                 return 0
 
@@ -608,7 +772,7 @@
                             at = h * (mat.blocks // 2) + j
                         flat[pl.ds(at, mat.rows, stride=mat.blocks), :] = x[:, 128 * j : 128 * (j + 1)]
 
-            p = s * mat.pieces + d - mat.first
+            p = piece(mat)
             left = home_rows(
                 flat, 0, mat.start + p * mat.flat, mat.flat, USED[mat.row], mat.row, holds(mat)
             )
@@ -796,6 +960,7 @@
                 device_id=(s, 2 * c + 1 - k),
                 device_id_type=MESH,
             ).start()
+        spread(MID0, ln_mid0, st_mid0, w_mid0)
         for q in range(4):
             here = u.at[q, pl.ds(2 * (1 - k), 2)]
             pltpu.make_async_copy(here, here, br.at[10 + q]).wait()
@@ -814,6 +979,8 @@
             return 0
 
         lax.fori_loop(0, 8, mask_block, 0)
+        pass_table()
+        pass_on(MID0, w_mid0)
         full_wait(w_in0.at[k], c_r.at[0])
 
         def z1_block(p, carry):
@@ -827,10 +994,11 @@
         put(0, 1, jnp.sum(t1, axis=0, keepdims=True))
         put(0, 2, side_row)
         send(0, 8)
-        pass_on(MID0, w_mid0)
-        spread(REST0, ln_rest0, None, rest0)
+        sent = scatter_early(sent)
+        pass_far(MID0, w_mid0)
         spread(SC0, ln_sc, st_sc, w_sc)
-        full_wait(table, t_r)
+        spread(OUT1, ln_out1, st_out1, w_out1)
+        table_arrived()
         receive(0, 8)
         total = totals(0, 8)
         sides = across(0, k, 2, 128)
@@ -887,10 +1055,10 @@
             )
             return w_sq, w_ex
 
-        def attention_forward(ph, twin, total, rest, zref, rr, aref, beside):
+        def attention_forward(ph, twin, total, at, rest, zref, rr, aref, beside):
             mu, rs = mean_rstd(total, 0, 256, counts[256])
-            lin = rs * rows_of(rest, 2 * k, 2)
-            off = rows_of(rest, 4 + 2 * k, 2) - mu * lin
+            lin = rs * rows_of(table, at + 2 * k, 2)
+            off = rows_of(table, at + 4 + 2 * k, 2) - mu * lin
 
             def block(b, acc):
                 rows = pl.ds(pl.multiple_of(b * 64, 64), 64)
@@ -1024,23 +1192,27 @@
 
         arrived(MID0, w_mid0)
         conv_forward(1, cols1, w_mid0, z2)
-        pass_on(REST0, rest0)
+        spread_rest(REST0, ln_rest0, rest0)
+        scatter_late(sent)
         pass_on(SC0, w_sc)
-        spread(OUT1, ln_out1, st_out1, w_out1)
+        pass_on(OUT1, w_out1)
         spread(IN1, ln_in1, st_in1, w_in1)
-        arrived(REST0, rest0)
         receive(1, 8)
 
         def short_forward():
-            pass_on(OUT1, w_out1)
+            share_rest(REST0, rest0, 15)
+            pass_far(SC0, w_sc)
+            pass_far(OUT1, w_out1)
+            pass_on(IN1, w_in1)
+            spread(MID2, ln_mid2, st_mid2, w_mid2)
             arrived(SC0, w_sc)
             z = dot(pool[...], w_sc[...].reshape(CIN, 512))
             zs[...] = z
             put(3, 8, jnp.sum(z, axis=0, keepdims=True))
             put(3, 12, jnp.sum(z * z, axis=0, keepdims=True))
-            pass_on(IN1, w_in1)
-
-        mid1, q1 = attention_forward(2, 2, totals(1, 8), rest0, z2, rr1, a1, short_forward)
+            rest_arrived(rest0, 15)
+
+        mid1, q1 = attention_forward(2, 2, totals(1, 8), AT_MID[0], rest0, z2, rr1, a1, short_forward)
         arrived(OUT1, w_out1)
 
         def wide_forward(ph, rows, aref, w, zref):
@@ -1051,8 +1223,8 @@
             send(ph, rows)
 
         wide_forward(3, 16, a1, w_out1, z3)
-        spread(MID2, ln_mid2, st_mid2, w_mid2)
-        arrived(IN1, w_in1)
+        pass_far(IN1, w_in1)
+        pass_on(MID2, w_mid2)
         receive(3, 16)
         total = totals(3, 16)
         mus, rss = mean_rstd(total, 8, 512, counts[512])
@@ -1072,6 +1244,7 @@
             return 0
 
         lax.fori_loop(0, 8, y1_block, 0)
+        arrived(IN1, w_in1)
         pz[0] = dot(y1[...], w_in1[1 - k].reshape(512, 128))
         swap = to_twin(3, pz.at[0], pz.at[1])
         swap.start()
@@ -1082,8 +1255,9 @@
         put(4, 0, jnp.sum(z, axis=0, keepdims=True))
         put(4, 1, jnp.sum(z * z, axis=0, keepdims=True))
         send(4, 8)
-        pass_on(MID2, w_mid2)
-        spread(REST2, ln_rest2, None, rest2)
+        pass_far(MID2, w_mid2)
+        spread_rest(REST2, ln_rest2, rest2)
+        spread(OUT3, ln_out3, st_out3, w_out3)
         receive(4, 8)
         mu4, rs4 = mean_rstd(totals(4, 8), 0, 128, count1)
         lin4 = rs4 * vrow((1, "g_in"))
@@ -1097,16 +1271,24 @@
 
         arrived(MID2, w_mid2)
         conv_forward(5, cols2, w_mid2, z5)
-        pass_on(REST2, rest2)
-        spread(OUT3, ln_out3, st_out3, w_out3)
-        arrived(REST2, rest2)
+        share_rest(REST2, rest2, 16)
+        pass_on(OUT3, w_out3)
         receive(5, 8)
 
         def last_weights():
-            pass_on(OUT3, w_out3)
+            pass_far(OUT3, w_out3)
+            rest_arrived(rest2, 16)
+            for slot in range(2):
+                move(
+                    cot.at[slot],
+                    ctb.at[lax.rem(s, 2)],
+                    ct_s.at[slot],
+                    ct_r.at[lax.rem(s, 2)],
+                    (2 * k + slot, 2 * c + s // 2),
+                )
             to_twin(14, w_in0.at[k], w_in0.at[k]).start()
 
-        mid2, q2 = attention_forward(6, 4, totals(5, 8), rest2, z5, rr2, a2, last_weights)
+        mid2, q2 = attention_forward(6, 4, totals(5, 8), AT_MID[2], rest2, z5, rr2, a2, last_weights)
         arrived(OUT3, w_out3)
         wide_forward(7, 8, a2, w_out3, z6)
         to_twin(14, w_in0.at[k], w_in0.at[k]).wait()
@@ -1144,13 +1326,10 @@
                 oo_r.at[lax.rem(s, 2)],
                 (2 * k + j, 2 * c + s // 2),
             )
-        for mat, land, stage, whole in (
-            (MID0, ln_mid0, st_mid0, w_mid0),
-            (REST0, ln_rest0, None, rest0),
-            (SC0, ln_sc, st_sc, w_sc),
-            (OUT1, ln_out1, st_out1, w_out1),
-        ):
-            end_spread(mat, land, stage, whole)
+        for mat, whole in ((MID0, w_mid0), (SC0, w_sc), (OUT1, w_out1)):
+            end_spread(mat, whole)
+        end_rest(REST0, rest0, 15)
+        end_table()
         receive(8, 8)
 
         def wide_back(total, base, key_g, key_b, lin, mu, rs, zref, dvf, dst):
@@ -1197,13 +1376,9 @@
         attended_grad(5, w_out3, a2, OUT3, gw_out3, ga_out3)
 
         def beside9():
-            for mat, land, stage, whole in (
-                (IN1, ln_in1, st_in1, w_in1),
-                (MID2, ln_mid2, st_mid2, w_mid2),
-                (REST2, ln_rest2, None, rest2),
-                (OUT3, ln_out3, st_out3, w_out3),
-            ):
-                end_spread(mat, land, stage, whole)
+            for mat, whole in ((IN1, w_in1), (MID2, w_mid2), (OUT3, w_out3)):
+                end_spread(mat, whole)
+            end_rest(REST2, rest2, 16)
             shed_more(OUT3, gw_out3, ga_out3, gp_out3, gb_out3)
 
         grad_rest2 = attention_backward(
@@ -1491,7 +1666,7 @@
 def call_kernel(n, operands):
     chips = n // 2
     shard_rows = WSLOTS // (128 * n)
-    fill_rows = shard_rows + 20 * (4 * n - 1)
+    fill_rows = max(shard_rows + 28 * n, 96 * (n - 1), 100 * n, 8 * (4 * n - 1), 16 * (2 * n - 1))
 
     def vm(*shape, dtype=F32):
         return pltpu.VMEM(shape, dtype)
@@ -1568,6 +1743,12 @@
         low(2, 2, 16, 128),
         low(2, 48, 256),
         low(2, 16, 512),
+        low(shard_rows // 32 + 2, 2, 16, 128),
+        low(shard_rows // 192 + 2, 2, 48, 256),
+        low(shard_rows // 128 + 2, 2, 16, 512),
+        low(shard_rows // 128 + 2, 2, 16, 512),
+        low(shard_rows // 192 + 2, 2, 48, 256),
+        low(shard_rows // 128 + 2, 2, 16, 512),
         low(32, 16, 128),
         low(24, 48, 256),
         low(32, 16, 512),
@@ -1607,13 +1788,13 @@
         vm(REST_PART, 128),
         vm(REST_PART, 128),
         vm(REST_PART, 128),
-        vm(64, 128),
-        vm(64, 128),
-        vm(64, 128),
+        vm(TABLE_ROWS, 128),
+        vm(TABLE_ROWS, 128),
+        vm(TABLE_ROWS, 128),
         dma((PHASES,)),
         dma((PHASES, 2)),
-        dma((15,)),
-        dma((15,)),
+        dma((17,)),
+        dma((17,)),
         dma((2, 2)),
         dma((4,)),
         dma((2,)),
@@ -1624,11 +1805,12 @@
         dma((2,)),
         dma,
         dma,
+        dma((2,)),
         dma((9,)),
         dma((9,)),
         dma((9,)),
         dma((9,)),
-        dma((9,)),
+        dma((9, 4)),
         dma((9,)),
         dma((9,)),
         dma((9,)),

time: 180 us -> 162 us (0.900)
  Pallas kernels: 174 us -> 155 us
    pallas_call x1, Pallas kernels: 174 us -> 155 us  [call_kernel(): pl.pallas_call(make_kernel(n), out_shape=outs, in_specs=[smem if i == 2 e...]
where the time goes in v2:
time: 162 us
  Pallas kernels  155 us (96%)
  local copies, waits for them, and re-layouts  5.91 us (4%)
    pallas_call x1, Pallas kernels, call_kernel(): pl.pallas_call(make_kernel(n), out_shape=outs, in_specs=[smem if i == 2 e...  155 us

profile of v2, /device:TPU:9, one launch (start us, length us, event | category | flops | bytes accessed | tf_op | source)
XLA Modules:
  0.0 161.9 jit_solution(3190022368913774122)
XLA Ops:
  0.6 1.9 %copy.7 = bf16[2,16,2,16,2,128]{5,3,1,4,2,0:T(8,128)(2,1)} copy(bf16[2,16,2,16,2,128]{5,4,3,2,1,0:T(2,128)(2,1)} %bitcast.15) | data formatting | bytes 1048576 | tf_op jit(solution)/shard_map/reshape | solution.py:1845
  2.5 155.4 %shard_map.67 = (bf16[2,256,256]{2,1,0:T(8,128)(2,1)}, bf16[2,4,256,128]{3,2,1,0:T(8,128)(2,1)}, f32[1320,128]{1,0:T(8,128)}) custom-call(bf16[2,4,256,128]{3,2,1,0:T(8,128)(2,1)} %bitcast.12, bf16[2,256,256]{2,1,0:T(8,128)(2,1)} %bitcast.19, s32[2]{0:T(128)} %codes.1, f32[1320,128]{1,0:T(8,128)} %bitcast.13), custom_call_target="tpu_custom_call" | custom-call | tf_op jit(solution)/shard_map/pallas_call | solution.py:1831
  157.9 0.0 copy-start.1
  157.9 0.0 copy-start
  157.9 2.5 %copy.8 = bf16[2,16,2,16,2,128]{5,4,3,2,1,0:T(2,128)(2,1)} copy(bf16[2,16,2,16,2,128]{5,3,1,4,2,0:T(8,128)(2,1)} %bitcast.17) | data formatting | bytes 1048576 | tf_op jit(solution)/shard_map/transpose | solution.py:1857
  160.4 0.0 copy-done.1
  160.4 0.7 copy.11
  161.1 0.0 copy-done
  161.1 0.8 copy.12
Async XLA Ops:
  157.9 2.5 %copy-start.1 = (bf16[2,256,256]{2,1,0:T(8,128)(2,1)S(1)}, bf16[2,256,256]{2,1,0:T(8,128)(2,1)}, u32[]{:S(2)}) copy-start(bf16[2,256,256]{2,1,0:T(8,128)(2,1)} %get-tuple-element.6) | copy-start | bytes 786436
  157.9 3.2 %copy-start = (f32[1320,128]{1,0:T(8,128)S(1)}, f32[1320,128]{1,0:T(8,128)}, u32[]{:S(2)}) copy-start(f32[1320,128]{1,0:T(8,128)} %get-tuple-element.8) | copy-start | bytes 2027524

commit v3 on v2

--- a/solution.py
+++ b/solution.py
@@ -19,6 +19,22 @@
 F32 = jnp.float32
 BF16 = jnp.bfloat16
 PHASES = 14
+ROWS = (
+    (3, 0),
+    (4, 0),
+    (2, 2),
+    (16, 0),
+    (2, 0),
+    (4, 0),
+    (2, 2),
+    (8, 0),
+    (8, 0),
+    (10, 2),
+    (2, 0),
+    (16, 0),
+    (10, 2),
+    (2, 0),
+)
 
 
 class Matrix:
@@ -50,27 +66,32 @@
 USED = (10530, 4116, 5390, 2064)
 REST_ROWS = 782
 HOME_ROWS = 1152
-REST_PART = 98
+REST_PART = 97
 AT_SQ, AT_GSQ, AT_BSQ, AT_EX, AT_BEX = 8, 264, 265, 266, 778
 TABLE = {
     (0, "g_in"): (0, 1024, 1),
     (0, "b_in"): (2, 1026, 1),
-    (0, "g_sc"): (4, 10514, 4),
-    (0, "b_sc"): (12, 10522, 4),
+    (0, "g_mid"): (4, 5636, 2),
+    (0, "b_mid"): (8, 5640, 2),
+    (0, "g_sc"): (12, 10514, 4),
+    (0, "b_sc"): (20, 10522, 4),
     (1, "g_out"): (28, 2048, 4),
     (1, "b_out"): (36, 2056, 4),
     (1, "g_in"): (44, 4112, 1),
     (1, "b_in"): (46, 4114, 1),
     (3, "g_out"): (48, 2048, 4),
     (3, "b_out"): (56, 2056, 4),
+    (2, "g_mid"): (64, 4608, 2),
+    (2, "b_mid"): (68, 4612, 2),
 }
 TABLE_ROWS = 72
+LATE_ROWS = 12
 SECTION_ROWS = {0: (0, 28), 1: (28, 20), 2: (64, 8), 3: (48, 16)}
-AT_MID = {0: 20, 2: 64}
+AT_MID = {0: 4, 2: 64}
 RANGES = (
     (0, 1024, 4, 0),
-    (0, 5636, 8, 20),
-    (0, 10514, 16, 4),
+    (0, 5636, 8, 4),
+    (0, 10514, 16, 12),
     (1, 2048, 16, 28),
     (1, 4112, 4, 44),
     (2, 4608, 8, 64),
@@ -234,6 +255,18 @@
         gvt,
         gvl,
         gvs,
+        gd_mid0,
+        gt_mid0,
+        gd_mid2,
+        gt_mid2,
+        gd_sc,
+        gt_sc,
+        gd_out1,
+        gt_out1,
+        gd_out3,
+        gt_out3,
+        gd_in1,
+        gt_in1,
         ssem,
         rsem,
         bs,
@@ -262,6 +295,8 @@
         gc_r,
         v_s,
         v_r,
+        gd_s,
+        gd_r,
     ):
         s = lax.axis_index("section")
         d = lax.axis_index("dp")
@@ -703,36 +738,62 @@
 
             lax.fori_loop(0, 4 * n, one, 0)
 
+        def part_of(mat, ref, quarter, part):
+            half = mat.pieces // 2
+            return ref.at[pl.ds(quarter * mat.pieces + part * half, half)]
+
         def shed(mat, gw, land):
-            for i in range(1, 4):
-                to = lax.rem(s + i, 4)
+            for part, to in enumerate((beside_x, beside_y)):
+                for i, quarter in enumerate((to, 3 - s)):
+                    pltpu.make_async_remote_copy(
+                        part_of(mat, gw, quarter, part),
+                        land.at[part, i],
+                        ga_s.at[mat.index],
+                        ga_r.at[mat.index, part],
+                        device_id=(to, d),
+                        device_id_type=MESH,
+                    ).start()
+
+        def shed_mid(mat, gw, land, add, land3):
+            half = mat.pieces // 2
+            for part, to in enumerate((beside_y, beside_x)):
+                full_wait(land.at[part], ga_r.at[mat.index, part])
+                base = to * mat.pieces + part * half
+
+                def one(i, _):
+                    x = gw[base + i].astype(F32) + land[part, 1, i].astype(F32)
+                    add[part, i] = x.astype(BF16)
+                    return 0
+
+                lax.fori_loop(0, half, one, 0)
                 pltpu.make_async_remote_copy(
-                    gw.at[pl.ds(to * mat.pieces, mat.pieces)],
-                    land.at[i - 1],
-                    ga_s.at[mat.index],
-                    ga_r.at[mat.index],
+                    add.at[part],
+                    land3.at[part],
+                    gd_s.at[mat.index],
+                    gd_r.at[mat.index, part],
                     device_id=(to, d),
                     device_id_type=MESH,
                 ).start()
 
-        def shed_more(mat, gw, land, part, land2):
-            full_wait(land, ga_r.at[mat.index])
-
-            def one(i, _):
-                x = gw[s * mat.pieces + i].astype(F32)
-                for j in range(3):
-                    x = x + land[j, i].astype(F32)
-                part[i] = x.astype(BF16)
-                move(
-                    part.at[i],
-                    land2.at[c, k],
-                    gb_s.at[mat.index],
-                    gb_r.at[mat.index],
-                    (s, mat.first + mat.step * i),
-                )
-                return 0
-
-            lax.fori_loop(0, mat.pieces, one, 0)
+        def shed_more(mat, gw, land, land3, part_sum, land2):
+            half = mat.pieces // 2
+            for part in range(2):
+                full_wait(land3.at[part], gd_r.at[mat.index, part])
+
+                def one(j, _):
+                    i = part * half + j
+                    x = gw[s * mat.pieces + i].astype(F32) + land[part, 0, j].astype(F32)
+                    part_sum[i] = (x + land3[part, j].astype(F32)).astype(BF16)
+                    move(
+                        part_sum.at[i],
+                        land2.at[c, k],
+                        gb_s.at[mat.index],
+                        gb_r.at[mat.index],
+                        (s, mat.first + mat.step * i),
+                    )
+                    return 0
+
+                lax.fori_loop(0, half, one, 0)
 
         def home_rows(src, src_at, start, rows, limit, r, active):
             left = jnp.int32(0)
@@ -789,8 +850,9 @@
                 )
             return left
 
-        def end_shed(mat, gw, land):
-            full_wait(land, ga_s.at[mat.index])
+        def end_shed(mat, gw):
+            full_wait(gw.at[pl.ds(0, 2 * mat.pieces)], ga_s.at[mat.index])
+            full_wait(gw.at[pl.ds(0, mat.pieces)], gd_s.at[mat.index])
 
             @pl.when(holds(mat))
             def _():
@@ -804,7 +866,7 @@
             @pl.when((s == mat.row) & (d < 8))
             def _():
                 pltpu.make_async_remote_copy(
-                    rg.at[pl.ds(REST_PART * d, REST_PART)],
+                    rg.at[pl.ds(AT_SQ + REST_PART * d, REST_PART)],
                     land,
                     v_s.at[i],
                     v_r.at[i],
@@ -814,7 +876,7 @@
 
         def rest_home(i, mat, rg, land, flat):
             active = (s == mat.row + 1) & (d < 8)
-            at = REST_PART * jnp.minimum(d, 7)
+            at = AT_SQ + REST_PART * jnp.minimum(d, 7)
 
             @pl.when(active)
             def _():
@@ -864,47 +926,37 @@
             for j in range(value.shape[1] // 128):
                 snd[ph, base + j : base + j + 1, :] = value[:, 128 * j : 128 * (j + 1)]
 
-        def send(ph, rows, both=False):
-            def one(o, _):
+        def send(ph):
+            mine, theirs = ROWS[ph]
+
+            def to(o, kk, rows):
                 pltpu.make_async_remote_copy(
                     snd.at[ph, pl.ds(0, rows)],
                     rcv.at[ph, k, o, pl.ds(0, rows)],
                     ssem.at[ph],
                     rsem.at[ph, k],
-                    device_id=peer(o, k),
+                    device_id=peer(o, kk),
                     device_id_type=MESH,
                 ).start()
                 return 0
 
-            def other(o, _):
-                pltpu.make_async_remote_copy(
-                    snd.at[ph, pl.ds(0, rows)],
-                    rcv.at[ph, k, o, pl.ds(0, rows)],
-                    ssem.at[ph],
-                    rsem.at[ph, k],
-                    device_id=peer(o, 1 - k),
-                    device_id_type=MESH,
-                ).start()
-                return 0
-
-            lax.fori_loop(1, n, one, 0)
-            if both:
-                lax.fori_loop(0, n, other, 0)
-            rcv[ph, k, 0, 0:rows] = snd[ph, 0:rows]
-
-        def receive(ph, rows, both=False):
-            mine = rcv.at[ph, k, pl.ds(1, n - 1), pl.ds(0, rows)]
-            pltpu.make_async_copy(mine, mine, rsem.at[ph, k]).wait()
-            if both:
-                theirs = rcv.at[ph, 1 - k, :, pl.ds(0, rows)]
-                pltpu.make_async_copy(theirs, theirs, rsem.at[ph, 1 - k]).wait()
-
-        def end_send(ph, rows, both=False):
-            many = 2 * n - 1 if both else n - 1
-            full_wait(fill.at[pl.ds(0, many * rows)], ssem.at[ph])
-
-        def totals(ph, rows):
-            return jnp.sum(rcv[ph, k, :, 0:rows, :], axis=0)
+            lax.fori_loop(1, n, lambda o, _: to(o, k, mine), 0)
+            if theirs:
+                lax.fori_loop(0, n, lambda o, _: to(o, 1 - k, theirs), 0)
+            rcv[ph, k, 0] = snd[ph]
+
+        def receive(ph):
+            mine, theirs = ROWS[ph]
+            full_wait(rcv.at[ph, k, pl.ds(1, n - 1), pl.ds(0, mine)], rsem.at[ph, k])
+            if theirs:
+                full_wait(rcv.at[ph, 1 - k, :, pl.ds(0, theirs)], rsem.at[ph, 1 - k])
+
+        def end_send(ph):
+            mine, theirs = ROWS[ph]
+            full_wait(fill.at[pl.ds(0, (n - 1) * mine + n * theirs)], ssem.at[ph])
+
+        def totals(ph):
+            return jnp.sum(rcv[ph, k, :, 0 : -(-ROWS[ph][0] // 8) * 8, :], axis=0)
 
         def row(total, base, width):
             return jnp.concatenate(
@@ -993,14 +1045,14 @@
         put(0, 0, jnp.sum(t0, axis=0, keepdims=True))
         put(0, 1, jnp.sum(t1, axis=0, keepdims=True))
         put(0, 2, side_row)
-        send(0, 8)
+        send(0)
         sent = scatter_early(sent)
         pass_far(MID0, w_mid0)
         spread(SC0, ln_sc, st_sc, w_sc)
         spread(OUT1, ln_out1, st_out1, w_out1)
         table_arrived()
-        receive(0, 8)
-        total = totals(0, 8)
+        receive(0)
+        total = totals(0)
         sides = across(0, k, 2, 128)
         inv_area = 1.0 / (sides * sides)
         count1 = jnp.sum(sides * sides, axis=0, keepdims=True)
@@ -1046,7 +1098,7 @@
             zm = z * lanes(mref[...], 2)
             put(ph, 0, jnp.sum(zm, axis=0, keepdims=True))
             put(ph, 2, jnp.sum(zm * z, axis=0, keepdims=True))
-            send(ph, 8)
+            send(ph)
 
         def small(rest):
             w_sq = rest[AT_SQ : AT_SQ + CMID, :]
@@ -1070,11 +1122,11 @@
             acc = lax.fori_loop(0, 4, block, jnp.zeros((8, 256), F32))
             pooled_own = jnp.sum(acc, axis=0, keepdims=True) * lanes(inv_own, 2)
             put(ph, 0, pooled_own)
-            send(ph, 8, both=True)
+            send(ph)
             swap = to_twin(twin, rr.at[k], rr.at[k])
             swap.start()
             beside()
-            receive(ph, 8, both=True)
+            receive(ph)
             w_sq, w_ex = small(rest)
             pooled = across(ph, 0, 0, 256) + across(ph, 1, 0, 256)
             zq = dot_hi(pooled, w_sq)
@@ -1127,9 +1179,9 @@
             acc = lax.fori_loop(0, 8, block, (jnp.zeros((8, 256), F32),) * 5)
             for j, x in enumerate(acc):
                 put(ph, 2 * j, jnp.sum(x, axis=0, keepdims=True))
-            send(ph, 16, both=True)
+            send(ph)
             beside()
-            receive(ph, 16, both=True)
+            receive(ph)
             ds0 = across(ph, 0, 0, 256)
             ds1 = across(ph, 1, 0, 256)
             mean = sh0 * ds0 + sh1 * ds1
@@ -1149,19 +1201,17 @@
             dpool = dot_hi(dzq, w_sq, ((1,), (1,))) * lanes(inv_area, 2)
             share = jnp.where(k == 0, sh0, sh1)
 
-            def both_sums(h, part, first, second):
+            def both_sums(first, second):
                 return jnp.sum(
-                    part * across(ph, h, first, 256) + dpool * across(ph, h, second, 256),
+                    share * across(ph, k, first, 256) + dpool * across(ph, k, second, 256),
                     axis=0,
                     keepdims=True,
                 )
 
-            sums = [(both_sums(h, x, 2, 4), both_sums(h, x, 6, 8)) for h, x in enumerate((sh0, sh1))]
-            for h in range(2):
-                set_rows(rg, 2 * h, sums[h][1])
-                set_rows(rg, 4 + 2 * h, sums[h][0])
-            sdv = jnp.where(k == 0, sums[0][0], sums[1][0])
-            sdh = jnp.where(k == 0, sums[0][1], sums[1][1])
+            sdv = both_sums(2, 4)
+            sdh = both_sums(6, 8)
+            set_gvec((mat.row, "b_mid"), sdv)
+            set_gvec((mat.row, "g_mid"), sdh)
             own_share = share[0:1, :]
             own_pool = dpool[0:1, :]
             c1 = sdv / counts[256]
@@ -1197,7 +1247,7 @@
         pass_on(SC0, w_sc)
         pass_on(OUT1, w_out1)
         spread(IN1, ln_in1, st_in1, w_in1)
-        receive(1, 8)
+        receive(1)
 
         def short_forward():
             share_rest(REST0, rest0, 15)
@@ -1212,21 +1262,21 @@
             put(3, 12, jnp.sum(z * z, axis=0, keepdims=True))
             rest_arrived(rest0, 15)
 
-        mid1, q1 = attention_forward(2, 2, totals(1, 8), AT_MID[0], rest0, z2, rr1, a1, short_forward)
+        mid1, q1 = attention_forward(2, 2, totals(1), AT_MID[0], rest0, z2, rr1, a1, short_forward)
         arrived(OUT1, w_out1)
 
-        def wide_forward(ph, rows, aref, w, zref):
+        def wide_forward(ph, aref, w, zref):
             z = dot(aref[...], w[...].reshape(CMID, 512))
             zref[...] = z
             put(ph, 0, jnp.sum(z, axis=0, keepdims=True))
             put(ph, 4, jnp.sum(z * z, axis=0, keepdims=True))
-            send(ph, rows)
-
-        wide_forward(3, 16, a1, w_out1, z3)
+            send(ph)
+
+        wide_forward(3, a1, w_out1, z3)
         pass_far(IN1, w_in1)
         pass_on(MID2, w_mid2)
-        receive(3, 16)
-        total = totals(3, 16)
+        receive(3)
+        total = totals(3)
         mus, rss = mean_rstd(total, 8, 512, counts[512])
         lins = rss * vrow((0, "g_sc"))
         offs = vrow((0, "b_sc")) - mus * lins
@@ -1254,12 +1304,12 @@
         z4[...] = z
         put(4, 0, jnp.sum(z, axis=0, keepdims=True))
         put(4, 1, jnp.sum(z * z, axis=0, keepdims=True))
-        send(4, 8)
+        send(4)
         pass_far(MID2, w_mid2)
         spread_rest(REST2, ln_rest2, rest2)
         spread(OUT3, ln_out3, st_out3, w_out3)
-        receive(4, 8)
-        mu4, rs4 = mean_rstd(totals(4, 8), 0, 128, count1)
+        receive(4)
+        mu4, rs4 = mean_rstd(totals(4), 0, 128, count1)
         lin4 = rs4 * vrow((1, "g_in"))
         off4 = vrow((1, "b_in")) - mu4 * lin4
         v = z4[...] * lin4 + off4
@@ -1273,7 +1323,7 @@
         conv_forward(5, cols2, w_mid2, z5)
         share_rest(REST2, rest2, 16)
         pass_on(OUT3, w_out3)
-        receive(5, 8)
+        receive(5)
 
         def last_weights():
             pass_far(OUT3, w_out3)
@@ -1288,14 +1338,14 @@
                 )
             to_twin(14, w_in0.at[k], w_in0.at[k]).start()
 
-        mid2, q2 = attention_forward(6, 4, totals(5, 8), AT_MID[2], rest2, z5, rr2, a2, last_weights)
+        mid2, q2 = attention_forward(6, 4, totals(5), AT_MID[2], rest2, z5, rr2, a2, last_weights)
         arrived(OUT3, w_out3)
-        wide_forward(7, 8, a2, w_out3, z6)
+        wide_forward(7, a2, w_out3, z6)
         to_twin(14, w_in0.at[k], w_in0.at[k]).wait()
         for i in range(2):
             pltpu.make_async_copy(ctb.at[i], ctb.at[i], ct_r.at[i]).wait()
-        receive(7, 8)
-        mu6, rs6 = mean_rstd(totals(7, 8), 0, 512, counts[512])
+        receive(7)
+        mu6, rs6 = mean_rstd(totals(7), 0, 512, counts[512])
         lin6 = rs6 * vrow((3, "g_out"))
         off6 = vrow((3, "b_out")) - mu6 * lin6
 
@@ -1317,7 +1367,7 @@
         t0, t1 = lax.fori_loop(0, 8, out_block, (zero512, zero512))
         put(8, 0, jnp.sum(t0, axis=0, keepdims=True))
         put(8, 4, jnp.sum(t1, axis=0, keepdims=True))
-        send(8, 8)
+        send(8)
         for j in range(2):
             move(
                 obuf.at[j],
@@ -1330,7 +1380,7 @@
             end_spread(mat, whole)
         end_rest(REST0, rest0, 15)
         end_table()
-        receive(8, 8)
+        receive(8)
 
         def wide_back(total, base, key_g, key_b, lin, mu, rs, zref, dvf, dst):
             sdv = row(total, base, 512)
@@ -1350,7 +1400,7 @@
             lax.fori_loop(0, 8, block, 0)
 
         wide_back(
-            totals(8, 8),
+            totals(8),
             0,
             (3, "g_out"),
             (3, "b_out"),
@@ -1379,7 +1429,7 @@
             for mat, whole in ((IN1, w_in1), (MID2, w_mid2), (OUT3, w_out3)):
                 end_spread(mat, whole)
             end_rest(REST2, rest2, 16)
-            shed_more(OUT3, gw_out3, ga_out3, gp_out3, gb_out3)
+            shed_mid(OUT3, gw_out3, ga_out3, gt_out3, gd_out3)
 
         grad_rest2 = attention_backward(
             9,
@@ -1414,12 +1464,12 @@
         dh[0] = dv4
         put(10, 0, jnp.sum(dv4, axis=0, keepdims=True))
         put(10, 1, jnp.sum(dv4 * hat4, axis=0, keepdims=True))
-        send(10, 8)
+        send(10)
         grad_rest2()
         rest_meet(2, REST2, rg2, rl2)
-        left = home(OUT3, gb_out3, gf_out3)
-        receive(10, 8)
-        total = totals(10, 8)
+        shed_more(OUT3, gw_out3, ga_out3, gd_out3, gp_out3, gb_out3)
+        receive(10)
+        total = totals(10)
         set_gvec((1, "b_in"), total[0:1, :])
         set_gvec((1, "g_in"), total[1:2, :])
         hat4 = (z4[...] - mu4) * rs4
@@ -1448,14 +1498,14 @@
         acc = lax.fori_loop(0, 4, dy_block, (zero512,) * 4)
         for j, x in enumerate(acc):
             put(11, 4 * j, jnp.sum(x, axis=0, keepdims=True))
-        send(11, 16)
+        send(11)
         both4 = jnp.concatenate([dz4[0], dz4[1]], axis=1)
         gw_in1[...] = dot_lt(y1[...], both4).astype(BF16).reshape(32, 16, 256)
         shed(IN1, gw_in1, ga_in1)
-        shed_more(MID2, gw_mid2, ga_mid2, gp_mid2, gb_mid2)
-        left = left + rest_home(2, REST2, rg2, rl2, rf2)
-        receive(11, 16)
-        total = totals(11, 16)
+        shed_mid(MID2, gw_mid2, ga_mid2, gt_mid2, gd_mid2)
+        left = home(OUT3, gb_out3, gf_out3) + rest_home(2, REST2, rg2, rl2, rf2)
+        receive(11)
+        total = totals(11)
         wide_back(
             total,
             0,
@@ -1489,9 +1539,10 @@
             pdp[2] = jnp.where(k == 0, part[:, 0:256], part[:, 256:512])
             gw_sc[...] = dot_lt(pool[...], dzs[...]).astype(BF16).reshape(32, 16, 512)
             shed(SC0, gw_sc, ga_sc)
-            table_meet(0, 4, TABLE_ROWS - 4)
-            shed_more(IN1, gw_in1, ga_in1, gp_in1, gb_in1)
-            shed_more(OUT1, gw_out1, ga_out1, gp_out1, gb_out1)
+            table_meet(0, LATE_ROWS, TABLE_ROWS - LATE_ROWS)
+            shed_mid(IN1, gw_in1, ga_in1, gt_in1, gd_in1)
+            shed_mid(OUT1, gw_out1, ga_out1, gt_out1, gd_out1)
+            shed_more(MID2, gw_mid2, ga_mid2, gd_mid2, gp_mid2, gb_mid2)
 
         grad_rest0 = attention_backward(
             12,
@@ -1535,19 +1586,19 @@
         t0, t1 = lax.fori_loop(0, 4, dv1_block, (zero8, zero8))
         put(13, 0, jnp.sum(t0, axis=0, keepdims=True))
         put(13, 1, jnp.sum(t1, axis=0, keepdims=True))
-        send(13, 8)
+        send(13)
         grad_rest0()
         rest_meet(1, REST0, rg0, rl0)
-        shed_more(SC0, gw_sc, ga_sc, gp_sc, gb_sc)
+        shed_more(IN1, gw_in1, ga_in1, gd_in1, gp_in1, gb_in1)
+        shed_more(OUT1, gw_out1, ga_out1, gd_out1, gp_out1, gb_out1)
+        shed_mid(SC0, gw_sc, ga_sc, gt_sc, gd_sc)
         left = left + home(MID2, gb_mid2, gf_mid2)
-        left = left + home(IN1, gb_in1, gf_in1)
-        left = left + home(OUT1, gb_out1, gf_out1)
-        left = left + table_home(0, 4, TABLE_ROWS - 4)
-        receive(13, 8)
-        total = totals(13, 8)
+        left = left + table_home(0, LATE_ROWS, TABLE_ROWS - LATE_ROWS)
+        receive(13)
+        total = totals(13)
         set_gvec((0, "b_in"), total[0:1, :])
         set_gvec((0, "g_in"), total[1:2, :])
-        table_meet(3, 0, 4)
+        table_meet(3, 0, LATE_ROWS)
         k1 = total[0:1, :] / (4.0 * count1)
         k2 = total[1:2, :] / (4.0 * count1)
 
@@ -1576,7 +1627,8 @@
             return 0
 
         lax.fori_loop(0, 32, shed_in0, 0)
-        shed_more(MID0, gw_mid0, ga_mid0, gp_mid0, gb_mid0)
+        shed_more(SC0, gw_sc, ga_sc, gd_sc, gp_sc, gb_sc)
+        shed_mid(MID0, gw_mid0, ga_mid0, gt_mid0, gd_mid0)
         swap.wait()
         to_twin(8, pdp.at[0], pdp.at[1]).wait()
 
@@ -1600,21 +1652,24 @@
                 (2 * k + j, 2 * c + s // 2),
             )
 
+        left = left + home(IN1, gb_in1, gf_in1)
+        left = left + home(OUT1, gb_out1, gf_out1)
+        shed_more(MID0, gw_mid0, ga_mid0, gd_mid0, gp_mid0, gb_mid0)
         left = left + home(SC0, gb_sc, gf_sc)
         left = left + rest_home(1, REST0, rg0, rl0, rf0)
-        left = left + table_home(3, 0, 4)
+        left = left + table_home(3, 0, LATE_ROWS)
         left = left + home(IN0, gb_in0, gf_in0)
         left = left + home(MID0, gb_mid0, gf_mid0)
 
-        for mat, gw, land in (
-            (MID0, gw_mid0, ga_mid0),
-            (SC0, gw_sc, ga_sc),
-            (OUT1, gw_out1, ga_out1),
-            (IN1, gw_in1, ga_in1),
-            (MID2, gw_mid2, ga_mid2),
-            (OUT3, gw_out3, ga_out3),
+        for mat, gw in (
+            (MID0, gw_mid0),
+            (SC0, gw_sc),
+            (OUT1, gw_out1),
+            (IN1, gw_in1),
+            (MID2, gw_mid2),
+            (OUT3, gw_out3),
         ):
-            end_shed(mat, gw, land)
+            end_shed(mat, gw)
 
         @pl.when(holds(IN0))
         def _():
@@ -1633,8 +1688,8 @@
 
         @pl.when((s == 0) & (d < 2))
         def _():
-            full_wait(gvl.at[pl.ds(4, TABLE_ROWS - 4)], v_s.at[0])
-            full_wait(gvl.at[pl.ds(0, 4)], v_s.at[3])
+            full_wait(gvl.at[pl.ds(LATE_ROWS, TABLE_ROWS - LATE_ROWS)], v_s.at[0])
+            full_wait(gvl.at[pl.ds(0, LATE_ROWS)], v_s.at[3])
 
         fill_up(nought, fill2, left, HOME_ROWS, gc_s)
         full_wait(fill2, gc_s)
@@ -1658,7 +1713,7 @@
             here = u.at[q, pl.ds(2 * k, 2)]
             pltpu.make_async_copy(here, here, bs.at[10 + q]).wait()
         for ph in range(PHASES):
-            end_send(ph, 16 if ph in (3, 9, 11, 12) else 8, ph in (2, 6, 9, 12))
+            end_send(ph)
 
     return kernel
 
@@ -1756,12 +1811,12 @@
         low(32, 16, 256),
         low(24, 48, 256),
         low(16, 16, 512),
-        low(3, 6, 48, 256),
-        low(3, 8, 16, 512),
-        low(3, 4, 16, 512),
-        low(3, 8, 16, 256),
-        low(3, 6, 48, 256),
-        low(3, 4, 16, 512),
+        low(2, 2, 3, 48, 256),
+        low(2, 2, 4, 16, 512),
+        low(2, 2, 2, 16, 512),
+        low(2, 2, 4, 16, 256),
+        low(2, 2, 3, 48, 256),
+        low(2, 2, 2, 16, 512),
         low(6, 48, 256),
         low(8, 16, 512),
         low(4, 16, 512),
@@ -1791,6 +1846,18 @@
         vm(TABLE_ROWS, 128),
         vm(TABLE_ROWS, 128),
         vm(TABLE_ROWS, 128),
+        low(2, 3, 48, 256),
+        low(2, 3, 48, 256),
+        low(2, 3, 48, 256),
+        low(2, 3, 48, 256),
+        low(2, 4, 16, 512),
+        low(2, 4, 16, 512),
+        low(2, 2, 16, 512),
+        low(2, 2, 16, 512),
+        low(2, 2, 16, 512),
+        low(2, 2, 16, 512),
+        low(2, 4, 16, 256),
+        low(2, 4, 16, 256),
         dma((PHASES,)),
         dma((PHASES, 2)),
         dma((17,)),
@@ -1812,13 +1879,15 @@
         dma((9,)),
         dma((9, 4)),
         dma((9,)),
-        dma((9,)),
+        dma((9, 2)),
         dma((9,)),
         dma((9,)),
         dma,
         dma,
         dma((4,)),
         dma((4,)),
+        dma((9,)),
+        dma((9, 2)),
     ]
     sds = jax.ShapeDtypeStruct
     outs = (

time: 162 us -> 157 us (0.969)
  Pallas kernels: 155 us -> 150 us
    pallas_call x1, Pallas kernels: 155 us -> 150 us  [call_kernel(): pl.pallas_call(make_kernel(n), out_shape=outs, in_specs=[smem if i == 2 e...]
where the time goes in v3:
time: 157 us
  Pallas kernels  150 us (96%)
  local copies, waits for them, and re-layouts  5.91 us (4%)
    pallas_call x1, Pallas kernels, call_kernel(): pl.pallas_call(make_kernel(n), out_shape=outs, in_specs=[smem if i == 2 e...  150 us

profile of v3, /device:TPU:9, one launch (start us, length us, event | category | flops | bytes accessed | tf_op | source)
XLA Modules:
  0.0 156.6 jit_solution(6787526665947635279)
XLA Ops:
  0.6 1.9 %copy.7 = bf16[2,16,2,16,2,128]{5,3,1,4,2,0:T(8,128)(2,1)} copy(bf16[2,16,2,16,2,128]{5,4,3,2,1,0:T(2,128)(2,1)} %bitcast.15) | data formatting | bytes 1048576 | tf_op jit(solution)/shard_map/reshape | solution.py:1914
  2.5 150.0 %shard_map.67 = (bf16[2,256,256]{2,1,0:T(8,128)(2,1)}, bf16[2,4,256,128]{3,2,1,0:T(8,128)(2,1)}, f32[1320,128]{1,0:T(8,128)}) custom-call(bf16[2,4,256,128]{3,2,1,0:T(8,128)(2,1)} %bitcast.12, bf16[2,256,256]{2,1,0:T(8,128)(2,1)} %bitcast.19, s32[2]{0:T(128)} %codes.1, f32[1320,128]{1,0:T(8,128)} %bitcast.13), custom_call_target="tpu_custom_call" | custom-call | tf_op jit(solution)/shard_map/pallas_call | solution.py:1900
  152.6 0.0 copy-start.1
  152.6 0.0 copy-start
  152.6 2.5 %copy.8 = bf16[2,16,2,16,2,128]{5,4,3,2,1,0:T(2,128)(2,1)} copy(bf16[2,16,2,16,2,128]{5,3,1,4,2,0:T(8,128)(2,1)} %bitcast.17) | data formatting | bytes 1048576 | tf_op jit(solution)/shard_map/transpose | solution.py:1926
  155.0 0.0 copy-done.1
  155.0 0.7 copy.11
  155.7 0.0 copy-done
  155.7 0.8 copy.12
Async XLA Ops:
  152.6 2.5 %copy-start.1 = (bf16[2,256,256]{2,1,0:T(8,128)(2,1)S(1)}, bf16[2,256,256]{2,1,0:T(8,128)(2,1)}, u32[]{:S(2)}) copy-start(bf16[2,256,256]{2,1,0:T(8,128)(2,1)} %get-tuple-element.6) | copy-start | bytes 786436
  152.6 3.2 %copy-start = (f32[1320,128]{1,0:T(8,128)S(1)}, f32[1320,128]{1,0:T(8,128)}, u32[]{:S(2)}) copy-start(f32[1320,128]{1,0:T(8,128)} %get-tuple-element.8) | copy-start | bytes 2027524

commit v4 on v3

--- a/solution.py
+++ b/solution.py
@@ -62,7 +62,7 @@
 REST2 = Matrix(7, 2, 4608, 1, 8, 25, 0, 1, split="none")
 OUT3 = Matrix(8, 3, 0, 8, 4, 16, 0, 2)
 MATRICES = (IN0, MID0, REST0, SC0, OUT1, IN1, MID2, REST2, OUT3)
-PRODUCTS = (IN0, MID0, SC0, OUT1, IN1, MID2, OUT3)
+CUT = (IN0, MID0, SC0, OUT1, MID2, OUT3)
 USED = (10530, 4116, 5390, 2064)
 REST_ROWS = 782
 HOME_ROWS = 1152
@@ -267,6 +267,22 @@
         gt_out3,
         gd_in1,
         gt_in1,
+        hb_in0,
+        hi_in0,
+        hb_mid0,
+        hi_mid0,
+        hb_sc,
+        hi_sc,
+        hb_out1,
+        hi_out1,
+        hb_mid2,
+        hi_mid2,
+        hb_out3,
+        hi_out3,
+        fill3,
+        pixels,
+        planes,
+        merged,
         ssem,
         rsem,
         bs,
@@ -297,6 +313,13 @@
         v_r,
         gd_s,
         gd_r,
+        hr_in0,
+        hr_mid0,
+        hr_sc,
+        hr_out1,
+        hr_mid2,
+        hr_out3,
+        hs_s,
     ):
         s = lax.axis_index("section")
         d = lax.axis_index("dp")
@@ -306,12 +329,12 @@
         g = (s // 2) * chips + c
 
         def peer(o, kk):
-            gg = lax.rem(g + o, n)
+            gg = g ^ o
             return ((gg // chips) * 2 + m, 2 * (gg % chips) + kk)
 
+        order = sorted(range(1, n), key=lambda o: (o % chips) + o // chips, reverse=True)
+
         nought[...] = jnp.zeros(nought.shape, F32)
-        sround[...] = shard[...].astype(BF16).astype(F32)
-
         barrier = pltpu.get_barrier_semaphore()
         me = s * n + d
         beside_x = s + 1 - 2 * (s % 2)
@@ -323,6 +346,25 @@
             return 0
 
         lax.fori_loop(1, 4 * n, greet, 0)
+        sround[...] = shard[...].astype(BF16).astype(F32)
+
+        for slot in range(2):
+
+            def widen(i, _):
+                rows = pl.ds(pl.multiple_of(i * 128, 128), 128)
+                pixels[rows, :] = img[slot, rows, :].astype(F32)
+                return 0
+
+            lax.fori_loop(0, 8, widen, 0)
+
+            def split(r, _):
+                for p in range(4):
+                    at = (2 * r + p // 2) * 2 * SIDE + p % 2
+                    x = pixels[pl.ds(at, SIDE, stride=2), :]
+                    planes[slot, p, pl.ds(pl.multiple_of(r * SIDE, SIDE), SIDE), :] = x.astype(BF16)
+                return 0
+
+            lax.fori_loop(0, SIDE, split, 0)
         pl.semaphore_wait(barrier, 4 * n - 1)
 
         def to_twin(i, src, dst):
@@ -406,7 +448,6 @@
         used = jnp.where(
             s == 0, USED[0], jnp.where(s == 1, USED[1], jnp.where(s == 2, USED[2], USED[3]))
         )
-        fill_up(nought, out_w, jnp.clip(used - d * shard_rows, 0, shard_rows), shard_rows, gc_r)
 
         mine_from = d * shard_rows
         mine_to = mine_from + shard_rows
@@ -568,12 +609,15 @@
         def when_row(r, body):
             return lax.cond(s == r, body, lambda: jnp.int32(0))
 
-        sent = when_row(0, lambda: scatter_cut(IN0, ln_in0, st_in0, cu_in0))
+        sent = when_row(
+            0,
+            lambda: scatter_cut(MID0, ln_mid0, st_mid0, cu_mid0) + scatter_cut(IN0, ln_in0, st_in0, cu_in0),
+        )
 
         for slot in range(2):
             for kk in range(2):
                 move(
-                    img.at[slot, pl.ds(2 * kk, 2)],
+                    planes.at[slot, pl.ds(2 * kk, 2)],
                     u.at[s, pl.ds(2 * kk, 2)],
                     img_s.at[slot, kk],
                     img_r.at[s],
@@ -587,7 +631,7 @@
         snd[...] = jnp.zeros(snd.shape, F32)
 
         def row0():
-            count = scatter_cut(MID0, ln_mid0, st_mid0, cu_mid0) + scatter_table(*RANGES[0][1:])
+            count = scatter_table(*RANGES[0][1:])
             count = count + scatter_table(*RANGES[1][1:]) + scatter_table(*RANGES[2][1:])
             return count + scatter_cut(SC0, ln_sc, st_sc, cu_sc)
 
@@ -605,7 +649,6 @@
             return sent + when_row(3, lambda: scatter_cut(OUT3, ln_out3, st_out3, cu_out3, part, parts))
 
         def scatter_early(sent):
-            sent = sent + when_row(0, lambda: scatter_pieces(REST0, ln_rest0))
             sent = sent + when_row(1, lambda: scatter_pieces(IN1, ln_in1))
             return scatter_some(sent, 1, 3)
 
@@ -615,6 +658,7 @@
             fill_up(nought, fill, sent, fill_rows, h_s)
 
         sent = scatter_some(sent, 0, 3)
+        sent = sent + when_row(0, lambda: scatter_pieces(REST0, ln_rest0))
 
         def spread(mat, land, stage, whole):
             @pl.when(holds(mat))
@@ -737,6 +781,13 @@
                 return 0
 
             lax.fori_loop(0, 4 * n, one, 0)
+
+        def whole_rows():
+            count = jnp.int32(0)
+            for mat in CUT:
+                low, high = whole_range(mat)
+                count = count + jnp.where(s == mat.row, (high - low) * mat.flat, 0)
+            return count
 
         def part_of(mat, ref, quarter, part):
             half = mat.pieces // 2
@@ -850,6 +901,81 @@
                 )
             return left
 
+        def first_piece(mat, owner):
+            return jnp.maximum(owner * shard_rows - mat.start, 0) // mat.flat
+
+        def home_whole(mat):
+            start = mat.start + piece(mat) * mat.flat
+            return start, start // shard_rows == (start + mat.flat - 1) // shard_rows
+
+        def home_cut(mat, land2, flat, ready, inbox, in_sem, turn=None):
+            start, whole = home_whole(mat)
+            owner = jnp.minimum(start // shard_rows, n - 1)
+            held = holds(mat)
+            if turn is not None:
+                held = held & ((c < chips // 2) if turn == 0 else (c >= chips // 2))
+
+            @pl.when(held)
+            def _():
+                full_wait(land2, gb_r.at[mat.index])
+
+            @pl.when(held & whole)
+            def _():
+                for h in range(2):
+                    ready[h] = jnp.sum(land2[:, h].astype(F32), axis=0).astype(BF16)
+                slot = piece(mat) - first_piece(mat, owner)
+                move(ready, inbox.at[slot], hs_s.at[mat.index], in_sem.at[slot], (mat.row, owner))
+
+            @pl.when(held & jnp.logical_not(whole))
+            def _():
+                for h in range(2):
+                    x = jnp.sum(land2[:, h].astype(F32), axis=0)
+                    for j in range(mat.width // 128):
+                        at = h * (mat.blocks // 2) + j
+                        flat[pl.ds(at, mat.rows, stride=mat.blocks), :] = x[:, 128 * j : 128 * (j + 1)]
+
+            return home_rows(
+                flat,
+                0,
+                start,
+                mat.flat,
+                USED[mat.row],
+                mat.row,
+                held & jnp.logical_not(whole),
+            )
+
+        def end_home_cut(mat, ready):
+            start, whole = home_whole(mat)
+            away = (s != mat.row) | (d != start // shard_rows)
+
+            @pl.when(holds(mat) & whole & away)
+            def _():
+                full_wait(ready, hs_s.at[mat.index])
+
+        def whole_range(mat):
+            low = (jnp.maximum(mine_from - mat.start, 0) + mat.flat - 1) // mat.flat
+            high = jnp.minimum(jnp.maximum(mine_to - mat.start, 0) // mat.flat, 4 * mat.pieces)
+            return low, jnp.maximum(high, low)
+
+        def take(mat, inbox, in_sem):
+            @pl.when(s == mat.row)
+            def _():
+                low, high = whole_range(mat)
+                first = first_piece(mat, d)
+
+                def one(p, _):
+                    slot = p - first
+                    full_wait(inbox.at[slot], in_sem.at[slot])
+                    at = mat.start + p * mat.flat - mine_from
+                    for h in range(2):
+                        for j in range(mat.width // 128):
+                            x = inbox[slot, h, :, 128 * j : 128 * (j + 1)].astype(F32)
+                            row_at = at + h * (mat.blocks // 2) + j
+                            out_w[pl.ds(row_at, mat.rows, stride=mat.blocks), :] = x
+                    return 0
+
+                lax.fori_loop(low, high, one, 0)
+
         def end_shed(mat, gw):
             full_wait(gw.at[pl.ds(0, 2 * mat.pieces)], ga_s.at[mat.index])
             full_wait(gw.at[pl.ds(0, mat.pieces)], gd_s.at[mat.index])
@@ -940,9 +1066,17 @@
                 ).start()
                 return 0
 
-            lax.fori_loop(1, n, lambda o, _: to(o, k, mine), 0)
-            if theirs:
-                lax.fori_loop(0, n, lambda o, _: to(o, 1 - k, theirs), 0)
+            if n > 8:
+                lax.fori_loop(1, n, lambda o, _: to(o, k, mine), 0)
+                if theirs:
+                    lax.fori_loop(0, n, lambda o, _: to(o, 1 - k, theirs), 0)
+            else:
+                for o in order:
+                    to(o, k, mine)
+                    if theirs:
+                        to(o, 1 - k, theirs)
+                if theirs:
+                    to(0, 1 - k, theirs)
             rcv[ph, k, 0] = snd[ph]
 
         def receive(ph):
@@ -1001,6 +1135,7 @@
         mref[...] = jnp.where((prow < side_row) & (pcol < side_row), 1.0, 0.0)
         inv_own = 1.0 / (side_row * side_row)
 
+        spread(MID0, ln_mid0, st_mid0, w_mid0)
         for q in range(4):
             here = u.at[q, pl.ds(2 * k, 2)]
             pltpu.make_async_copy(here, here, img_r.at[q]).wait()
@@ -1012,7 +1147,6 @@
                 device_id=(s, 2 * c + 1 - k),
                 device_id_type=MESH,
             ).start()
-        spread(MID0, ln_mid0, st_mid0, w_mid0)
         for q in range(4):
             here = u.at[q, pl.ds(2 * (1 - k), 2)]
             pltpu.make_async_copy(here, here, br.at[10 + q]).wait()
@@ -1032,7 +1166,6 @@
 
         lax.fori_loop(0, 8, mask_block, 0)
         pass_table()
-        pass_on(MID0, w_mid0)
         full_wait(w_in0.at[k], c_r.at[0])
 
         def z1_block(p, carry):
@@ -1046,6 +1179,7 @@
         put(0, 1, jnp.sum(t1, axis=0, keepdims=True))
         put(0, 2, side_row)
         send(0)
+        pass_on(MID0, w_mid0)
         sent = scatter_early(sent)
         pass_far(MID0, w_mid0)
         spread(SC0, ln_sc, st_sc, w_sc)
@@ -1275,6 +1409,7 @@
         wide_forward(3, a1, w_out1, z3)
         pass_far(IN1, w_in1)
         pass_on(MID2, w_mid2)
+        spread_rest(REST2, ln_rest2, rest2)
         receive(3)
         total = totals(3)
         mus, rss = mean_rstd(total, 8, 512, counts[512])
@@ -1306,7 +1441,6 @@
         put(4, 1, jnp.sum(z * z, axis=0, keepdims=True))
         send(4)
         pass_far(MID2, w_mid2)
-        spread_rest(REST2, ln_rest2, rest2)
         spread(OUT3, ln_out3, st_out3, w_out3)
         receive(4)
         mu4, rs4 = mean_rstd(totals(4), 0, 128, count1)
@@ -1368,6 +1502,8 @@
         put(8, 0, jnp.sum(t0, axis=0, keepdims=True))
         put(8, 4, jnp.sum(t1, axis=0, keepdims=True))
         send(8)
+        fill_up(nought, out_w, jnp.clip(used - d * shard_rows, 0, shard_rows), shard_rows, gc_r)
+        fill_up(nought, fill3, 0, whole_rows(), gc_r)
         for j in range(2):
             move(
                 obuf.at[j],
@@ -1503,7 +1639,7 @@
         gw_in1[...] = dot_lt(y1[...], both4).astype(BF16).reshape(32, 16, 256)
         shed(IN1, gw_in1, ga_in1)
         shed_mid(MID2, gw_mid2, ga_mid2, gt_mid2, gd_mid2)
-        left = home(OUT3, gb_out3, gf_out3) + rest_home(2, REST2, rg2, rl2, rf2)
+        left = rest_home(2, REST2, rg2, rl2, rf2)
         receive(11)
         total = totals(11)
         wide_back(
@@ -1592,7 +1728,7 @@
         shed_more(IN1, gw_in1, ga_in1, gd_in1, gp_in1, gb_in1)
         shed_more(OUT1, gw_out1, ga_out1, gd_out1, gp_out1, gb_out1)
         shed_mid(SC0, gw_sc, ga_sc, gt_sc, gd_sc)
-        left = left + home(MID2, gb_mid2, gf_mid2)
+        left = left + home_cut(OUT3, gb_out3, gf_out3, hb_out3, hi_out3, hr_out3)
         left = left + table_home(0, LATE_ROWS, TABLE_ROWS - LATE_ROWS)
         receive(13)
         total = totals(13)
@@ -1627,8 +1763,11 @@
             return 0
 
         lax.fori_loop(0, 32, shed_in0, 0)
+        shed_mid(MID0, gw_mid0, ga_mid0, gt_mid0, gd_mid0)
         shed_more(SC0, gw_sc, ga_sc, gd_sc, gp_sc, gb_sc)
-        shed_mid(MID0, gw_mid0, ga_mid0, gt_mid0, gd_mid0)
+        left = left + home_cut(MID2, gb_mid2, gf_mid2, hb_mid2, hi_mid2, hr_mid2)
+        left = left + home(IN1, gb_in1, gf_in1)
+        left = left + home_cut(OUT1, gb_out1, gf_out1, hb_out1, hi_out1, hr_out1)
         swap.wait()
         to_twin(8, pdp.at[0], pdp.at[1]).wait()
 
@@ -1637,12 +1776,22 @@
             grad = dot_rt(dz1[0, p], w_in0[0, mine].reshape(256, 128))
             grad = grad + dot_rt(dz1[1, p], w_in0[1, mine].reshape(256, 128))
             grad = (grad + 0.25 * (pdp[1] + pdp[2])) * lanes(mref[...], 2)
-            low = grad.astype(BF16)
-            ibuf[0, p] = low[:, 0:128]
-            ibuf[1, p] = low[:, 128:256]
+            for r in range(SIDE):
+                at = (2 * r + p // 2) * 2 * SIDE + p % 2
+                for j in range(2):
+                    x = grad[SIDE * r : SIDE * (r + 1), 128 * j : 128 * (j + 1)]
+                    merged[j, pl.ds(at, SIDE, stride=2), :] = x
             return 0
 
         lax.fori_loop(0, 4, du_block, 0)
+
+        def narrow(i, _):
+            rows = pl.ds(pl.multiple_of(i * 128, 128), 128)
+            for j in range(2):
+                ibuf[j, rows, :] = merged[j, rows, :].astype(BF16)
+            return 0
+
+        lax.fori_loop(0, 8, narrow, 0)
         for j in range(2):
             move(
                 ibuf.at[j],
@@ -1652,15 +1801,29 @@
                 (2 * k + j, 2 * c + s // 2),
             )
 
-        left = left + home(IN1, gb_in1, gf_in1)
-        left = left + home(OUT1, gb_out1, gf_out1)
         shed_more(MID0, gw_mid0, ga_mid0, gd_mid0, gp_mid0, gb_mid0)
-        left = left + home(SC0, gb_sc, gf_sc)
+        left = left + home_cut(SC0, gb_sc, gf_sc, hb_sc, hi_sc, hr_sc)
         left = left + rest_home(1, REST0, rg0, rl0, rf0)
         left = left + table_home(3, 0, LATE_ROWS)
-        left = left + home(IN0, gb_in0, gf_in0)
-        left = left + home(MID0, gb_mid0, gf_mid0)
-
+        left = left + home_cut(IN0, gb_in0, gf_in0, hb_in0, hi_in0, hr_in0)
+        left = left + home_cut(MID0, gb_mid0, gf_mid0, hb_mid0, hi_mid0, hr_mid0)
+
+        take(OUT3, hi_out3, hr_out3)
+        take(MID2, hi_mid2, hr_mid2)
+        take(OUT1, hi_out1, hr_out1)
+        take(SC0, hi_sc, hr_sc)
+        take(IN0, hi_in0, hr_in0)
+        take(MID0, hi_mid0, hr_mid0)
+
+        for mat, ready in (
+            (IN0, hb_in0),
+            (MID0, hb_mid0),
+            (SC0, hb_sc),
+            (OUT1, hb_out1),
+            (MID2, hb_mid2),
+            (OUT3, hb_out3),
+        ):
+            end_home_cut(mat, ready)
         for mat, gw in (
             (MID0, gw_mid0),
             (SC0, gw_sc),
@@ -1701,7 +1864,7 @@
         for slot in range(2):
             for kk in range(2):
                 end_move(
-                    img.at[slot, pl.ds(2 * kk, 2)],
+                    planes.at[slot, pl.ds(2 * kk, 2)],
                     img_s.at[slot, kk],
                     (2 * k + slot, 2 * c + kk),
                 )
@@ -1767,7 +1930,7 @@
         vm(3, PX + 2 * SIDE, 128),
         vm(4, PX, 128),
         low(2, PX, 256),
-        low(2, 4, PX, 128),
+        low(2, 4 * PX, 128),
         vm(shard_rows, 128),
         vm(128, 128),
         vm(fill_rows, 128),
@@ -1858,6 +2021,22 @@
         low(2, 2, 16, 512),
         low(2, 4, 16, 256),
         low(2, 4, 16, 256),
+        low(2, 16, 128),
+        low(shard_rows // 32 + 2, 2, 16, 128),
+        low(2, 48, 256),
+        low(shard_rows // 192 + 2, 2, 48, 256),
+        low(2, 16, 512),
+        low(shard_rows // 128 + 2, 2, 16, 512),
+        low(2, 16, 512),
+        low(shard_rows // 128 + 2, 2, 16, 512),
+        low(2, 48, 256),
+        low(shard_rows // 192 + 2, 2, 48, 256),
+        low(2, 16, 512),
+        low(shard_rows // 128 + 2, 2, 16, 512),
+        vm(shard_rows, 128),
+        vm(4 * PX, 128),
+        low(2, 4, PX, 128),
+        vm(2, 4 * PX, 128),
         dma((PHASES,)),
         dma((PHASES, 2)),
         dma((17,)),
@@ -1888,11 +2067,18 @@
         dma((4,)),
         dma((9,)),
         dma((9, 2)),
+        dma((shard_rows // 32 + 2,)),
+        dma((shard_rows // 192 + 2,)),
+        dma((shard_rows // 128 + 2,)),
+        dma((shard_rows // 128 + 2,)),
+        dma((shard_rows // 192 + 2,)),
+        dma((shard_rows // 128 + 2,)),
+        dma((9,)),
     ]
     sds = jax.ShapeDtypeStruct
     outs = (
         sds((2, PX, 256), BF16),
-        sds((2, 4, PX, 128), BF16),
+        sds((2, 4 * PX, 128), BF16),
         sds((shard_rows, 128), F32),
     )
     vmem = pl.BlockSpec(memory_space=pltpu.VMEM)
@@ -1911,20 +2097,17 @@
 
 def per_device(images, cotangent, res_codes, section_weights):
     n = lax.axis_size("dp")
-    planes = images.reshape(2, SIDE, 2, SIDE, 2, 128).transpose(0, 2, 4, 1, 3, 5)
     out_o, out_i, out_w = call_kernel(
         n,
         (
-            planes.reshape(2, 4, PX, 128),
+            images.reshape(2, 4 * PX, 128),
             cotangent.reshape(2, PX, 256),
             res_codes,
             section_weights.reshape(-1, 128),
         ),
     )
     block_out = out_o.reshape(2, SIDE, SIDE, 256)
-    input_grad = (
-        out_i.reshape(2, 2, 2, SIDE, SIDE, 128).transpose(0, 3, 1, 4, 2, 5).reshape(images.shape)
-    )
+    input_grad = out_i.reshape(images.shape)
     return block_out, input_grad, out_w.reshape(section_weights.shape)
 
 

time: 157 us -> 139 us (0.89)
  Pallas kernels: 150 us -> 134 us
  local copies, waits for them, and re-layouts: 5.91 us -> 3.41 us
    pallas_call x1, Pallas kernels: 150 us -> 134 us  [call_kernel(): pl.pallas_call(make_kernel(n), out_shape=outs, in_specs=[smem if i == 2 e...]
    transpose x1 -> x0, local copies, waits for them, and re-layouts: 2.45 us -> none  [per_device(): out_i.reshape(2, 2, 2, SIDE, SIDE, 128).transpose(0, 3, 1, 4, 2, 5)]
    reshape x1 -> x0, local copies, waits for them, and re-layouts: 1.9 us -> none  [per_device(): images.reshape(2, SIDE, 2, SIDE, 2, 128).transpose(0, 2, 4, 1, 3, 5)]
    unnamed x6 -> x7, local copies, waits for them, and re-layouts: 1.55 us -> 3.41 us
where the time goes in v4:
time: 139 us; the launch traced here: 138 us
  Pallas kernels  134 us (96%)
  local copies, waits for them, and re-layouts  3.41 us (2%)
    pallas_call x1, Pallas kernels, call_kernel(): pl.pallas_call(make_kernel(n), out_shape=outs, in_specs=[smem if i == 2 e...  134 us
    unnamed x7, local copies, waits for them, and re-layouts  3.41 us

profile of v4, /device:TPU:9, one launch (start us, length us, event | category | flops | bytes accessed | tf_op | source)
XLA Modules:
  0.0 138.5 jit_solution(9320567307926352047)
XLA Ops:
  0.6 134.4 %shard_map.67 = (bf16[2,256,256]{2,1,0:T(8,128)(2,1)}, bf16[2,1024,128]{2,1,0:T(8,128)(2,1)}, f32[1320,128]{1,0:T(8,128)}) custom-call(bf16[2,1024,128]{2,1,0:T(8,128)(2,1)} %bitcast.8, bf16[2,256,256]{2,1,0:T(8,128)(2,1)} %bitcast.11, s32[2]{0:T(128)} %codes.1, f32[1320,128]{1,0:T(8,128)} %bitcast.6), custom_call_target="tpu_custom_call" | custom-call | tf_op jit(solution)/shard_map/pallas_call | solution.py:2086
  135.0 0.0 copy-start.1
  135.0 0.0 copy-start
  135.1 1.8 %copy.10 = bf16[2,16,16,256]{3,2,1,0:T(8,128)(2,1)} copy(bf16[2,16,16,256]{3,2,1,0:T(8,128)(2,1)} %bitcast.10) | data formatting | bytes 524288
  136.8 0.0 copy-done.1
  136.8 0.8 copy.11
  137.6 0.0 copy-done
  137.6 0.8 copy.12
Async XLA Ops:
  135.0 1.8 %copy-start.1 = (bf16[2,1024,128]{2,1,0:T(8,128)(2,1)S(1)}, bf16[2,1024,128]{2,1,0:T(8,128)(2,1)}, u32[]{:S(2)}) copy-start(bf16[2,1024,128]{2,1,0:T(8,128)(2,1)} %get-tuple-element.7) | copy-start | bytes 1572868
  135.0 2.6 %copy-start = (f32[1320,128]{1,0:T(8,128)S(1)}, f32[1320,128]{1,0:T(8,128)}, u32[]{:S(2)}) copy-start(f32[1320,128]{1,0:T(8,128)} %get-tuple-element.8) | copy-start | bytes 2027524

commit v5 on v4

--- a/solution.py
+++ b/solution.py
@@ -61,7 +61,10 @@
 MID2 = Matrix(6, 2, 0, 4, 6, 48, 2, 1)
 REST2 = Matrix(7, 2, 4608, 1, 8, 25, 0, 1, split="none")
 OUT3 = Matrix(8, 3, 0, 8, 4, 16, 0, 2)
-MATRICES = (IN0, MID0, REST0, SC0, OUT1, IN1, MID2, REST2, OUT3)
+SQ0 = Matrix(2, 0, 5644, 1, 4, 16, 0, 2, split="none")
+EX0 = Matrix(9, 0, 5902, 1, 8, 16, 0, 1, split="none")
+SQ2 = Matrix(7, 2, 4616, 1, 4, 16, 1, 2, split="none")
+EX2 = Matrix(10, 2, 4874, 1, 8, 16, 0, 1, split="none")
 CUT = (IN0, MID0, SC0, OUT1, MID2, OUT3)
 USED = (10530, 4116, 5390, 2064)
 REST_ROWS = 782
@@ -75,27 +78,32 @@
     (0, "b_mid"): (8, 5640, 2),
     (0, "g_sc"): (12, 10514, 4),
     (0, "b_sc"): (20, 10522, 4),
-    (1, "g_out"): (28, 2048, 4),
-    (1, "b_out"): (36, 2056, 4),
-    (1, "g_in"): (44, 4112, 1),
-    (1, "b_in"): (46, 4114, 1),
-    (3, "g_out"): (48, 2048, 4),
-    (3, "b_out"): (56, 2056, 4),
-    (2, "g_mid"): (64, 4608, 2),
-    (2, "b_mid"): (68, 4612, 2),
+    (1, "g_out"): (34, 2048, 4),
+    (1, "b_out"): (42, 2056, 4),
+    (1, "g_in"): (50, 4112, 1),
+    (1, "b_in"): (52, 4114, 1),
+    (3, "g_out"): (54, 2048, 4),
+    (3, "b_out"): (62, 2056, 4),
+    (2, "g_mid"): (70, 4608, 2),
+    (2, "b_mid"): (74, 4612, 2),
 }
-TABLE_ROWS = 72
+TABLE_ROWS = 84
 LATE_ROWS = 12
-SECTION_ROWS = {0: (0, 28), 1: (28, 20), 2: (64, 8), 3: (48, 16)}
-AT_MID = {0: 4, 2: 64}
+SECTION_ROWS = {0: (0, 34), 1: (34, 20), 2: (70, 14), 3: (54, 16)}
+AT_MID = {0: 4, 2: 70}
+AT_SMALL = {0: 28, 2: 78}
 RANGES = (
     (0, 1024, 4, 0),
     (0, 5636, 8, 4),
     (0, 10514, 16, 12),
-    (1, 2048, 16, 28),
-    (1, 4112, 4, 44),
-    (2, 4608, 8, 64),
-    (3, 2048, 16, 48),
+    (0, 5900, 2, 28),
+    (0, 6414, 4, 30),
+    (1, 2048, 16, 34),
+    (1, 4112, 4, 50),
+    (2, 4608, 8, 70),
+    (2, 4872, 2, 78),
+    (2, 5386, 4, 80),
+    (3, 2048, 16, 54),
 )
 
 
@@ -130,7 +138,7 @@
 def make_kernel(n):
     chips = n // 2
     shard_rows = WSLOTS // (128 * n)
-    fill_rows = max(shard_rows + 28 * n, 96 * (n - 1), 100 * n, 8 * (4 * n - 1), 16 * (2 * n - 1))
+    fill_rows = max(shard_rows + 34 * n, 96 * (n - 1), 100 * n, 8 * (4 * n - 1), 16 * (2 * n - 1))
 
     def kernel(
         img,
@@ -184,21 +192,17 @@
         table,
         w_in0,
         w_mid0,
-        rest0,
         w_sc,
         w_out1,
         w_in1,
         w_mid2,
-        rest2,
         w_out3,
         ln_in0,
         ln_mid0,
-        ln_rest0,
         ln_sc,
         ln_out1,
         ln_in1,
         ln_mid2,
-        ln_rest2,
         ln_out3,
         st_in0,
         st_mid0,
@@ -283,6 +287,24 @@
         pixels,
         planes,
         merged,
+        w_sq0,
+        ln_sq0,
+        st_sq0,
+        cu_sq0,
+        w_ex0,
+        ln_ex0,
+        st_ex0,
+        cu_ex0,
+        ex0,
+        w_sq2,
+        ln_sq2,
+        st_sq2,
+        cu_sq2,
+        w_ex2,
+        ln_ex2,
+        st_ex2,
+        cu_ex2,
+        ex2,
         ssem,
         rsem,
         bs,
@@ -453,6 +475,9 @@
         mine_to = mine_from + shard_rows
 
         def cut(mat, land, stage, base):
+            if mat.split == "none":
+                stage[...] = land[pl.ds(base, mat.flat), :].astype(BF16)
+                return
             for j in range(mat.blocks):
                 for h in range(2):
                     if mat.split == "rows":
@@ -630,19 +655,17 @@
         side_copy.start()
         snd[...] = jnp.zeros(snd.shape, F32)
 
-        def row0():
-            count = scatter_table(*RANGES[0][1:])
-            count = count + scatter_table(*RANGES[1][1:]) + scatter_table(*RANGES[2][1:])
-            return count + scatter_cut(SC0, ln_sc, st_sc, cu_sc)
-
-        def row1():
-            count = scatter_cut(OUT1, ln_out1, st_out1, cu_out1) + scatter_table(*RANGES[3][1:])
-            return count + scatter_table(*RANGES[4][1:])
-
-        sent = sent + when_row(0, row0)
-        sent = sent + when_row(1, row1)
-        sent = sent + when_row(2, lambda: scatter_table(*RANGES[5][1:]))
-        sent = sent + when_row(3, lambda: scatter_table(*RANGES[6][1:]))
+        def tables(r):
+            count = jnp.int32(0)
+            for row_of, start, rows, at in RANGES:
+                if row_of == r:
+                    count = count + scatter_table(start, rows, at)
+            return count
+
+        sent = sent + when_row(0, lambda: tables(0) + scatter_cut(SC0, ln_sc, st_sc, cu_sc))
+        sent = sent + when_row(1, lambda: scatter_cut(OUT1, ln_out1, st_out1, cu_out1) + tables(1))
+        sent = sent + when_row(2, lambda: tables(2))
+        sent = sent + when_row(3, lambda: tables(3))
 
         def scatter_some(sent, part, parts):
             sent = sent + when_row(2, lambda: scatter_cut(MID2, ln_mid2, st_mid2, cu_mid2, part, parts))
@@ -654,11 +677,18 @@
 
         def scatter_late(sent):
             sent = scatter_some(sent, 2, 3)
-            sent = sent + when_row(2, lambda: scatter_pieces(REST2, ln_rest2))
+            sent = sent + when_row(
+                2,
+                lambda: scatter_cut(SQ2, ln_sq2, st_sq2, cu_sq2)
+                + scatter_cut(EX2, ln_ex2, st_ex2, cu_ex2),
+            )
             fill_up(nought, fill, sent, fill_rows, h_s)
 
         sent = scatter_some(sent, 0, 3)
-        sent = sent + when_row(0, lambda: scatter_pieces(REST0, ln_rest0))
+        sent = sent + when_row(
+            0,
+            lambda: scatter_cut(SQ0, ln_sq0, st_sq0, cu_sq0) + scatter_cut(EX0, ln_ex0, st_ex0, cu_ex0),
+        )
 
         def spread(mat, land, stage, whole):
             @pl.when(holds(mat))
@@ -703,6 +733,16 @@
             hand(mat, here, 0, beside_x)
             hand(mat, here, 1, beside_y)
 
+        def pass_all(mat, whole):
+            here = quarters(mat, whole, s, 1)
+            full_wait(here, c_r.at[mat.index])
+            for i, to in enumerate((beside_x, beside_y, 3 - s)):
+                hand(mat, here, i, to)
+
+        def all_arrived(mat, whole):
+            for i, q in enumerate((beside_x, beside_y, 3 - s)):
+                full_wait(quarters(mat, whole, q, 1), q_r.at[mat.index, i])
+
         def pass_far(mat, whole):
             full_wait(quarters(mat, whole, beside_x, 1), q_r.at[mat.index, 0])
             hand(mat, quarters(mat, whole, beside_x, 1, 0), 2, beside_y)
@@ -722,17 +762,17 @@
 
             full_wait(quarters(mat, whole, 0, 3), f_s.at[mat.index])
 
-        def spread_rest(mat, land, whole):
+        def spread_small(mat, land, stage, whole):
             @pl.when(holds(mat))
             def _():
-                full_wait(land, h_r.at[mat.index])
-                at = piece(mat) * mat.flat
+                stage_ready(mat, land, stage)
+                p = piece(mat)
 
                 def one(i, _):
                     e = lax.rem(s * chips + c + i, 4 * chips)
                     move(
-                        land,
-                        whole.at[pl.ds(at, mat.flat)],
+                        stage,
+                        whole.at[p],
                         a_s.at[mat.index],
                         c_r.at[mat.index],
                         (e // chips, 2 * (e % chips)),
@@ -741,18 +781,18 @@
 
                 lax.fori_loop(0, 4 * chips, one, 0)
 
-        def share_rest(mat, whole, i):
+        def share_small(mat, whole, i):
             @pl.when(k == 0)
             def _():
                 full_wait(whole, c_r.at[mat.index])
                 to_twin(i, whole, whole).start()
 
-        def rest_arrived(whole, i):
+        def small_arrived(whole, i):
             @pl.when(k == 1)
             def _():
                 to_twin(i, whole, whole).wait_recv()
 
-        def end_rest(mat, whole, i):
+        def end_small(mat, whole, i):
             @pl.when(k == 0)
             def _():
                 to_twin(i, whole, whole).wait_send()
@@ -761,7 +801,7 @@
 
                 @pl.when(holds(mat) & (k == kk))
                 def _():
-                    rows = (4 * chips - 1 + kk) * mat.flat
+                    rows = (4 * chips - 1 + kk) * mat.flat // 2
                     full_wait(fill.at[pl.ds(0, rows)], a_s.at[mat.index])
 
         @pl.when(holds(IN0))
@@ -1235,11 +1275,9 @@
             send(ph)
 
         def small(rest):
-            w_sq = rest[AT_SQ : AT_SQ + CMID, :]
-            w_ex = jnp.concatenate(
-                [rest[pl.ds(AT_EX + j, CSQ, stride=4), :] for j in range(4)], axis=1
-            )
-            return w_sq, w_ex
+            _, w_sq, ex = rest
+            w_ex = jnp.concatenate([ex[pl.ds(j, CSQ, stride=4), :] for j in range(4)], axis=1)
+            return w_sq[...].reshape(CMID, CSQ).astype(F32), w_ex
 
         def attention_forward(ph, twin, total, at, rest, zref, rr, aref, beside):
             mu, rs = mean_rstd(total, 0, 256, counts[256])
@@ -1268,10 +1306,10 @@
             vq = jnp.mean(zq * zq, axis=0, keepdims=True) - mq * mq
             rq = lax.rsqrt(jnp.maximum(vq, 0.0) + EPS)
             hq = (zq - mq) * rq
-            nq = hq * rows_of(rest, AT_GSQ, 1) + rows_of(rest, AT_BSQ, 1)
+            nq = hq * rows_of(table, rest[0], 1) + rows_of(table, rest[0] + 1, 1)
             sgq = sigmoid(nq)
             qq = nq * sgq
-            logits = dot_hi(qq, w_ex) + rows_of(rest, AT_BEX, 4)
+            logits = dot_hi(qq, w_ex) + rows_of(table, rest[0] + 2, 4)
             diff = logits[:, 0:256] - logits[:, 256:512]
             sh0 = sigmoid(diff)
             sh1 = sigmoid(-diff)
@@ -1326,7 +1364,7 @@
             dn = dq * sgq * (1.0 + nq * (1.0 - sgq))
             set_rows(rg, AT_GSQ, jnp.sum(dn * hq, axis=0, keepdims=True))
             set_rows(rg, AT_BSQ, jnp.sum(dn, axis=0, keepdims=True))
-            dn = dn * rows_of(rest, AT_GSQ, 1)
+            dn = dn * rows_of(table, rest[0], 1)
             dzq = rq * (
                 dn
                 - jnp.mean(dn, axis=0, keepdims=True)
@@ -1374,9 +1412,12 @@
 
         dz_low = dz3.at[:, pl.ds(0, 256)]
 
+        rest0 = (AT_SMALL[0], w_sq0, ex0)
+        rest2 = (AT_SMALL[2], w_sq2, ex2)
         arrived(MID0, w_mid0)
         conv_forward(1, cols1, w_mid0, z2)
-        spread_rest(REST0, ln_rest0, rest0)
+        spread_small(SQ0, ln_sq0, st_sq0, w_sq0)
+        spread_small(EX0, ln_ex0, st_ex0, w_ex0)
         scatter_late(sent)
         pass_on(SC0, w_sc)
         pass_on(OUT1, w_out1)
@@ -1384,17 +1425,20 @@
         receive(1)
 
         def short_forward():
-            share_rest(REST0, rest0, 15)
+            spread(MID2, ln_mid2, st_mid2, w_mid2)
+            share_small(SQ0, w_sq0, 15)
+            share_small(EX0, w_ex0, 17)
             pass_far(SC0, w_sc)
             pass_far(OUT1, w_out1)
-            pass_on(IN1, w_in1)
-            spread(MID2, ln_mid2, st_mid2, w_mid2)
+            pass_all(IN1, w_in1)
             arrived(SC0, w_sc)
             z = dot(pool[...], w_sc[...].reshape(CIN, 512))
             zs[...] = z
             put(3, 8, jnp.sum(z, axis=0, keepdims=True))
             put(3, 12, jnp.sum(z * z, axis=0, keepdims=True))
-            rest_arrived(rest0, 15)
+            small_arrived(w_sq0, 15)
+            small_arrived(w_ex0, 17)
+            ex0[...] = w_ex0[...].reshape(512, 128).astype(F32)
 
         mid1, q1 = attention_forward(2, 2, totals(1), AT_MID[0], rest0, z2, rr1, a1, short_forward)
         arrived(OUT1, w_out1)
@@ -1407,9 +1451,9 @@
             send(ph)
 
         wide_forward(3, a1, w_out1, z3)
-        pass_far(IN1, w_in1)
-        pass_on(MID2, w_mid2)
-        spread_rest(REST2, ln_rest2, rest2)
+        pass_all(MID2, w_mid2)
+        spread_small(SQ2, ln_sq2, st_sq2, w_sq2)
+        spread_small(EX2, ln_ex2, st_ex2, w_ex2)
         receive(3)
         total = totals(3)
         mus, rss = mean_rstd(total, 8, 512, counts[512])
@@ -1429,7 +1473,7 @@
             return 0
 
         lax.fori_loop(0, 8, y1_block, 0)
-        arrived(IN1, w_in1)
+        all_arrived(IN1, w_in1)
         pz[0] = dot(y1[...], w_in1[1 - k].reshape(512, 128))
         swap = to_twin(3, pz.at[0], pz.at[1])
         swap.start()
@@ -1440,7 +1484,6 @@
         put(4, 0, jnp.sum(z, axis=0, keepdims=True))
         put(4, 1, jnp.sum(z * z, axis=0, keepdims=True))
         send(4)
-        pass_far(MID2, w_mid2)
         spread(OUT3, ln_out3, st_out3, w_out3)
         receive(4)
         mu4, rs4 = mean_rstd(totals(4), 0, 128, count1)
@@ -1453,15 +1496,18 @@
             for di in range(3):
                 store_tap(cols2, di, dj, x, 1 - di)
 
-        arrived(MID2, w_mid2)
+        all_arrived(MID2, w_mid2)
         conv_forward(5, cols2, w_mid2, z5)
-        share_rest(REST2, rest2, 16)
+        share_small(SQ2, w_sq2, 16)
+        share_small(EX2, w_ex2, 18)
         pass_on(OUT3, w_out3)
         receive(5)
 
         def last_weights():
             pass_far(OUT3, w_out3)
-            rest_arrived(rest2, 16)
+            small_arrived(w_sq2, 16)
+            small_arrived(w_ex2, 18)
+            ex2[...] = w_ex2[...].reshape(512, 128).astype(F32)
             for slot in range(2):
                 move(
                     cot.at[slot],
@@ -1514,7 +1560,8 @@
             )
         for mat, whole in ((MID0, w_mid0), (SC0, w_sc), (OUT1, w_out1)):
             end_spread(mat, whole)
-        end_rest(REST0, rest0, 15)
+        end_small(SQ0, w_sq0, 15)
+        end_small(EX0, w_ex0, 17)
         end_table()
         receive(8)
 
@@ -1564,7 +1611,8 @@
         def beside9():
             for mat, whole in ((IN1, w_in1), (MID2, w_mid2), (OUT3, w_out3)):
                 end_spread(mat, whole)
-            end_rest(REST2, rest2, 16)
+            end_small(SQ2, w_sq2, 16)
+            end_small(EX2, w_ex2, 18)
             shed_mid(OUT3, gw_out3, ga_out3, gt_out3, gd_out3)
 
         grad_rest2 = attention_backward(
@@ -1765,9 +1813,6 @@
         lax.fori_loop(0, 32, shed_in0, 0)
         shed_mid(MID0, gw_mid0, ga_mid0, gt_mid0, gd_mid0)
         shed_more(SC0, gw_sc, ga_sc, gd_sc, gp_sc, gb_sc)
-        left = left + home_cut(MID2, gb_mid2, gf_mid2, hb_mid2, hi_mid2, hr_mid2)
-        left = left + home(IN1, gb_in1, gf_in1)
-        left = left + home_cut(OUT1, gb_out1, gf_out1, hb_out1, hi_out1, hr_out1)
         swap.wait()
         to_twin(8, pdp.at[0], pdp.at[1]).wait()
 
@@ -1802,6 +1847,9 @@
             )
 
         shed_more(MID0, gw_mid0, ga_mid0, gd_mid0, gp_mid0, gb_mid0)
+        left = left + home_cut(MID2, gb_mid2, gf_mid2, hb_mid2, hi_mid2, hr_mid2)
+        left = left + home(IN1, gb_in1, gf_in1)
+        left = left + home_cut(OUT1, gb_out1, gf_out1, hb_out1, hi_out1, hr_out1)
         left = left + home_cut(SC0, gb_sc, gf_sc, hb_sc, hi_sc, hr_sc)
         left = left + rest_home(1, REST0, rg0, rl0, rf0)
         left = left + table_home(3, 0, LATE_ROWS)
@@ -1884,7 +1932,7 @@
 def call_kernel(n, operands):
     chips = n // 2
     shard_rows = WSLOTS // (128 * n)
-    fill_rows = max(shard_rows + 28 * n, 96 * (n - 1), 100 * n, 8 * (4 * n - 1), 16 * (2 * n - 1))
+    fill_rows = max(shard_rows + 34 * n, 96 * (n - 1), 100 * n, 8 * (4 * n - 1), 16 * (2 * n - 1))
 
     def vm(*shape, dtype=F32):
         return pltpu.VMEM(shape, dtype)
@@ -1938,21 +1986,17 @@
         vm(TABLE_ROWS, 128),
         low(2, 32, 16, 128),
         low(24, 48, 256),
-        vm(800, 128),
         low(32, 16, 512),
         low(16, 16, 512),
         low(2, 32, 16, 128),
         low(24, 48, 256),
-        vm(800, 128),
         low(16, 16, 512),
         vm(32, 128),
         vm(192, 128),
-        vm(25, 128),
         vm(128, 128),
         vm(128, 128),
         vm(64, 128),
         vm(192, 128),
-        vm(25, 128),
         vm(128, 128),
         low(2, 16, 128),
         low(2, 48, 256),
@@ -2037,10 +2081,28 @@
         vm(4 * PX, 128),
         low(2, 4, PX, 128),
         vm(2, 4 * PX, 128),
+        low(16, 16, 128),
+        vm(16, 128),
+        low(16, 128),
+        low(min(shard_rows // 16 + 2, 16), 16, 128),
+        low(32, 16, 128),
+        vm(16, 128),
+        low(16, 128),
+        low(min(shard_rows // 16 + 2, 32), 16, 128),
+        vm(512, 128),
+        low(16, 16, 128),
+        vm(16, 128),
+        low(16, 128),
+        low(min(shard_rows // 16 + 2, 16), 16, 128),
+        low(32, 16, 128),
+        vm(16, 128),
+        low(16, 128),
+        low(min(shard_rows // 16 + 2, 32), 16, 128),
+        vm(512, 128),
         dma((PHASES,)),
         dma((PHASES, 2)),
-        dma((17,)),
-        dma((17,)),
+        dma((19,)),
+        dma((19,)),
         dma((2, 2)),
         dma((4,)),
         dma((2,)),
@@ -2052,28 +2114,28 @@
         dma,
         dma,
         dma((2,)),
-        dma((9,)),
-        dma((9,)),
-        dma((9,)),
-        dma((9,)),
-        dma((9, 4)),
-        dma((9,)),
-        dma((9, 2)),
-        dma((9,)),
-        dma((9,)),
+        dma((11,)),
+        dma((11,)),
+        dma((11,)),
+        dma((11,)),
+        dma((11, 4)),
+        dma((11,)),
+        dma((11, 2)),
+        dma((11,)),
+        dma((11,)),
         dma,
         dma,
         dma((4,)),
         dma((4,)),
-        dma((9,)),
-        dma((9, 2)),
+        dma((11,)),
+        dma((11, 2)),
         dma((shard_rows // 32 + 2,)),
         dma((shard_rows // 192 + 2,)),
         dma((shard_rows // 128 + 2,)),
         dma((shard_rows // 128 + 2,)),
         dma((shard_rows // 192 + 2,)),
         dma((shard_rows // 128 + 2,)),
-        dma((9,)),
+        dma((11,)),
     ]
     sds = jax.ShapeDtypeStruct
     outs = (

time: 139 us -> 135 us (0.971)
  Pallas kernels: 134 us -> 129 us
    pallas_call x1, Pallas kernels: 134 us -> 129 us  [call_kernel(): pl.pallas_call(make_kernel(n), out_shape=outs, in_specs=[smem if i == 2 e...]
where the time goes in v5:
time: 135 us; the launch traced here: 133 us
  Pallas kernels  129 us (96%)
  local copies, waits for them, and re-layouts  3.41 us (3%)
    pallas_call x1, Pallas kernels, call_kernel(): pl.pallas_call(make_kernel(n), out_shape=outs, in_specs=[smem if i == 2 e...  129 us
    unnamed x7, local copies, waits for them, and re-layouts  3.41 us

profile of v5, /device:TPU:9, one launch (start us, length us, event | category | flops | bytes accessed | tf_op | source)
XLA Modules:
  0.0 133.4 jit_solution(12359908552762239354)
XLA Ops:
  0.6 129.4 %shard_map.67 = (bf16[2,256,256]{2,1,0:T(8,128)(2,1)}, bf16[2,1024,128]{2,1,0:T(8,128)(2,1)}, f32[1320,128]{1,0:T(8,128)}) custom-call(bf16[2,1024,128]{2,1,0:T(8,128)(2,1)} %bitcast.8, bf16[2,256,256]{2,1,0:T(8,128)(2,1)} %bitcast.11, s32[2]{0:T(128)} %codes.1, f32[1320,128]{1,0:T(8,128)} %bitcast.6), custom_call_target="tpu_custom_call" | custom-call | tf_op jit(solution)/shard_map/pallas_call | solution.py:2148
  130.0 0.0 copy-start.1
  130.0 0.0 copy-start
  130.0 1.8 %copy.10 = bf16[2,16,16,256]{3,2,1,0:T(8,128)(2,1)} copy(bf16[2,16,16,256]{3,2,1,0:T(8,128)(2,1)} %bitcast.10) | data formatting | bytes 524288
  131.8 0.0 copy-done.1
  131.8 0.8 copy.11
  132.6 0.0 copy-done
  132.6 0.8 copy.12
Async XLA Ops:
  130.0 1.8 %copy-start.1 = (bf16[2,1024,128]{2,1,0:T(8,128)(2,1)S(1)}, bf16[2,1024,128]{2,1,0:T(8,128)(2,1)}, u32[]{:S(2)}) copy-start(bf16[2,1024,128]{2,1,0:T(8,128)(2,1)} %get-tuple-element.7) | copy-start | bytes 1572868
  130.0 2.6 %copy-start = (f32[1320,128]{1,0:T(8,128)S(1)}, f32[1320,128]{1,0:T(8,128)}, u32[]{:S(2)}) copy-start(f32[1320,128]{1,0:T(8,128)} %get-tuple-element.8) | copy-start | bytes 2027524

commit v6 on v5

--- a/solution.py
+++ b/solution.py
@@ -305,6 +305,9 @@
         st_ex2,
         cu_ex2,
         ex2,
+        spb2,
+        d1,
+        d4,
         ssem,
         rsem,
         bs,
@@ -1325,32 +1328,42 @@
             lax.fori_loop(0, 4, mix, 0)
             return (mu, rs, lin, off), (pooled, rq, hq, nq, sgq, qq, sh0, sh1)
 
+        def slope(v):
+            sg = sigmoid(v)
+            return sg * (1.0 + v * (1.0 - sg))
+
+        def attention_slopes(ph, kept_mid, zref, sp_ref):
+            mu, rs, lin, off = kept_mid
+
+            def block(b, acc):
+                rows = pl.ds(pl.multiple_of(b * 32, 32), 32)
+                z = zref[rows, :]
+                sp = slope(z * lin + off) * lanes(mref[rows, :], 2)
+                sp_ref[rows, :] = sp
+                return (acc[0] + fold8(sp), acc[1] + fold8(sp * ((z - mu) * rs)))
+
+            sums = lax.fori_loop(0, 8, block, (jnp.zeros((8, 256), F32),) * 2)
+            put(ph, 4, jnp.sum(sums[0], axis=0, keepdims=True))
+            put(ph, 8, jnp.sum(sums[1], axis=0, keepdims=True))
+
         def attention_backward(
-            ph, kept_mid, kept_q, rest, rg, zref, rr, cols, mat, gw_mid, ga_mid, da, beside
+            ph, kept_mid, kept_q, rest, rg, zref, spb, rr, cols, mat, gw_mid, ga_mid, da, beside
         ):
             mu, rs, lin, off = kept_mid
             pooled, rq, hq, nq, sgq, qq, sh0, sh1 = kept_q
 
             def block(b, acc):
                 rows = pl.ds(pl.multiple_of(b * 32, 32), 32)
-                z = zref[rows, :]
-                v = z * lin + off
-                hat = (z - mu) * rs
-                sg = sigmoid(v)
-                sp = sg * (1.0 + v * (1.0 - sg)) * lanes(mref[rows, :], 2)
+                hat = (zref[rows, :] - mu) * rs
                 grad = da(rows)
-                t = grad * sp
+                t = grad * spb[rows, :]
                 dbuf[rows, :] = grad
-                spb[rows, :] = sp
                 r = rr[k, rows, :]
-                return tuple(
-                    x + fold8(y)
-                    for x, y in zip(acc, (grad * r, t, sp, t * hat, sp * hat))
-                )
-
-            acc = lax.fori_loop(0, 8, block, (jnp.zeros((8, 256), F32),) * 5)
-            for j, x in enumerate(acc):
-                put(ph, 2 * j, jnp.sum(x, axis=0, keepdims=True))
+                return tuple(x + fold8(y) for x, y in zip(acc, (grad * r, t, t * hat)))
+
+            acc = lax.fori_loop(0, 8, block, (jnp.zeros((8, 256), F32),) * 3)
+            for j, x in zip((0, 2, 6), acc):
+                put(ph, j, jnp.sum(x, axis=0, keepdims=True))
             send(ph)
             beside()
             receive(ph)
@@ -1501,6 +1514,13 @@
         share_small(SQ2, w_sq2, 16)
         share_small(EX2, w_ex2, 18)
         pass_on(OUT3, w_out3)
+
+        def slope3(b, _):
+            rows = pl.ds(pl.multiple_of(b * 32, 32), 32)
+            v3[rows, :] = slope(v3[rows, :]) * lanes(mref[rows, :], 4)
+            return 0
+
+        lax.fori_loop(0, 8, slope3, 0)
         receive(5)
 
         def last_weights():
@@ -1524,6 +1544,8 @@
         to_twin(14, w_in0.at[k], w_in0.at[k]).wait()
         for i in range(2):
             pltpu.make_async_copy(ctb.at[i], ctb.at[i], ct_r.at[i]).wait()
+        attention_slopes(9, mid2, z5, spb2)
+        d4[...] = slope(z4[...] * lin4 + off4) * mref[...]
         receive(7)
         mu6, rs6 = mean_rstd(totals(7), 0, 512, counts[512])
         lin6 = rs6 * vrow((3, "g_out"))
@@ -1563,6 +1585,13 @@
         end_small(SQ0, w_sq0, 15)
         end_small(EX0, w_ex0, 17)
         end_table()
+        attention_slopes(12, mid1, z2, spb)
+
+        def slope1(p, _):
+            d1[p] = slope(z1[p] * lin1 + off1) * mref[...]
+            return 0
+
+        lax.fori_loop(0, 4, slope1, 0)
         receive(8)
 
         def wide_back(total, base, key_g, key_b, lin, mu, rs, zref, dvf, dst):
@@ -1622,6 +1651,7 @@
             rest2,
             rg2,
             z5,
+            spb2,
             rr2,
             cols2,
             MID2,
@@ -1641,10 +1671,8 @@
         grad = grad + shift_cols(ep[0, SIDE : SIDE + PX, :], -1)
         grad = grad + shift_cols(ep[2, SIDE : SIDE + PX, :], 1)
         grad = grad.astype(BF16).astype(F32)
-        v = z4[...] * lin4 + off4
         hat4 = (z4[...] - mu4) * rs4
-        sg = sigmoid(v)
-        dv4 = grad * (sg * (1.0 + v * (1.0 - sg)) * mref[...])
+        dv4 = grad * d4[...]
         dh[0] = dv4
         put(10, 0, jnp.sum(dv4, axis=0, keepdims=True))
         put(10, 1, jnp.sum(dv4 * hat4, axis=0, keepdims=True))
@@ -1668,9 +1696,7 @@
             dy = dot_rt(dz4[0, rows, :], w_in1[0].reshape(512, 128))
             dy = dy + dot_rt(dz4[1, rows, :], w_in1[1].reshape(512, 128))
             dy = dy + dv6[rows, :].astype(BF16).astype(F32)
-            v = v3[rows, :]
-            sg = sigmoid(v)
-            dv = dy * (sg * (1.0 + v * (1.0 - sg)) * lanes(mref[rows, :], 4))
+            dv = dy * v3[rows, :]
             v3[rows, :] = dv
             low = dv.astype(BF16).astype(F32)
             hat = (z3[rows, :] - mu3) * rs3
@@ -1735,6 +1761,7 @@
             rest0,
             rg0,
             z2,
+            spb,
             rr1,
             cols1,
             MID0,
@@ -1761,9 +1788,7 @@
 
         def dv1_block(p, acc):
             z = z1[p]
-            v = z * lin1 + off1
-            sg = sigmoid(v)
-            dv = dh[p] * (sg * (1.0 + v * (1.0 - sg)) * mref[...])
+            dv = dh[p] * d1[p]
             dh[p] = dv
             return (acc[0] + fold8(dv), acc[1] + fold8(dv * ((z - mu1) * rs1)))
 
@@ -1777,6 +1802,7 @@
         shed_more(OUT1, gw_out1, ga_out1, gd_out1, gp_out1, gb_out1)
         shed_mid(SC0, gw_sc, ga_sc, gt_sc, gd_sc)
         left = left + home_cut(OUT3, gb_out3, gf_out3, hb_out3, hi_out3, hr_out3)
+        left = left + home_cut(MID2, gb_mid2, gf_mid2, hb_mid2, hi_mid2, hr_mid2, 0)
         left = left + table_home(0, LATE_ROWS, TABLE_ROWS - LATE_ROWS)
         receive(13)
         total = totals(13)
@@ -1847,7 +1873,7 @@
             )
 
         shed_more(MID0, gw_mid0, ga_mid0, gd_mid0, gp_mid0, gb_mid0)
-        left = left + home_cut(MID2, gb_mid2, gf_mid2, hb_mid2, hi_mid2, hr_mid2)
+        left = left + home_cut(MID2, gb_mid2, gf_mid2, hb_mid2, hi_mid2, hr_mid2, 1)
         left = left + home(IN1, gb_in1, gf_in1)
         left = left + home_cut(OUT1, gb_out1, gf_out1, hb_out1, hi_out1, hr_out1)
         left = left + home_cut(SC0, gb_sc, gf_sc, hb_sc, hi_sc, hr_sc)
@@ -1856,59 +1882,10 @@
         left = left + home_cut(IN0, gb_in0, gf_in0, hb_in0, hi_in0, hr_in0)
         left = left + home_cut(MID0, gb_mid0, gf_mid0, hb_mid0, hi_mid0, hr_mid0)
 
-        take(OUT3, hi_out3, hr_out3)
-        take(MID2, hi_mid2, hr_mid2)
-        take(OUT1, hi_out1, hr_out1)
-        take(SC0, hi_sc, hr_sc)
-        take(IN0, hi_in0, hr_in0)
-        take(MID0, hi_mid0, hr_mid0)
-
-        for mat, ready in (
-            (IN0, hb_in0),
-            (MID0, hb_mid0),
-            (SC0, hb_sc),
-            (OUT1, hb_out1),
-            (MID2, hb_mid2),
-            (OUT3, hb_out3),
-        ):
-            end_home_cut(mat, ready)
-        for mat, gw in (
-            (MID0, gw_mid0),
-            (SC0, gw_sc),
-            (OUT1, gw_out1),
-            (IN1, gw_in1),
-            (MID2, gw_mid2),
-            (OUT3, gw_out3),
-        ):
-            end_shed(mat, gw)
-
-        @pl.when(holds(IN0))
-        def _():
-            full_wait(gw_in0.at[pl.ds(0, 31)], gb_s.at[0])
-            full_wait(fill.at[pl.ds(0, 8 * (4 * n - 1))], a_s.at[0])
-
-        @pl.when(jnp.logical_not(holds(IN0)))
-        def _():
-            full_wait(gw_in0, gb_s.at[0])
-
-        for i, mat, land in ((1, REST0, rl0), (2, REST2, rl2)):
-
-            @pl.when((s == mat.row) & (d < 8))
-            def _():
-                full_wait(land, v_s.at[i])
-
-        @pl.when((s == 0) & (d < 2))
-        def _():
-            full_wait(gvl.at[pl.ds(LATE_ROWS, TABLE_ROWS - LATE_ROWS)], v_s.at[0])
-            full_wait(gvl.at[pl.ds(0, LATE_ROWS)], v_s.at[3])
-
         fill_up(nought, fill2, left, HOME_ROWS, gc_s)
-        full_wait(fill2, gc_s)
-        full_wait(fill, h_s)
-        full_wait(out_w, gc_r)
-        for slot in range(2):
-            pltpu.make_async_copy(out_o.at[slot], out_o.at[slot], oo_r.at[slot]).wait()
-            pltpu.make_async_copy(out_i.at[slot], out_i.at[slot], oi_r.at[slot]).wait()
+
+        for ph in range(PHASES):
+            end_send(ph)
         for slot in range(2):
             for kk in range(2):
                 end_move(
@@ -1919,12 +1896,61 @@
             end_move(cot.at[slot], ct_s.at[slot], (2 * k + slot, 2 * c + s // 2))
         for j in range(2):
             end_move(obuf.at[j], oo_s.at[j], (2 * k + j, 2 * c + s // 2))
+        for q in range(4):
+            full_wait(u.at[q, pl.ds(2 * k, 2)], bs.at[10 + q])
+        full_wait(fill, h_s)
+        for mat, gw in ((OUT1, gw_out1), (IN1, gw_in1), (MID2, gw_mid2), (OUT3, gw_out3)):
+            end_shed(mat, gw)
+
+        @pl.when(holds(IN0))
+        def _():
+            full_wait(fill.at[pl.ds(0, 8 * (4 * n - 1))], a_s.at[0])
+
+        for i, mat, land in ((1, REST0, rl0), (2, REST2, rl2)):
+
+            @pl.when((s == mat.row) & (d < 8))
+            def _():
+                full_wait(land, v_s.at[i])
+
+        @pl.when((s == 0) & (d < 2))
+        def _():
+            full_wait(gvl.at[pl.ds(LATE_ROWS, TABLE_ROWS - LATE_ROWS)], v_s.at[0])
+            full_wait(gvl.at[pl.ds(0, LATE_ROWS)], v_s.at[3])
+
+        take(OUT3, hi_out3, hr_out3)
+        take(MID2, hi_mid2, hr_mid2)
+        take(OUT1, hi_out1, hr_out1)
+        take(SC0, hi_sc, hr_sc)
+        take(IN0, hi_in0, hr_in0)
+        take(MID0, hi_mid0, hr_mid0)
+
+        for mat, ready in (
+            (IN0, hb_in0),
+            (MID0, hb_mid0),
+            (SC0, hb_sc),
+            (OUT1, hb_out1),
+            (MID2, hb_mid2),
+            (OUT3, hb_out3),
+        ):
+            end_home_cut(mat, ready)
+        for mat, gw in ((MID0, gw_mid0), (SC0, gw_sc)):
+            end_shed(mat, gw)
+
+        @pl.when(holds(IN0))
+        def _():
+            full_wait(gw_in0.at[pl.ds(0, 31)], gb_s.at[0])
+
+        @pl.when(jnp.logical_not(holds(IN0)))
+        def _():
+            full_wait(gw_in0, gb_s.at[0])
+
+        full_wait(fill2, gc_s)
+        full_wait(out_w, gc_r)
+        for slot in range(2):
+            full_wait(out_o.at[slot], oo_r.at[slot])
+            full_wait(out_i.at[slot], oi_r.at[slot])
+        for j in range(2):
             end_move(ibuf.at[j], oi_s.at[j], (2 * k + j, 2 * c + s // 2))
-        for q in range(4):
-            here = u.at[q, pl.ds(2 * k, 2)]
-            pltpu.make_async_copy(here, here, bs.at[10 + q]).wait()
-        for ph in range(PHASES):
-            end_send(ph)
 
     return kernel
 
@@ -2099,6 +2125,9 @@
         low(16, 128),
         low(min(shard_rows // 16 + 2, 32), 16, 128),
         vm(512, 128),
+        vm(PX, 256),
+        vm(4, PX, 128),
+        vm(PX, 128),
         dma((PHASES,)),
         dma((PHASES, 2)),
         dma((19,)),

time: 135 us -> 133 us (0.985); the launches traced: 133 us -> 133 us
  no operation moved by 1% of the time
where the time goes in v6:
time: 133 us
  Pallas kernels  129 us (97%)
  local copies, waits for them, and re-layouts  3.41 us (3%)
    pallas_call x1, Pallas kernels, call_kernel(): pl.pallas_call(make_kernel(n), out_shape=outs, in_specs=[smem if i == 2 e...  129 us
    unnamed x7, local copies, waits for them, and re-layouts  3.41 us

profile of v6, /device:TPU:9, one launch (start us, length us, event | category | flops | bytes accessed | tf_op | source)
XLA Modules:
  0.0 133.2 jit_solution(11870015503970958102)
XLA Ops:
  0.6 129.1 %shard_map.67 = (bf16[2,256,256]{2,1,0:T(8,128)(2,1)}, bf16[2,1024,128]{2,1,0:T(8,128)(2,1)}, f32[1320,128]{1,0:T(8,128)}) custom-call(bf16[2,1024,128]{2,1,0:T(8,128)(2,1)} %bitcast.8, bf16[2,256,256]{2,1,0:T(8,128)(2,1)} %bitcast.11, s32[2]{0:T(128)} %codes.1, f32[1320,128]{1,0:T(8,128)} %bitcast.6), custom_call_target="tpu_custom_call" | custom-call | tf_op jit(solution)/shard_map/pallas_call | solution.py:2177
  129.8 0.0 copy-start.1
  129.8 0.0 copy-start
  129.8 1.8 %copy.10 = bf16[2,16,16,256]{3,2,1,0:T(8,128)(2,1)} copy(bf16[2,16,16,256]{3,2,1,0:T(8,128)(2,1)} %bitcast.10) | data formatting | bytes 524288
  131.6 0.0 copy-done.1
  131.6 0.8 copy.11
  132.4 0.0 copy-done
  132.4 0.8 copy.12
Async XLA Ops:
  129.8 1.8 %copy-start.1 = (bf16[2,1024,128]{2,1,0:T(8,128)(2,1)S(1)}, bf16[2,1024,128]{2,1,0:T(8,128)(2,1)}, u32[]{:S(2)}) copy-start(bf16[2,1024,128]{2,1,0:T(8,128)(2,1)} %get-tuple-element.7) | copy-start | bytes 1572868
  129.8 2.6 %copy-start = (f32[1320,128]{1,0:T(8,128)S(1)}, f32[1320,128]{1,0:T(8,128)}, u32[]{:S(2)}) copy-start(f32[1320,128]{1,0:T(8,128)} %get-tuple-element.8) | copy-start | bytes 2027524
